TPU v7x, 128 devices: a whole 4x4x4 slice. The times are simulated.
128 devices in a mesh: dp: 32 (over z, y, core), head: 2 (over x_hi), pos: 2 (over x_lo).
Axes of the slice: x: 4 (x_hi: 2, x_lo: 2; x = x_hi * 2 + x_lo), y: 4, z: 4, core: 2. Of those that a mesh axis runs over, the one named last changes fastest.
Arguments:
- queries: bfloat16 [768, 128, 1024], P('dp', 'pos', 'head'), may hold values from -28 to 28
- output_gradient: bfloat16 [768, 128, 1024], P('dp', 'pos', 'head'), may hold values from -24 to 24
- prefix_keys: bfloat16 [32, 256, 256], P('dp', 'pos', 'head'), may hold values from -12 to 12
- prefix_values: bfloat16 [32, 256, 256], P('dp', 'pos', 'head'), may hold values from -6 to 6
- tile_prefix: int32 [768, 1], replicated, may hold values from 0 to 31; in each aligned block of 24 rows (0 to 23, 24 to 47, ...) at most 2 rows name the same one
- suffix_lse: float32 [768, 128, 8], P(None, None, 'head'), may hold values from 5 to 12
- suffix_dot: float32 [768, 128, 8], P(None, None, 'head'), may hold values from -64 to 64
Outputs:
- query_grad: bfloat16 [768, 128, 1024], P('dp', 'pos', 'head')
- key_grad: bfloat16 [32, 256, 256], P('dp', 'pos', 'head')
- value_grad: bfloat16 [32, 256, 256], P('dp', 'pos', 'head')
Inputs may be any that keep to these rules, and one draw needn't show every extreme that they name: `tile_prefix`: in each aligned block of 24 tiles (the tiles of one dp index) no prefix is named by more than 2 tiles, and some block has a prefix named exactly 2 times.
All inputs are finite; a program needn't handle non-finite values.
Results may differ from a plain program's by a relative error of at most 0.012.
Values may be sent and summed in bfloat16 or wider, within the bound.
No kernel may reach another device: no remote copies, remote signals or barrier semaphores. Data moves between devices by JAX's collectives and lax.ppermute only.
A program may use at most 128 MiB of HBM per device.

v0:
```python
import math

import jax
import jax.numpy as jnp
from jax import lax
from jax.sharding import PartitionSpec as P


def joined(value, axis, join):
    pieces = jax.tree.map(lambda part: lax.all_gather(part, axis), value)
    head = jax.tree.map(lambda part: part[0], pieces)
    tail = jax.tree.map(lambda part: part[1:], pieces)
    running, _ = lax.scan(lambda running, piece: (join(running, piece), None), head, tail)
    return running


def block_stats(query_row_set, grad_rows, key_rows, value_rows, scaling):
    scores = (
        jnp.einsum("nd,jd->nj", query_row_set, key_rows, preferred_element_type=jnp.float32)
        * scaling
    )
    prob_grad = jnp.einsum("nd,jd->nj", grad_rows, value_rows, preferred_element_type=jnp.float32)
    row_peak = jnp.max(scores, axis=1)
    shifted = jnp.exp(scores - row_peak[:, None])
    return (row_peak, jnp.sum(shifted, axis=1), jnp.sum(shifted * prob_grad, axis=1))


def block_grads(query_row_set, grad_rows, key_rows, value_rows, row_lse, row_delta, scaling):
    scores = (
        jnp.einsum("nd,jd->nj", query_row_set, key_rows, preferred_element_type=jnp.float32)
        * scaling
    )
    prob_grad = jnp.einsum("nd,jd->nj", grad_rows, value_rows, preferred_element_type=jnp.float32)
    weights = jnp.exp(scores - row_lse[:, None])
    prob_half = weights.astype(jnp.bfloat16)
    score_grad = (weights * (prob_grad - row_delta[:, None])).astype(jnp.bfloat16)
    query_part = jnp.dot(score_grad, key_rows, preferred_element_type=jnp.float32) * scaling
    key_part = (
        jnp.einsum("nj,nd->jd", score_grad, query_row_set, preferred_element_type=jnp.float32)
        * scaling
    )
    value_part = jnp.einsum("nj,nd->jd", prob_half, grad_rows, preferred_element_type=jnp.float32)
    return (query_part, key_part, value_part)


def combine_stats(earlier, later):
    row_peak = jnp.maximum(earlier[0], later[0])
    early_scale = jnp.exp(earlier[0] - row_peak)
    late_scale = jnp.exp(later[0] - row_peak)
    return (
        row_peak,
        earlier[1] * early_scale + later[1] * late_scale,
        earlier[2] * early_scale + later[2] * late_scale,
    )


def finish_stats(row_peak, row_total, row_moment, suffix_l, suffix_d):
    row_top = jnp.maximum(row_peak, suffix_l)
    prefix_part = jnp.exp(row_peak - row_top)
    suffix_part = jnp.exp(suffix_l - row_top)
    row_mass = row_total * prefix_part + suffix_part
    row_lse = row_top + jnp.log(row_mass)
    row_delta = (row_moment * prefix_part + suffix_d * suffix_part) / row_mass
    return (row_lse, row_delta)


def shards(
    queries, output_gradient, prefix_keys, prefix_values, tile_prefix, suffix_lse, suffix_dot
):
    dp_count = lax.axis_size("dp")
    pos_count = lax.axis_size("pos")
    dp_index = lax.axis_index("dp")
    tile_count, row_count, row_width = queries.shape
    head_dim = prefix_keys.shape[2]
    head_count = row_width // head_dim
    tile_rows = row_count * pos_count
    scaling = head_dim ** (-0.5)
    position_limit = max(2, tile_count // dp_count)
    target = tile_prefix[:, 0].reshape(dp_count, tile_count)
    owners = lax.broadcasted_iota(jnp.int32, (1, 1, dp_count), 2)
    onehot = (target[:, :, None] == owners).astype(jnp.int32)
    before = jnp.cumsum(onehot, axis=1) - onehot
    slot_rank = jnp.sum(before * onehot, axis=2)
    own_target = lax.dynamic_index_in_dim(target, dp_index, 0, keepdims=False)
    own_rank = lax.dynamic_index_in_dim(slot_rank, dp_index, 0, keepdims=False)
    dest_ids = lax.broadcasted_iota(jnp.int32, (dp_count, 1, 1), 0)
    slot_ids = lax.broadcasted_iota(jnp.int32, (1, position_limit, 1), 1)
    outgoing_mask = (
        (own_target[None, None, :] == dest_ids) & (own_rank[None, None, :] == slot_ids)
    ).astype(jnp.bfloat16)
    send_query = jnp.einsum(
        "qhb,blo->qhlo", outgoing_mask, queries, preferred_element_type=jnp.float32
    ).astype(jnp.bfloat16)
    send_grad = jnp.einsum(
        "qhb,blo->qhlo", outgoing_mask, output_gradient, preferred_element_type=jnp.float32
    ).astype(jnp.bfloat16)
    came_query, came_grad = (
        lax.all_to_all(send_query, "dp", split_axis=0, concat_axis=0, tiled=True),
        lax.all_to_all(send_grad, "dp", split_axis=0, concat_axis=0, tiled=True),
    )
    source_ids = lax.broadcasted_iota(jnp.int32, (dp_count, 1, 1, 1), 0)
    slot_four = lax.broadcasted_iota(jnp.int32, (1, position_limit, 1, 1), 1)
    block_ids = lax.broadcasted_iota(jnp.int32, (1, 1, dp_count, 1), 2)
    slot_pick = (
        (source_ids == block_ids)
        & (target[None, None] == dp_index)
        & (slot_rank[None, None] == slot_four)
    ).astype(jnp.float32)
    slot_pick = slot_pick.reshape(dp_count * position_limit, dp_count * tile_count)
    slot_lse = jnp.einsum(
        "kt,trh->krh", slot_pick, suffix_lse, precision=lax.Precision.HIGHEST
    ).reshape(dp_count, position_limit, tile_rows, head_count)
    slot_dot = jnp.einsum(
        "kt,trh->krh", slot_pick, suffix_dot, precision=lax.Precision.HIGHEST
    ).reshape(dp_count, position_limit, tile_rows, head_count)
    key_rows = prefix_keys[0]
    value_rows = prefix_values[0]
    all_query, all_grad = (
        lax.all_gather(came_query, "pos", axis=2, tiled=True),
        lax.all_gather(came_grad, "pos", axis=2, tiled=True),
    )
    group_size = math.gcd(dp_count, 8)
    turn_count = dp_count // group_size
    grouped_shape = (turn_count, group_size * position_limit, tile_rows, row_width)
    group_query = all_query.reshape(grouped_shape)
    group_grad = all_grad.reshape(grouped_shape)

    def stats_turn(running, block_list):
        block_query, block_grad = block_list
        stats = block_stats(
            block_query.reshape(-1, head_dim),
            block_grad.reshape(-1, head_dim),
            key_rows,
            value_rows,
            scaling,
        )
        return (running, stats)

    _, partials = lax.scan(stats_turn, jnp.zeros((), jnp.float32), (group_query, group_grad))
    row_peak, row_total, row_moment = joined(partials, "pos", combine_stats)
    flat_shape = (turn_count, group_size * position_limit * tile_rows * head_count)
    row_lse, row_delta = finish_stats(
        row_peak, row_total, row_moment, slot_lse.reshape(flat_shape), slot_dot.reshape(flat_shape)
    )

    def grad_turn(running, pieces):
        block_query, block_grad, block_lse, block_delta = pieces
        query_part, key_part, value_part = block_grads(
            block_query.reshape(-1, head_dim),
            block_grad.reshape(-1, head_dim),
            key_rows,
            value_rows,
            block_lse,
            block_delta,
            scaling,
        )
        return (
            (running[0] + key_part, running[1] + value_part),
            query_part.reshape(group_size * position_limit, tile_rows, row_width),
        )

    zero_sum = jnp.zeros((key_rows.shape[0], head_dim), jnp.float32)
    (key_sum, value_sum), query_all = lax.scan(
        grad_turn, (zero_sum, zero_sum), (group_query, group_grad, row_lse, row_delta)
    )
    query_all = query_all.reshape(dp_count, position_limit, tile_rows, row_width)
    query_mine = lax.psum_scatter(
        query_all.astype(jnp.bfloat16), "pos", scatter_dimension=2, tiled=True
    )
    returned_gradient = lax.all_to_all(query_mine, "dp", split_axis=0, concat_axis=0, tiled=True)
    query_grad = jnp.einsum(
        "byh,byqp->hqp", outgoing_mask, returned_gradient, preferred_element_type=jnp.float32
    ).astype(jnp.bfloat16)
    return (query_grad, key_sum.astype(jnp.bfloat16)[None], value_sum.astype(jnp.bfloat16)[None])


def solution(mesh):
    in_specs = (
        P("dp", "pos", "head"),
        P("dp", "pos", "head"),
        P("dp", "pos", "head"),
        P("dp", "pos", "head"),
        P(),
        P(None, None, "head"),
        P(None, None, "head"),
    )
    out_specs = (P("dp", "pos", "head"), P("dp", "pos", "head"), P("dp", "pos", "head"))
    return jax.shard_map(shards, mesh=mesh, in_specs=in_specs, out_specs=out_specs, check_vma=False)
```

profile of v0, /device:TPU:0, one launch (start us, length us, event | category | flops | bytes accessed | tf_op | source)
XLA Modules:
  0.0 660.2 jit_solution(6844778687906361062)
XLA Ops:
  14.5 59.4 %all_to_all.15 = bf16[32,2,64,512]{3,2,1,0:T(8,128)(2,1)} all-to-all(bf16[32,2,64,512]{3,2,1,0:T(8,128)(2,1)S(1)} %copy.42), channel_id=1, replica_groups=mesh['dp'=32,'head'=2,'pos'=2] {'dp'}, dimensions={0} | all-to-all | bytes 8388608 | tf_op jit(solution)/shard_map/all_to_all | solution.py:98
  79.1 54.8 %all_to_all.16 = bf16[32,2,64,512]{3,2,1,0:T(8,128)(2,1)} all-to-all(bf16[32,2,64,512]{3,2,1,0:T(8,128)(2,1)S(1)} %copy.44), channel_id=1, replica_groups=mesh['dp'=32,'head'=2,'pos'=2] {'dp'}, dimensions={0} | all-to-all | bytes 8388608 | tf_op jit(solution)/shard_map/all_to_all | solution.py:99
  138.8 6.1 reshape_reshape.6
  148.3 6.0 reshape_reshape.7
  154.3 24.0 %all-gather.9.cloned.1.call-done = bf16[32,2,128,512]{3,2,1,0:T(8,128)(2,1)} async-done(((bf16[32,2,64,512]{3,2,1,0:T(8,128)(2,1)}), bf16[32,2,128,512]{3,2,1,0:T(8,128)(2,1)}) %all-gather.9.cloned.1.call-update) | async-done | bytes 8388624 | tf_op jit(solution)/shard_map/all_gather | solution.py:119
  178.4 109.2 %all-gather.11.cloned.1.call-done = bf16[32,2,128,512]{3,2,1,0:T(8,128)(2,1)} async-done(((bf16[32,2,64,512]{3,2,1,0:T(8,128)(2,1)}), bf16[32,2,128,512]{3,2,1,0:T(8,128)(2,1)}) %all-gather.11.cloned.1.call-update) | async-done | bytes 8388624 | tf_op jit(solution)/shard_map/all_gather | solution.py:120
  287.5 67.7 %while.11 = (s32[]{:T(128)}, f32[4,8192]{1,0:T(4,128)S(1)}, f32[4,8192]{1,0:T(4,128)S(1)}, f32[4,8192]{1,0:T(4,128)S(1)}, bf16[4,16,128,512]{3,2,1,0:T(8,128)(2,...) while((s32[]{:T(128)}, f32[4,8192]{1,0:T(4,128)S(1)}, ...), condition=%wide.region_6.7_spmd, body=%wide.region_2.6_spmd.sunk | while | flops 544186368 | bytes 42369176 | solution.py:139
  287.7 4.6 constant_dynamic-slice_fusion.9
  304.6 4.6 constant_dynamic-slice_fusion.9
  321.5 4.6 constant_dynamic-slice_fusion.9
  338.3 4.6 constant_dynamic-slice_fusion.9
  355.2 5.9 all-gather.3
  361.1 5.6 all-gather.5
  366.7 5.6 all-gather.4
  372.7 101.5 %while.36 = (s32[]{:T(128)}, f32[128,128]{1,0:T(8,128)S(1)}, f32[128,128]{1,0:T(8,128)S(1)}, bf16[4,16,128,512]{3,2,1,0:T(8,128)(2,1)}, bf16[4,16,128,512]{3,2,1...) while((s32[]{:T(128)}, f32[128,128]{1,0:T(8,128)S(1)}, ...), condition=%wide.region_8.9_spmd.clone, body=%wide.region_7.8_spmd.clone.sunk | while | flops 1350647808 | bytes 63471788 | solution.py:163
  372.7 4.6 constant_dynamic-slice_fusion.10
  398.1 4.6 constant_dynamic-slice_fusion.10
  423.5 4.6 constant_dynamic-slice_fusion.10
  448.9 4.6 constant_dynamic-slice_fusion.10
  474.2 102.9 %reduce-scatter.2.cloned.1.call-done = bf16[32,2,64,512]{3,2,1,0:T(8,128)(2,1)} async-done(((bf16[32,2,128,512]{3,2,1,0:T(8,128)(2,1)}), bf16[32,2,64,512]{3,2,1,0:T(8,128)(2,1)}) %reduce-scatter.2.cloned.1.call-update) | async-done | bytes 4194320 | tf_op jit(solution)/shard_map/reduce_scatter | solution.py:167
  577.1 8.5 %copy.50 = bf16[32,2,64,512]{3,1,2,0:T(2,128)(2,1)} copy(bf16[32,2,64,512]{3,2,1,0:T(8,128)(2,1)} %reduce-scatter.2.cloned.1.call-done) | data formatting | bytes 8388608 | tf_op jit(solution)/shard_map/reduce_scatter | solution.py:167
  585.6 7.8 %all-to-all-start.2 = ((bf16[32,2,64,512]{3,1,2,0:T(2,128)(2,1)}), bf16[32,2,64,512]{3,1,2,0:T(2,128)(2,1)}, u32[]{:S(2)}, u32[]{:S(2)}) async-start(bf16[32,2,64,512]{3,1,2,0:T(2,128)(2,1)} %copy.50), calls=%async_computation.3 | async-start | bytes 8388608 | tf_op jit(solution)/shard_map/all_to_all | solution.py:170
  594.1 52.8 %all-to-all-done.2 = bf16[32,2,64,512]{3,1,2,0:T(2,128)(2,1)} async-done(((bf16[32,2,64,512]{3,1,2,0:T(2,128)(2,1)}), bf16[32,2,64,512]{3,1,2,0:T(2,128)(2,1)}, u32[]{:S(2)}, u32[]{:S(2)}) %all-to-all-start.2) | async-done | bytes 4194336 | tf_op jit(solution)/shard_map/all_to_all | solution.py:170
  646.9 4.7 bitcast_convert_fusion
  (146 shorter events, 154.8 us)
Async XLA Ops:
  7.2 128.1 %copy-start = (f32[768,128,4]{1,2,0:T(4,128)S(1)}, f32[768,128,4]{1,2,0:T(4,128)}, u32[]{:S(2)}) copy-start(f32[768,128,4]{1,2,0:T(4,128)} %param.16) | copy-start | bytes 4718596
  7.2 171.2 %all-gather.9.cloned.1.call-start = ((), (), s32[]{:S(2)}) async-start(), calls=%async_computation.4 | async-start | bytes 12582912 | tf_op jit(solution)/shard_map/all_gather | solution.py:119
  8.3 65.7 %copy-start.8 = (pred[32,24]{0,1:T(8,128)(4,1)}, pred[32,24]{0,1:T(8,128)(4,1)S(1)}, u32[]{:S(2)}) copy-start(pred[32,24]{0,1:T(8,128)(4,1)S(1)} %iota_compare_fusion.4) | copy-start | bytes 2308
  9.3 64.7 %copy-start.10 = (pred[2,24]{1,0:T(4,128)(4,1)}, pred[2,24]{1,0:T(4,128)(4,1)S(1)}, u32[]{:S(2)}) copy-start(pred[2,24]{1,0:T(4,128)(4,1)S(1)} %iota_compare_fusion.5) | copy-start | bytes 148
  73.9 1.4 copy-start.7
  73.9 213.6 %all-gather.11.cloned.1.call-start = ((), (), s32[]{:S(2)}) async-start(), calls=%async_computation.5 | async-start | bytes 12582912 | tf_op jit(solution)/shard_map/all_gather | solution.py:120
  133.9 443.2 %reduce-scatter.2.cloned.1.call-start = ((), (), s32[]{:S(2)}) async-start(), calls=%async_computation.6 | async-start | bytes 12582912 | tf_op jit(solution)/shard_map/reduce_scatter | solution.py:167
  138.8 6.1 copy-start.6
  148.3 139.2 %copy-start.4 = (bf16[1,128,128]{2,1,0:T(8,128)(2,1)S(1)}, bf16[1,128,128]{2,1,0:T(8,128)(2,1)}, u32[]{:S(2)}) copy-start(bf16[1,128,128]{2,1,0:T(8,128)(2,1)} %param.13) | copy-start | bytes 98308
  148.3 139.2 %copy-start.5 = (bf16[1,128,128]{2,1,0:T(8,128)(2,1)S(1)}, bf16[1,128,128]{2,1,0:T(8,128)(2,1)}, u32[]{:S(2)}) copy-start(bf16[1,128,128]{2,1,0:T(8,128)(2,1)} %param.14) | copy-start | bytes 98308
  299.9 1.6 copy-start.3
  316.7 1.6 copy-start.3
  333.6 1.6 copy-start.3
  350.5 1.6 copy-start.3
  384.9 1.6 copy-start.2
  410.3 1.6 copy-start.2
  435.6 1.6 copy-start.2
  461.0 1.6 copy-start.2
  585.6 61.2 %copy-start.9 = (pred[32,24]{0,1:T(8,128)(4,1)S(1)}, pred[32,24]{0,1:T(8,128)(4,1)}, u32[]{:S(2)}) copy-start(pred[32,24]{0,1:T(8,128)(4,1)} %copy-done.8) | copy-start | bytes 2308
  585.6 61.2 %copy-start.11 = (pred[2,24]{1,0:T(4,128)(4,1)S(1)}, pred[2,24]{1,0:T(4,128)(4,1)}, u32[]{:S(2)}) copy-start(pred[2,24]{1,0:T(4,128)(4,1)} %copy-done.10) | copy-start | bytes 148
  585.6 61.2 %all-to-all-start.2 = ((bf16[32,2,64,512]{3,1,2,0:T(2,128)(2,1)}), bf16[32,2,64,512]{3,1,2,0:T(2,128)(2,1)}, u32[]{:S(2)}, u32[]{:S(2)}) async-start(bf16[32,2,64,512]{3,1,2,0:T(2,128)(2,1)} %copy.50), calls=%async_computation.3 | async-start | bytes 8388608 | tf_op jit(solution)/shard_map/all_to_all | solution.py:170
  646.9 6.4 copy-start.1
Sparse Core Ops, SparseCore 0:
  74.0 104.2 all-gather.8
  180.0 107.4 all-gather.10
  474.3 102.7 reduce-scatter.1
where the time goes:
time: 674 us; the launch traced here: 660 us
  waiting for transfers between devices  289 us (43%)
  local copies, waits for them, and re-layouts  164 us (24%)
  blocking collectives  131 us (19%)
  matrix products  47 us (7%)
  between operations  14.3 us (2%)
  starting transfers between devices  8.07 us (1%)
    all_gather x1, waiting for transfers between devices, shards(): lax.all_gather(came_grad, 'pos', axis=2, tiled=True)  109 us
    reduce_scatter x1, waiting for transfers between devices, shards(): lax.psum_scatter(query_all.astype(jnp.bfloat16), 'pos', scatter_dimension...  103 us
    all_to_all x1, blocking collectives, shards(): lax.all_to_all(send_query, 'dp', split_axis=0, concat_axis=0, tiled=True)  59.4 us
    all_to_all x1, blocking collectives, shards(): lax.all_to_all(send_grad, 'dp', split_axis=0, concat_axis=0, tiled=True)  54.8 us
    all_to_all x1, waiting for transfers between devices, shards(): lax.all_to_all(query_mine, 'dp', split_axis=0, concat_axis=0, tiled=True)  52.8 us
    dynamic_slice x8, local copies, waits for them, and re-layouts, shards(): lax.scan(stats_turn, jnp.zeros((), jnp.float32), (group_query, group_grad))  37.1 us
    all_gather x1, waiting for transfers between devices, shards(): lax.all_gather(came_query, 'pos', axis=2, tiled=True)  24 us
    reshape x4, local copies, waits for them, and re-layouts, stats_turn(): block_grad.reshape(-1, head_dim)  17.6 us
  transfers between devices with their start and end apart: 4, of which 4 were waited for; matrix products, arithmetic and copies ran while one was open for 4% of the time, Pallas kernels for 0%

commit v1 on v0

v1 whole, which is shorter than its diff:
```python
import functools
import math

import jax
import jax.numpy as jnp
from jax import lax
from jax.experimental import pallas as pl
from jax.experimental.pallas import tpu as pltpu
from jax.sharding import PartitionSpec as P

SIDE = 4
LOG2E = math.log2(math.e)


def place(z, y, core):
    return (z % SIDE) * 2 * SIDE + (y % SIDE) * 2 + core


def ring_pairs(second, step):
    pairs = []
    for z in range(SIDE):
        for y in range(SIDE):
            for core in range(2):
                along_y = (core == 0) != second
                target = place(z, y + step, core) if along_y else place(z + step, y, core)
                pairs.append((place(z, y, core), target))
    return pairs


def core_pairs():
    return [(i, i ^ 1) for i in range(2 * SIDE * SIDE)]


def shift(x, second, step):
    return lax.ppermute(x, "dp", ring_pairs(second, step))


def swap_cores(x):
    return lax.ppermute(x, "dp", core_pairs())


def swap_pos(x):
    return lax.ppermute(x, "pos", [(0, 1), (1, 0)])


def tile_grads(query, grad, keys, values, stat, scaling):
    nt = (((1,), (1,)), ((), ()))
    tn = (((0,), (0,)), ((), ()))
    f32 = jnp.float32
    scores = lax.dot_general(keys, query, nt, preferred_element_type=f32) * (scaling * LOG2E)
    prob_grad = lax.dot_general(values, grad, nt, preferred_element_type=f32)
    suffix_l = stat[0:1] * LOG2E
    suffix_d = stat[1:2]
    top = jnp.maximum(jnp.max(scores, axis=0, keepdims=True), suffix_l)
    raised = jnp.exp2(scores - top)
    suffix_part = jnp.exp2(suffix_l - top)
    inverse = 1.0 / (jnp.sum(raised, axis=0, keepdims=True) + suffix_part)
    moment = jnp.sum(raised * prob_grad, axis=0, keepdims=True) + suffix_part * suffix_d
    delta = moment * inverse
    probs = raised * inverse
    prob_half = probs.astype(jnp.bfloat16)
    score_grad = (probs * (prob_grad - delta)).astype(jnp.bfloat16)
    query_part = lax.dot_general(score_grad, keys, tn, preferred_element_type=f32) * scaling
    key_part = jnp.dot(score_grad, query, preferred_element_type=f32) * scaling
    value_part = jnp.dot(prob_half, grad, preferred_element_type=f32)
    return query_part, key_part, value_part


def stage_kernel(groups, per_group, chained, sched, queries, grads, stats, *refs):
    blocks = refs[:groups]
    refs = refs[groups + (1 if chained else 0):]
    query_grad, sums = refs[0], refs[1:1 + groups]
    query_buf, grad_buf, out_buf, in_sem, out_sem = refs[1 + groups:]
    heads = queries.shape[2] // 128
    rows = queries.shape[1]
    scaling = 128 ** -0.5
    slots = groups * per_group

    def fetch(slot, tile):
        return (
            pltpu.make_async_copy(queries.at[tile], query_buf.at[slot], in_sem.at[slot, 0]),
            pltpu.make_async_copy(grads.at[tile], grad_buf.at[slot], in_sem.at[slot, 1]),
        )

    def give(slot, tile):
        return pltpu.make_async_copy(out_buf.at[slot], query_grad.at[tile], out_sem.at[slot])

    def each(action):
        def step(slot, _):
            for turn in range(2):
                @pl.when(sched[slot, 2] > turn)
                def _():
                    action(2 * slot + turn, sched[slot, turn])
            return 0
        lax.fori_loop(0, slots, step, 0)

    def start(slot, tile):
        for copy in fetch(slot, tile):
            copy.start()

    each(start)

    def stacked(buf, slot):
        return jnp.concatenate([buf[slot, :, h * 128:(h + 1) * 128] for h in range(heads)], axis=0)

    def one(slot, tile, keys, values):
        for copy in fetch(slot, tile):
            copy.wait()
        query_part, key_part, value_part = tile_grads(
            stacked(query_buf, slot), stacked(grad_buf, slot), keys, values, stats[tile], scaling)
        query_part = query_part.astype(jnp.bfloat16)
        for h in range(heads):
            out_buf[slot, :, h * 128:(h + 1) * 128] = query_part[h * rows:(h + 1) * rows]
        give(slot, tile).start()
        return key_part, value_part

    for group in range(groups):
        def step(i, _, group=group):
            slot = group * per_group + i
            count = sched[slot, 2]
            block, total = blocks[group], sums[group]

            def store(key_part, value_part):
                total[i, :, 0:128] = key_part.astype(jnp.bfloat16)
                total[i, :, 128:256] = value_part.astype(jnp.bfloat16)

            @pl.when(count == 0)
            def _():
                total[i] = jnp.zeros(total.shape[1:], total.dtype)

            @pl.when(count == 1)
            def _():
                store(*one(2 * slot, sched[slot, 0], block[i, :, 0:128], block[i, :, 128:256]))

            @pl.when(count == 2)
            def _():
                keys, values = block[i, :, 0:128], block[i, :, 128:256]
                first = one(2 * slot, sched[slot, 0], keys, values)
                second = one(2 * slot + 1, sched[slot, 1], keys, values)
                store(first[0] + second[0], first[1] + second[1])
            return 0
        lax.fori_loop(0, per_group, step, 0)

    each(lambda slot, tile: give(slot, tile).wait())


def stage(sched, queries, grads, stats, blocks, query_grad):
    groups, per_group = len(blocks), blocks[0].shape[0]
    tiles = groups * per_group * 2
    rows, width = queries.shape[1:]
    whole = pl.BlockSpec(memory_space=pltpu.VMEM)
    away = pl.BlockSpec(memory_space=pl.ANY)
    chained = query_grad is not None
    operands = [sched, queries, grads, stats, *blocks] + ([query_grad] if chained else [])
    return pl.pallas_call(
        functools.partial(stage_kernel, groups, per_group, chained),
        out_shape=[jax.ShapeDtypeStruct(queries.shape, queries.dtype)]
        + [jax.ShapeDtypeStruct(b.shape, b.dtype) for b in blocks],
        in_specs=[pl.BlockSpec(memory_space=pltpu.SMEM), away, away, whole]
        + [whole] * groups + ([away] if chained else []),
        out_specs=[away] + [whole] * groups,
        scratch_shapes=[
            pltpu.VMEM((tiles, rows, width), queries.dtype),
            pltpu.VMEM((tiles, rows, width), queries.dtype),
            pltpu.VMEM((tiles, rows, width), queries.dtype),
            pltpu.SemaphoreType.DMA((tiles, 2)),
            pltpu.SemaphoreType.DMA((tiles,)),
        ],
        input_output_aliases={len(operands) - 1: 0} if chained else {},
        compiler_params=pltpu.CompilerParams(vmem_limit_bytes=24 << 20),
        cost_estimate=pl.CostEstimate(
            flops=6 * 5 * 2 * 256 * 256 * 128, bytes_accessed=4 << 20, transcendentals=6 * 65536),
        name="stage",
    )(*operands)


def add(*parts):
    total = parts[0].astype(jnp.float32)
    for part in parts[1:]:
        total = total + part.astype(jnp.float32)
    return total.astype(jnp.bfloat16)


def shards(queries, output_gradient, prefix_keys, prefix_values, tile_prefix, suffix_lse, suffix_dot):
    tile_count, row_count, _ = queries.shape
    dp = lax.axis_index("dp")
    pos = lax.axis_index("pos")
    z, y, core = dp // (2 * SIDE), dp // 2 % SIDE, dp % 2

    own_half = jnp.concatenate([prefix_keys[0], prefix_values[0]], axis=1)
    own = jnp.concatenate([own_half, swap_pos(own_half)], axis=0)
    line = jnp.stack([own, shift(own, False, 1), shift(own, False, 2), shift(own, False, 3)])
    mine = [line, shift(line, True, 1), shift(line, True, 3), shift(line, True, 2)]
    order = [0, 1, 3, 2]
    theirs = [swap_cores(group) for group in mine]

    target = lax.dynamic_slice(tile_prefix[:, 0], (dp * tile_count,), (tile_count,))
    far = jnp.array(order, jnp.int32).reshape(4, 1, 1)
    near = jnp.arange(4, dtype=jnp.int32).reshape(1, 1, 4)
    held_core = (core + jnp.arange(2, dtype=jnp.int32).reshape(1, 2, 1)) % 2
    along_y = jnp.where(held_core == 0, near, far)
    along_z = jnp.where(held_core == 0, far, near)
    named = (z - along_z) % SIDE * (2 * SIDE) + (y - along_y) % SIDE * 2 + held_core
    match = named.reshape(4, 8, 1) == target
    ids = lax.broadcasted_iota(jnp.int32, match.shape, 2)
    sched = jnp.stack(
        [
            jnp.min(jnp.where(match, ids, tile_count), axis=2),
            jnp.max(jnp.where(match, ids, -1), axis=2),
            jnp.sum(match.astype(jnp.int32), axis=2),
        ],
        axis=2,
    )

    def own_rows(x):
        x = jnp.transpose(x, (0, 2, 1))
        x = lax.dynamic_slice(
            x, (dp * tile_count, 0, pos * row_count), (tile_count, x.shape[1], row_count))
        return x.reshape(tile_count, 1, -1)

    stats = jnp.concatenate([own_rows(suffix_lse), own_rows(suffix_dot)], axis=1)

    query_grad = None
    parts = []
    for turn in range(4):
        query_grad, here, there = stage(
            sched[turn], queries, output_gradient, stats, [mine[turn], theirs[turn]], query_grad)
        parts.append(add(here, swap_cores(there)))
    line_sum = add(parts[0], *[shift(parts[turn], True, -order[turn]) for turn in (1, 2, 3)])
    own_sum = add(line_sum[0], *[shift(line_sum[k], False, -k) for k in (1, 2, 3)])
    half = own_sum.shape[0] // 2
    total = add(own_sum[:half], swap_pos(own_sum[half:]))
    return query_grad, total[None, :, 0:128], total[None, :, 128:256]


def solution(mesh):
    in_specs = (
        P("dp", "pos", "head"),
        P("dp", "pos", "head"),
        P("dp", "pos", "head"),
        P("dp", "pos", "head"),
        P(),
        P(None, None, "head"),
        P(None, None, "head"),
    )
    out_specs = (P("dp", "pos", "head"), P("dp", "pos", "head"), P("dp", "pos", "head"))
    return jax.shard_map(shards, mesh=mesh, in_specs=in_specs, out_specs=out_specs, check_vma=False)
```

time: 674 us -> 112 us (0.17); the launches traced: 660 us -> 111 us
  waiting for transfers between devices: 289 us -> 39.9 us
  local copies, waits for them, and re-layouts: 164 us -> 7.67 us
  blocking collectives: 131 us -> 0 us
  matrix products: 47 us -> 0 us
  Pallas kernels: 0 us -> 30 us
  starting transfers between devices: 8.07 us -> 27.4 us
  between operations: 14.3 us -> 0.87 us
    all_gather x2 -> x0, waiting for transfers between devices: 133 us -> none  [the longest x1 109 us: shards(): lax.all_gather(came_grad, 'pos', axis=2, tiled=True)]
    all_to_all x2 -> x0, blocking collectives: 114 us -> none  [the longest x1 59.4 us: shards(): lax.all_to_all(send_query, 'dp', split_axis=0, concat_axis=0, tiled=True)]
    reduce_scatter x1 -> x0, waiting for transfers between devices: 103 us -> none  [shards(): lax.psum_scatter(query_all.astype(jnp.bfloat16), 'pos', scatter_dimension...]
    reshape x16 -> x2, local copies, waits for them, and re-layouts: 59.9 us -> 0.2 us  [own_rows(): return x.reshape(tile_count, 1, -1)]
    all_to_all x1 -> x0, waiting for transfers between devices: 52.8 us -> none  [shards(): lax.all_to_all(query_mine, 'dp', split_axis=0, concat_axis=0, tiled=True)]
    dot_general x33 -> x0, matrix products: 47 us -> none  [the longest x4 14.5 us: block_grads(): jnp.einsum('nd,jd->nj', grad_rows, value_rows, preferred_element_type=jnp...]
    ppermute x0 -> x22, waiting for transfers between devices: none -> 39.9 us  [the longest x12 34.5 us: shift(): return lax.ppermute(x, 'dp', ring_pairs(second, step))]
    dynamic_slice x13 -> x1, local copies, waits for them, and re-layouts: 37.5 us -> 0.93 us  [own_rows(): lax.dynamic_slice(x, (dp * tile_count, 0, pos * row_count), (tile_count,...]
  transfers between devices with their start and end apart: 4 -> 22, of which waited for: 4 -> 13; matrix products, arithmetic and copies ran while one was open for 4% -> 5% of each run, Pallas kernels for 0% -> 27%
where the time goes in v1:
time: 112 us; the launch traced here: 111 us
  waiting for transfers between devices  39.9 us (36%)
  Pallas kernels  30 us (27%)
  starting transfers between devices  27.4 us (24%)
  local copies, waits for them, and re-layouts  7.67 us (7%)
  other arithmetic  5.26 us (5%)
    ppermute x12, waiting for transfers between devices, shift(): return lax.ppermute(x, 'dp', ring_pairs(second, step))  34.5 us
    pallas_call x4, Pallas kernels, stage(): pl.pallas_call(functools.partial(stage_kernel, groups, per_group, chained...  30 us
    ppermute x12, starting transfers between devices, shift(): return lax.ppermute(x, 'dp', ring_pairs(second, step))  21.2 us
    ppermute x2, waiting for transfers between devices, swap_pos(): return lax.ppermute(x, 'pos', [(0, 1), (1, 0)])  5.47 us
    unnamed x28, local copies, waits for them, and re-layouts  5.06 us
    ppermute x2, starting transfers between devices, swap_pos(): return lax.ppermute(x, 'pos', [(0, 1), (1, 0)])  3.22 us
    ppermute x8, starting transfers between devices, swap_cores(): return lax.ppermute(x, 'dp', core_pairs())  2.99 us
    convert_element_type x6, other arithmetic, add(): return total.astype(jnp.bfloat16)  2.98 us
  transfers between devices with their start and end apart: 22, of which 13 were waited for; matrix products, arithmetic and copies ran while one was open for 5% of the time, Pallas kernels for 27%

profile of v1, /device:TPU:0, one launch (start us, length us, event | category | flops | bytes accessed | tf_op | source)
XLA Modules:
  0.0 111.1 jit_solution(12167141540510149335)
XLA Ops:
  1.6 1.6 %collective-permute-start = (bf16[128,256]{1,0:T(8,128)(2,1)S(1)}, bf16[128,256]{1,0:T(8,128)(2,1)S(1)}, u32[]{:S(2)}, u32[]{:S(2)}) collective-permute-start(bf16[128,256]{1,0:T(8,128)(2,1)S(1)} %pad_maximum_fusion.2), channel_id=1, source_target_pairs={{0,1},{1,0},{2,3},{3,2},{4,5},{5,4},{6,7},{7,6},{8,9},{9,8},{10,11... | collective-permute-start | bytes 196616 | tf_op jit(solution)/shard_map/ppermute | solution.py:43
  3.2 2.7 %collective-permute-done = bf16[128,256]{1,0:T(8,128)(2,1)S(1)} collective-permute-done((bf16[128,256]{1,0:T(8,128)(2,1)S(1)}, bf16[128,256]{1,0:T(8,128)(2,1)S(1)}, u32[]{:S(2)}, u32[]{:S(2)}) %collective-permute-start) | collective-permute-done | bytes 65568 | tf_op jit(solution)/shard_map/ppermute | solution.py:43
  6.7 1.7 %collective-permute-start.1 = (bf16[256,256]{1,0:T(8,128)(2,1)S(1)}, bf16[256,256]{1,0:T(8,128)(2,1)S(1)}, u32[]{:S(2)}, u32[]{:S(2)}) collective-permute-start(bf16[256,256]{1,0:T(8,128)(2,1)S(1)} %get-tuple-element.34), channel_id=1, source_target_pairs={{0,8},{4,36},{8,16},{12,44},{16,24},{20,52},{24,0},{28,60},{32,40}... | collective-permute-start | bytes 393224 | tf_op jit(solution)/shard_map/ppermute | solution.py:35
  8.4 2.9 %collective-permute-start.2 = (bf16[256,256]{1,0:T(8,128)(2,1)S(1)}, bf16[256,256]{1,0:T(8,128)(2,1)S(1)}, u32[]{:S(2)}, u32[]{:S(2)}) collective-permute-start(bf16[256,256]{1,0:T(8,128)(2,1)S(1)} %get-tuple-element.34), channel_id=1, source_target_pairs={{0,16},{4,68},{8,24},{12,76},{16,0},{20,84},{24,8},{28,92},{32,48}... | collective-permute-start | bytes 393224 | tf_op jit(solution)/shard_map/ppermute | solution.py:35
  13.0 2.7 %collective-permute-done.2 = bf16[256,256]{1,0:T(8,128)(2,1)S(1)} collective-permute-done((bf16[256,256]{1,0:T(8,128)(2,1)S(1)}, bf16[256,256]{1,0:T(8,128)(2,1)S(1)}, u32[]{:S(2)}, u32[]{:S(2)}) %collective-permute-start.2) | collective-permute-done | bytes 131104 | tf_op jit(solution)/shard_map/ppermute | solution.py:35
  16.4 2.0 %collective-permute-start.8 = (bf16[4,256,256]{2,1,0:T(8,128)(2,1)S(1)}, bf16[4,256,256]{2,1,0:T(8,128)(2,1)S(1)}, u32[]{:S(2)}, u32[]{:S(2)}) collective-permute-start(bf16[4,256,256]{2,1,0:T(8,128)(2,1)S(1)} %pad_maximum_fusion.refs_0_), channel_id=1, source_target_pairs={{0,32},{4,12},{8,40},{12,20},{16,48},{20,28},{24,56},{28,4},{32,64... | collective-permute-start | bytes 1572872 | tf_op jit(solution)/shard_map/ppermute | solution.py:35
  18.7 2.2 %collective-permute-start.6 = (bf16[4,256,256]{2,1,0:T(8,128)(2,1)S(1)}, bf16[4,256,256]{2,1,0:T(8,128)(2,1)}, u32[]{:S(2)}, u32[]{:S(2)}) collective-permute-start(bf16[4,256,256]{2,1,0:T(8,128)(2,1)S(1)} %pad_maximum_fusion.refs_0_), channel_id=1, source_target_pairs={{0,96},{4,28},{8,104},{12,4},{16,112},{20,12},{24,120},{28,20},{32... | collective-permute-start | bytes 1572872 | tf_op jit(solution)/shard_map/ppermute | solution.py:35
  21.4 1.9 %collective-permute-start.4 = (bf16[4,256,256]{2,1,0:T(8,128)(2,1)S(1)}, bf16[4,256,256]{2,1,0:T(8,128)(2,1)}, u32[]{:S(2)}, u32[]{:S(2)}) collective-permute-start(bf16[4,256,256]{2,1,0:T(8,128)(2,1)S(1)} %pad_maximum_fusion.refs_0_), channel_id=1, source_target_pairs={{0,64},{4,20},{8,72},{12,28},{16,80},{20,4},{24,88},{28,12},{32,96... | collective-permute-start | bytes 1572872 | tf_op jit(solution)/shard_map/ppermute | solution.py:35
  23.3 4.3 %collective-permute-done.8.refs_0_ = bf16[4,256,256]{2,1,0:T(8,128)(2,1)S(1)} collective-permute-done((bf16[4,256,256]{2,1,0:T(8,128)(2,1)S(1)}, bf16[4,256,256]{2,1,0:T(8,128)(2,1)S(1)}, u32[]{:S(2)}, u32[]{:S(2)}) %collective-permute-start.8) | collective-permute-done | bytes 524320 | tf_op jit(solution)/shard_map/ppermute | solution.py:35
  27.8 5.5 %collective-permute-done.6.refs_0_ = bf16[4,256,256]{2,1,0:T(8,128)(2,1)} collective-permute-done((bf16[4,256,256]{2,1,0:T(8,128)(2,1)S(1)}, bf16[4,256,256]{2,1,0:T(8,128)(2,1)}, u32[]{:S(2)}, u32[]{:S(2)}) %collective-permute-start.6) | collective-permute-done | bytes 524320 | tf_op jit(solution)/shard_map/ppermute | solution.py:35
  35.1 1.4 %copy-done.2 = bf16[24,64,512]{2,1,0:T(8,128)(2,1)S(1)} copy-done((bf16[24,64,512]{2,1,0:T(8,128)(2,1)S(1)}, bf16[24,64,512]{2,1,0:T(8,128)(2,1)}, u32[]{:S(2)}) %copy-start.2) | copy-done | bytes 1572888
  36.5 8.2 %stage.4 = (bf16[24,64,512]{2,1,0:T(8,128)(2,1)}, bf16[4,256,256]{2,1,0:T(8,128)(2,1)S(1)}, bf16[4,256,256]{2,1,0:T(8,128)(2,1)S(1)}) custom-call(s32[8,3]{1,0:T(8,128)S(1)} %bitcast.35, bf16[24,64,512]{2,1,0:T(8,128)(2,1)S(1)} %copy-done.1, bf16[24,64,512]{2,1,0:T(8,128)(2,1)S(1)} %copy-done.2, f32[24,2,256]{2,1,0:T(2,128)S(1)} %pad_maximum_fusion.3.stats, ...), custom_call_target="tpu_custom_call" | custom-call | flops 503316480 | bytes 4194304 | tf_op jit(solution)/shard_map/stage/pallas_call | solution.py:155
  46.7 8.8 %stage.5 = (bf16[24,64,512]{2,1,0:T(8,128)(2,1)}, bf16[4,256,256]{2,1,0:T(8,128)(2,1)S(1)}, bf16[4,256,256]{2,1,0:T(8,128)(2,1)}) custom-call(s32[8,3]{1,0:T(8,128)S(1)} %bitcast.36, bf16[24,64,512]{2,1,0:T(8,128)(2,1)S(1)} %copy-done.1, bf16[24,64,512]{2,1,0:T(8,128)(2,1)S(1)} %copy-done.2, ...), custom_call_target="tpu_custom_call", output_to_operand_aliasing={{0}: (6, {})} | custom-call | flops 503316480 | bytes 4194304 | tf_op jit(solution)/shard_map/stage/pallas_call | solution.py:155
  56.4 6.5 %stage.6 = (bf16[24,64,512]{2,1,0:T(8,128)(2,1)}, bf16[4,256,256]{2,1,0:T(8,128)(2,1)S(1)}, bf16[4,256,256]{2,1,0:T(8,128)(2,1)}) custom-call(s32[8,3]{1,0:T(8,128)S(1)} %bitcast.38, bf16[24,64,512]{2,1,0:T(8,128)(2,1)S(1)} %copy-done.1, bf16[24,64,512]{2,1,0:T(8,128)(2,1)S(1)} %copy-done.3, ...), custom_call_target="tpu_custom_call", output_to_operand_aliasing={{0}: (6, {})} | custom-call | flops 503316480 | bytes 4194304 | tf_op jit(solution)/shard_map/stage/pallas_call | solution.py:155
  65.1 6.5 %stage.7 = (bf16[24,64,512]{2,1,0:T(8,128)(2,1)}, bf16[4,256,256]{2,1,0:T(8,128)(2,1)S(1)}, bf16[4,256,256]{2,1,0:T(8,128)(2,1)S(1)}) custom-call(s32[8,3]{1,0:T(8,128)S(1)} %bitcast.37, bf16[24,64,512]{2,1,0:T(8,128)(2,1)S(1)} %copy-done.1, bf16[24,64,512]{2,1,0:T(8,128)(2,1)S(1)} %copy-done.3, ...), custom_call_target="tpu_custom_call", output_to_operand_aliasing={{0}: (6, {})} | custom-call | flops 503316480 | bytes 4194304 | tf_op jit(solution)/shard_map/stage/pallas_call | solution.py:155
  74.2 5.0 %collective-permute-start.13 = (bf16[4,256,256]{2,1,0:T(8,128)(2,1)S(1)}, bf16[4,256,256]{2,1,0:T(8,128)(2,1)S(1)}, u32[]{:S(2)}, u32[]{:S(2)}) collective-permute-start(bf16[4,256,256]{2,1,0:T(8,128)(2,1)S(1)} %add_convert_fusion.3), channel_id=1, source_target_pairs={{0,96},{4,28},{8,104},{12,4},{16,112},{20,12},{24,120},{28,20},{32... | collective-permute-start | bytes 1572872 | tf_op jit(solution)/shard_map/ppermute | solution.py:35
  80.6 1.6 %collective-permute-start.17 = (bf16[4,256,256]{2,1,0:T(8,128)(2,1)S(1)}, bf16[4,256,256]{2,1,0:T(8,128)(2,1)S(1)}, u32[]{:S(2)}, u32[]{:S(2)}) collective-permute-start(bf16[4,256,256]{2,1,0:T(8,128)(2,1)S(1)} %add_convert_fusion.1), channel_id=1, source_target_pairs={{0,64},{4,20},{8,72},{12,28},{16,80},{20,4},{24,88},{28,12},{32,96... | collective-permute-start | bytes 1572872 | tf_op jit(solution)/shard_map/ppermute | solution.py:35
  82.2 9.3 %collective-permute-done.13 = bf16[4,256,256]{2,1,0:T(8,128)(2,1)S(1)} collective-permute-done((bf16[4,256,256]{2,1,0:T(8,128)(2,1)S(1)}, bf16[4,256,256]{2,1,0:T(8,128)(2,1)S(1)}, u32[]{:S(2)}, u32[]{:S(2)}) %collective-permute-start.13) | collective-permute-done | bytes 524320 | tf_op jit(solution)/shard_map/ppermute | solution.py:35
  91.5 5.0 %collective-permute-done.15 = bf16[4,256,256]{2,1,0:T(8,128)(2,1)S(1)} collective-permute-done((bf16[4,256,256]{2,1,0:T(8,128)(2,1)S(1)}, bf16[4,256,256]{2,1,0:T(8,128)(2,1)S(1)}, u32[]{:S(2)}, u32[]{:S(2)}) %collective-permute-start.15) | collective-permute-done | bytes 524320 | tf_op jit(solution)/shard_map/ppermute | solution.py:35
  96.9 1.6 %collective-permute-start.18 = (bf16[256,256]{1,0:T(8,128)(2,1)S(1)}, bf16[256,256]{1,0:T(8,128)(2,1)S(1)}, u32[]{:S(2)}, u32[]{:S(2)}) collective-permute-start(bf16[256,256]{1,0:T(8,128)(2,1)S(1)} %get-tuple-element.30), channel_id=1, source_target_pairs={{0,24},{4,100},{8,0},{12,108},{16,8},{20,116},{24,16},{28,124},{32... | collective-permute-start | bytes 393224 | tf_op jit(solution)/shard_map/ppermute | solution.py:35
  99.4 2.5 %collective-permute-done.18 = bf16[256,256]{1,0:T(8,128)(2,1)S(1)} collective-permute-done((bf16[256,256]{1,0:T(8,128)(2,1)S(1)}, bf16[256,256]{1,0:T(8,128)(2,1)S(1)}, u32[]{:S(2)}, u32[]{:S(2)}) %collective-permute-start.18) | collective-permute-done | bytes 131104 | tf_op jit(solution)/shard_map/ppermute | solution.py:35
  101.9 3.1 %collective-permute-done.19 = bf16[256,256]{1,0:T(8,128)(2,1)S(1)} collective-permute-done((bf16[256,256]{1,0:T(8,128)(2,1)S(1)}, bf16[256,256]{1,0:T(8,128)(2,1)S(1)}, u32[]{:S(2)}, u32[]{:S(2)}) %collective-permute-start.19) | collective-permute-done | bytes 131104 | tf_op jit(solution)/shard_map/ppermute | solution.py:35
  106.1 1.6 %collective-permute-start.21 = (bf16[128,256]{1,0:T(8,128)(2,1)S(1)}, bf16[128,256]{1,0:T(8,128)(2,1)S(1)}, u32[]{:S(2)}, u32[]{:S(2)}) collective-permute-start(bf16[128,256]{1,0:T(8,128)(2,1)S(1)} %slice.57), channel_id=1, source_target_pairs={{0,1},{1,0},{2,3},{3,2},{4,5},{5,4},{6,7},{7,6},{8,9},{9,8},{10,11... | collective-permute-start | bytes 196616 | tf_op jit(solution)/shard_map/ppermute | solution.py:43
  107.7 2.8 %collective-permute-done.21 = bf16[128,256]{1,0:T(8,128)(2,1)S(1)} collective-permute-done((bf16[128,256]{1,0:T(8,128)(2,1)S(1)}, bf16[128,256]{1,0:T(8,128)(2,1)S(1)}, u32[]{:S(2)}, u32[]{:S(2)}) %collective-permute-start.21) | collective-permute-done | bytes 65568 | tf_op jit(solution)/shard_map/ppermute | solution.py:43
  (85 shorter events, 18.9 us)
Async XLA Ops:
  0.6 20.3 %copy-start = (s32[768,1]{0,1:T(1,128)S(1)}, s32[768,1]{0,1:T(1,128)}, u32[]{:S(2)}) copy-start(s32[768,1]{0,1:T(1,128)} %param.12) | copy-start | bytes 9220
  0.7 34.5 %copy-start.1 = (bf16[24,64,512]{2,1,0:T(8,128)(2,1)S(1)}, bf16[24,64,512]{2,1,0:T(8,128)(2,1)}, u32[]{:S(2)}) copy-start(bf16[24,64,512]{2,1,0:T(8,128)(2,1)} %queries.7) | copy-start | bytes 4718596
  1.6 4.3 %collective-permute-start = (bf16[128,256]{1,0:T(8,128)(2,1)S(1)}, bf16[128,256]{1,0:T(8,128)(2,1)S(1)}, u32[]{:S(2)}, u32[]{:S(2)}) collective-permute-start(bf16[128,256]{1,0:T(8,128)(2,1)S(1)} %pad_maximum_fusion.2), channel_id=1, source_target_pairs={{0,1},{1,0},{2,3},{3,2},{4,5},{5,4},{6,7},{7,6},{8,9},{9,8},{10,11... | collective-permute-start | bytes 196616 | tf_op jit(solution)/shard_map/ppermute | solution.py:43
  6.7 6.2 %collective-permute-start.1 = (bf16[256,256]{1,0:T(8,128)(2,1)S(1)}, bf16[256,256]{1,0:T(8,128)(2,1)S(1)}, u32[]{:S(2)}, u32[]{:S(2)}) collective-permute-start(bf16[256,256]{1,0:T(8,128)(2,1)S(1)} %get-tuple-element.34), channel_id=1, source_target_pairs={{0,8},{4,36},{8,16},{12,44},{16,24},{20,52},{24,0},{28,60},{32,40}... | collective-permute-start | bytes 393224 | tf_op jit(solution)/shard_map/ppermute | solution.py:35
  8.4 7.2 %collective-permute-start.2 = (bf16[256,256]{1,0:T(8,128)(2,1)S(1)}, bf16[256,256]{1,0:T(8,128)(2,1)S(1)}, u32[]{:S(2)}, u32[]{:S(2)}) collective-permute-start(bf16[256,256]{1,0:T(8,128)(2,1)S(1)} %get-tuple-element.34), channel_id=1, source_target_pairs={{0,16},{4,68},{8,24},{12,76},{16,0},{20,84},{24,8},{28,92},{32,48}... | collective-permute-start | bytes 393224 | tf_op jit(solution)/shard_map/ppermute | solution.py:35
  11.3 5.0 %collective-permute-start.3 = (bf16[256,256]{1,0:T(8,128)(2,1)S(1)}, bf16[256,256]{1,0:T(8,128)(2,1)S(1)}, u32[]{:S(2)}, u32[]{:S(2)}) collective-permute-start(bf16[256,256]{1,0:T(8,128)(2,1)S(1)} %get-tuple-element.34), channel_id=1, source_target_pairs={{0,24},{4,100},{8,0},{12,108},{16,8},{20,116},{24,16},{28,124},{32... | collective-permute-start | bytes 393224 | tf_op jit(solution)/shard_map/ppermute | solution.py:35
  16.4 11.3 %collective-permute-start.8 = (bf16[4,256,256]{2,1,0:T(8,128)(2,1)S(1)}, bf16[4,256,256]{2,1,0:T(8,128)(2,1)S(1)}, u32[]{:S(2)}, u32[]{:S(2)}) collective-permute-start(bf16[4,256,256]{2,1,0:T(8,128)(2,1)S(1)} %pad_maximum_fusion.refs_0_), channel_id=1, source_target_pairs={{0,32},{4,12},{8,40},{12,20},{16,48},{20,28},{24,56},{28,4},{32,64... | collective-permute-start | bytes 1572872 | tf_op jit(solution)/shard_map/ppermute | solution.py:35
  18.7 14.5 %collective-permute-start.6 = (bf16[4,256,256]{2,1,0:T(8,128)(2,1)S(1)}, bf16[4,256,256]{2,1,0:T(8,128)(2,1)}, u32[]{:S(2)}, u32[]{:S(2)}) collective-permute-start(bf16[4,256,256]{2,1,0:T(8,128)(2,1)S(1)} %pad_maximum_fusion.refs_0_), channel_id=1, source_target_pairs={{0,96},{4,28},{8,104},{12,4},{16,112},{20,12},{24,120},{28,20},{32... | collective-permute-start | bytes 1572872 | tf_op jit(solution)/shard_map/ppermute | solution.py:35
  21.3 13.8 %collective-permute-start.10 = (bf16[4,256,256]{2,1,0:T(8,128)(2,1)S(1)}, bf16[4,256,256]{2,1,0:T(8,128)(2,1)S(1)}, u32[]{:S(2)}, u32[]{:S(2)}) collective-permute-start(bf16[4,256,256]{2,1,0:T(8,128)(2,1)S(1)} %pad_maximum_fusion.refs_0_), channel_id=1, source_target_pairs={{0,4},{4,0},{8,12},{12,8},{16,20},{20,16},{24,28},{28,24},{32,36},... | collective-permute-start | bytes 1572872 | tf_op jit(solution)/shard_map/ppermute | solution.py:39
  21.4 13.4 %collective-permute-start.4 = (bf16[4,256,256]{2,1,0:T(8,128)(2,1)S(1)}, bf16[4,256,256]{2,1,0:T(8,128)(2,1)}, u32[]{:S(2)}, u32[]{:S(2)}) collective-permute-start(bf16[4,256,256]{2,1,0:T(8,128)(2,1)S(1)} %pad_maximum_fusion.refs_0_), channel_id=1, source_target_pairs={{0,64},{4,20},{8,72},{12,28},{16,80},{20,4},{24,88},{28,12},{32,96... | collective-permute-start | bytes 1572872 | tf_op jit(solution)/shard_map/ppermute | solution.py:35
  27.6 17.9 %collective-permute-start.9 = (bf16[4,256,256]{2,1,0:T(8,128)(2,1)S(1)}, bf16[4,256,256]{2,1,0:T(8,128)(2,1)}, u32[]{:S(2)}, u32[]{:S(2)}) collective-permute-start(bf16[4,256,256]{2,1,0:T(8,128)(2,1)S(1)} %collective-permute-done.8.refs_0_), channel_id=1, source_target_pairs={{0,4},{4,0},{8,12},{12,8},{16,20},{20,16},{24,28},{28,24},{32,36},... | collective-permute-start | bytes 1572872 | tf_op jit(solution)/shard_map/ppermute | solution.py:39
  33.2 23.2 %collective-permute-start.7 = (bf16[4,256,256]{2,1,0:T(8,128)(2,1)}, bf16[4,256,256]{2,1,0:T(8,128)(2,1)}, u32[]{:S(2)}, u32[]{:S(2)}) collective-permute-start(bf16[4,256,256]{2,1,0:T(8,128)(2,1)} %collective-permute-done.6.refs_0_), channel_id=1, source_target_pairs={{0,4},{4,0},{8,12},{12,8},{16,20},{20,16},{24,28},{28,24},{32,36},... | collective-permute-start | bytes 1572872 | tf_op jit(solution)/shard_map/ppermute | solution.py:39
  34.8 30.2 %collective-permute-start.5 = (bf16[4,256,256]{2,1,0:T(8,128)(2,1)}, bf16[4,256,256]{2,1,0:T(8,128)(2,1)}, u32[]{:S(2)}, u32[]{:S(2)}) collective-permute-start(bf16[4,256,256]{2,1,0:T(8,128)(2,1)} %collective-permute-done.4.refs_0_), channel_id=1, source_target_pairs={{0,4},{4,0},{8,12},{12,8},{16,20},{20,16},{24,28},{28,24},{32,36},... | collective-permute-start | bytes 1572872 | tf_op jit(solution)/shard_map/ppermute | solution.py:39
  56.3 16.6 %collective-permute-start.12 = (bf16[4,256,256]{2,1,0:T(8,128)(2,1)}, bf16[4,256,256]{2,1,0:T(8,128)(2,1)}, u32[]{:S(2)}, u32[]{:S(2)}) collective-permute-start(bf16[4,256,256]{2,1,0:T(8,128)(2,1)} %get-tuple-element.22), channel_id=1, source_target_pairs={{0,4},{4,0},{8,12},{12,8},{16,20},{20,16},{24,28},{28,24},{32,36},... | collective-permute-start | bytes 1572872 | tf_op jit(solution)/shard_map/ppermute | solution.py:39
  63.8 15.4 %collective-permute-start.14 = (bf16[4,256,256]{2,1,0:T(8,128)(2,1)}, bf16[4,256,256]{2,1,0:T(8,128)(2,1)}, u32[]{:S(2)}, u32[]{:S(2)}) collective-permute-start(bf16[4,256,256]{2,1,0:T(8,128)(2,1)} %get-tuple-element.24), channel_id=1, source_target_pairs={{0,4},{4,0},{8,12},{12,8},{16,20},{20,16},{24,28},{28,24},{32,36},... | collective-permute-start | bytes 1572872 | tf_op jit(solution)/shard_map/ppermute | solution.py:39
  65.1 17.1 %collective-permute-start.11 = (bf16[4,256,256]{2,1,0:T(8,128)(2,1)}, bf16[4,256,256]{2,1,0:T(8,128)(2,1)S(1)}, u32[]{:S(2)}, u32[]{:S(2)}) collective-permute-start(bf16[4,256,256]{2,1,0:T(8,128)(2,1)} %copy-done.12), channel_id=1, source_target_pairs={{0,4},{4,0},{8,12},{12,8},{16,20},{20,16},{24,28},{28,24},{32,36},... | collective-permute-start | bytes 1572872 | tf_op jit(solution)/shard_map/ppermute | solution.py:39
  71.6 8.9 %collective-permute-start.16 = (bf16[4,256,256]{2,1,0:T(8,128)(2,1)S(1)}, bf16[4,256,256]{2,1,0:T(8,128)(2,1)S(1)}, u32[]{:S(2)}, u32[]{:S(2)}) collective-permute-start(bf16[4,256,256]{2,1,0:T(8,128)(2,1)S(1)} %get-tuple-element.26), channel_id=1, source_target_pairs={{0,4},{4,0},{8,12},{12,8},{16,20},{20,16},{24,28},{28,24},{32,36},... | collective-permute-start | bytes 1572872 | tf_op jit(solution)/shard_map/ppermute | solution.py:39
  74.2 17.3 %collective-permute-start.13 = (bf16[4,256,256]{2,1,0:T(8,128)(2,1)S(1)}, bf16[4,256,256]{2,1,0:T(8,128)(2,1)S(1)}, u32[]{:S(2)}, u32[]{:S(2)}) collective-permute-start(bf16[4,256,256]{2,1,0:T(8,128)(2,1)S(1)} %add_convert_fusion.3), channel_id=1, source_target_pairs={{0,96},{4,28},{8,104},{12,4},{16,112},{20,12},{24,120},{28,20},{32... | collective-permute-start | bytes 1572872 | tf_op jit(solution)/shard_map/ppermute | solution.py:35
  80.4 16.1 %collective-permute-start.15 = (bf16[4,256,256]{2,1,0:T(8,128)(2,1)S(1)}, bf16[4,256,256]{2,1,0:T(8,128)(2,1)S(1)}, u32[]{:S(2)}, u32[]{:S(2)}) collective-permute-start(bf16[4,256,256]{2,1,0:T(8,128)(2,1)S(1)} %add_convert_fusion.2), channel_id=1, source_target_pairs={{0,32},{4,12},{8,40},{12,20},{16,48},{20,28},{24,56},{28,4},{32,64... | collective-permute-start | bytes 1572872 | tf_op jit(solution)/shard_map/ppermute | solution.py:35
  80.6 15.8 %collective-permute-start.17 = (bf16[4,256,256]{2,1,0:T(8,128)(2,1)S(1)}, bf16[4,256,256]{2,1,0:T(8,128)(2,1)S(1)}, u32[]{:S(2)}, u32[]{:S(2)}) collective-permute-start(bf16[4,256,256]{2,1,0:T(8,128)(2,1)S(1)} %add_convert_fusion.1), channel_id=1, source_target_pairs={{0,64},{4,20},{8,72},{12,28},{16,80},{20,4},{24,88},{28,12},{32,96... | collective-permute-start | bytes 1572872 | tf_op jit(solution)/shard_map/ppermute | solution.py:35
  96.9 5.0 %collective-permute-start.18 = (bf16[256,256]{1,0:T(8,128)(2,1)S(1)}, bf16[256,256]{1,0:T(8,128)(2,1)S(1)}, u32[]{:S(2)}, u32[]{:S(2)}) collective-permute-start(bf16[256,256]{1,0:T(8,128)(2,1)S(1)} %get-tuple-element.30), channel_id=1, source_target_pairs={{0,24},{4,100},{8,0},{12,108},{16,8},{20,116},{24,16},{28,124},{32... | collective-permute-start | bytes 393224 | tf_op jit(solution)/shard_map/ppermute | solution.py:35
  98.4 6.6 %collective-permute-start.19 = (bf16[256,256]{1,0:T(8,128)(2,1)S(1)}, bf16[256,256]{1,0:T(8,128)(2,1)S(1)}, u32[]{:S(2)}, u32[]{:S(2)}) collective-permute-start(bf16[256,256]{1,0:T(8,128)(2,1)S(1)} %get-tuple-element.32), channel_id=1, source_target_pairs={{0,16},{4,68},{8,24},{12,76},{16,0},{20,84},{24,8},{28,92},{32,48}... | collective-permute-start | bytes 393224 | tf_op jit(solution)/shard_map/ppermute | solution.py:35
  98.4 7.6 %collective-permute-start.20 = (bf16[256,256]{1,0:T(8,128)(2,1)S(1)}, bf16[256,256]{1,0:T(8,128)(2,1)S(1)}, u32[]{:S(2)}, u32[]{:S(2)}) collective-permute-start(bf16[256,256]{1,0:T(8,128)(2,1)S(1)} %get-tuple-element.31), channel_id=1, source_target_pairs={{0,8},{4,36},{8,16},{12,44},{16,24},{20,52},{24,0},{28,60},{32,40}... | collective-permute-start | bytes 393224 | tf_op jit(solution)/shard_map/ppermute | solution.py:35
  106.1 4.3 %collective-permute-start.21 = (bf16[128,256]{1,0:T(8,128)(2,1)S(1)}, bf16[128,256]{1,0:T(8,128)(2,1)S(1)}, u32[]{:S(2)}, u32[]{:S(2)}) collective-permute-start(bf16[128,256]{1,0:T(8,128)(2,1)S(1)} %slice.57), channel_id=1, source_target_pairs={{0,1},{1,0},{2,3},{3,2},{4,5},{5,4},{6,7},{7,6},{8,9},{9,8},{10,11... | collective-permute-start | bytes 196616 | tf_op jit(solution)/shard_map/ppermute | solution.py:43
  (12 other events, 92.6 us)

commit v2 on v1

v2 whole, which is shorter than its diff:
```python
import functools
import math

import jax
import jax.numpy as jnp
from jax import lax
from jax.experimental import pallas as pl
from jax.experimental.pallas import tpu as pltpu
from jax.sharding import PartitionSpec as P

SIDE = 4
TILES = 24
PREFIXES = 32
BATCH = 4
LOG2E = math.log2(math.e)
PLACE, TILE, MODE, COUNT, NAMED, PART = 0, 32, 64, 80, 96, 128


def place(z, y, core):
    return (z % SIDE) * 2 * SIDE + (y % SIDE) * 2 + core


def line_groups():
    groups = []
    for core in range(2):
        for other in range(SIDE):
            ring = [place(other, k, 0) if core == 0 else place(k, other, 1) for k in range(SIDE)]
            groups.append([dp * 2 + pos for dp in ring for pos in range(2)])
    return groups


def exchange_line(x):
    return lax.all_to_all(x, ("dp", "pos"), 0, 0, axis_index_groups=line_groups(), tiled=True)


def shift(x, step):
    pairs = []
    for z in range(SIDE):
        for y in range(SIDE):
            pairs.append((place(z, y, 0), place(z + step, y, 0)))
            pairs.append((place(z, y, 1), place(z, y + step, 1)))
    return lax.ppermute(x, "dp", pairs)


def swap_cores(x):
    return lax.ppermute(x, "dp", [(i, i ^ 1) for i in range(2 * SIDE * SIDE)])


def held(x):
    return pltpu.with_memory_space_constraint(x, pltpu.VMEM)


def plan_kernel(spot, target, out, ids, count):
    z, y, core = spot[0], spot[1], spot[2]

    def clear(p, _):
        count[p] = 0
        ids[2 * p] = 0
        ids[2 * p + 1] = 0
        return 0

    lax.fori_loop(0, PREFIXES, clear, 0)

    def note(t, _):
        p = target[t]
        ids[2 * p + count[p]] = t
        count[p] = count[p] + 1
        return 0

    lax.fori_loop(0, TILES, note, 0)

    def where(p):
        far_z, far_y, held_core = p // (2 * SIDE), p // 2 % SIDE, p % 2
        on_first = held_core == 0
        near = jnp.where(on_first, far_y, far_z)
        far = jnp.where(on_first, z - far_z + SIDE, y - far_y + SIDE) % SIDE
        side = (held_core + core) % 2
        late = far == 2
        rank = jnp.where(far == 3, 2, far)
        return jnp.where(late, 1, 0), jnp.where(late, side * 4 + near, side * 12 + rank * 4 + near)

    def pairs(p, ends):
        late, at = where(p)
        base = late * PART
        n = jnp.where(late == 1, ends[1], ends[0])
        out[base + NAMED + at] = count[p]
        for turn in range(2):
            out[base + PLACE + n + turn] = at
            out[base + TILE + n + turn] = ids[2 * p + turn]
        out[base + MODE + n // 2] = 1
        step = jnp.where(count[p] == 2, 2, 0)
        return ends[0] + step * (1 - late), ends[1] + step * late

    def singles(p, ends):
        late, at = where(p)
        base = late * PART
        n = jnp.where(late == 1, ends[1], ends[0])
        out[base + PLACE + n] = at
        out[base + TILE + n] = ids[2 * p]
        out[base + MODE + n // 2] = 0
        step = jnp.where(count[p] == 1, 1, 0)
        return ends[0] + step * (1 - late), ends[1] + step * late

    zero = jnp.int32(0)
    ends = lax.fori_loop(0, PREFIXES, pairs, (zero, zero))
    ends = lax.fori_loop(0, PREFIXES, singles, ends)
    for late in range(2):
        base, n = late * PART, ends[late]
        last = jnp.maximum((n + 1) // 2 - 1, 0)
        out[base + COUNT] = (n + BATCH - 1) // BATCH

        def pad(j, _, base=base, n=n, last=last):
            pair = jnp.minimum(j // 2, last)
            source = jnp.maximum(jnp.minimum(2 * pair + j % 2, n - 1), 0)
            out[base + PLACE + j] = out[base + PLACE + source]
            out[base + TILE + j] = out[base + TILE + source]
            out[base + MODE + j // 2] = out[base + MODE + pair]
            return 0

        lax.fori_loop(n, (n + BATCH - 1) // BATCH * BATCH, pad, 0)


def plan(spot, target):
    small = pl.BlockSpec(memory_space=pltpu.SMEM)
    return pl.pallas_call(
        plan_kernel,
        out_shape=jax.ShapeDtypeStruct((2 * PART,), jnp.int32),
        in_specs=[small, small],
        out_specs=small,
        scratch_shapes=[pltpu.SMEM((2 * PREFIXES,), jnp.int32), pltpu.SMEM((PREFIXES,), jnp.int32)],
        name="plan",
    )(spot, target)


def tile_grads(query, grad, keys, values, stat, scaling):
    nt = (((1,), (1,)), ((), ()))
    tn = (((0,), (0,)), ((), ()))
    f32, half = jnp.float32, jnp.bfloat16
    tiles = range(len(query))
    scores = [
        lax.dot_general(keys[k], query[k], nt, preferred_element_type=f32) * (scaling * LOG2E)
        for k in tiles
    ]
    prob_grad = [
        lax.dot_general(values[k], grad[k], nt, preferred_element_type=f32) for k in tiles
    ]
    prob_half, score_grad = [], []
    for k in tiles:
        suffix_l = stat[k][0:1] * LOG2E
        suffix_d = stat[k][1:2]
        top = jnp.maximum(jnp.max(scores[k], axis=0, keepdims=True), suffix_l)
        raised = jnp.exp2(scores[k] - top)
        suffix_part = jnp.exp2(suffix_l - top)
        inverse = 1.0 / (jnp.sum(raised, axis=0, keepdims=True) + suffix_part)
        moment = jnp.sum(raised * prob_grad[k], axis=0, keepdims=True) + suffix_part * suffix_d
        probs = raised * inverse
        prob_half.append(probs.astype(half))
        score_grad.append((probs * (prob_grad[k] - moment * inverse)).astype(half))
    parts = []
    for k in tiles:
        query_part = lax.dot_general(keys[k], score_grad[k], tn, preferred_element_type=f32)
        parts.append((
            (query_part * scaling).astype(half).T,
            jnp.dot(score_grad[k], query[k], preferred_element_type=f32) * scaling,
            jnp.dot(prob_half[k], grad[k], preferred_element_type=f32),
        ))
    return parts


def stage_kernel(late, sizes, sched, queries, grads, stats, *refs):
    blocks = refs[:len(sizes)]
    query_grad, here, there, near = refs[len(sizes) + late:]
    heads = queries.shape[2] // 128
    rows = queries.shape[1]
    scaling = 128 ** -0.5
    base = late * PART
    places = here.shape[0]
    sums = (here, there)
    spans = []
    for block, size in zip(blocks, sizes):
        spans += [(block, first) for first in range(0, size, 2)]

    def clear(i, _):
        for side in range(2):
            @pl.when(sched[base + NAMED + side * places + i] == 0)
            def _():
                sums[side][i] = jnp.zeros(here.shape[1:], here.dtype)
        return 0

    lax.fori_loop(0, places, clear, 0)

    def stacked(buf, tile):
        return jnp.concatenate(
            [buf[tile, :, h * 128:(h + 1) * 128] for h in range(heads)], axis=0)

    def step(batch, _):
        at = [sched[base + PLACE + batch * BATCH + k] for k in range(BATCH)]
        tile = [sched[base + TILE + batch * BATCH + k] for k in range(BATCH)]
        mode = [sched[base + MODE + batch * (BATCH // 2) + k] for k in range(BATCH // 2)]
        for k in range(BATCH):
            for side in range(2):
                half = len(spans) // 2

                @pl.when(at[k] // places == side)
                def _():
                    for span in range(half):
                        block, first = spans[side * half + span]

                        @pl.when(at[k] % places // 2 == span)
                        def _():
                            near[k] = block[first + at[k] % 2]

        parts = tile_grads(
            [stacked(queries, t) for t in tile], [stacked(grads, t) for t in tile],
            [near[k, :, 0:128] for k in range(BATCH)], [near[k, :, 128:256] for k in range(BATCH)],
            [stats[t] for t in tile], scaling)
        for k in range(BATCH):
            for h in range(heads):
                query_grad[tile[k], :, h * 128:(h + 1) * 128] = parts[k][0][h * rows:(h + 1) * rows]

        def store(spot, key_part, value_part):
            for side in range(2):
                @pl.when(spot // places == side)
                def _():
                    sums[side][spot % places, :, 0:128] = key_part.astype(here.dtype)
                    sums[side][spot % places, :, 128:256] = value_part.astype(here.dtype)

        for pair in range(BATCH // 2):
            a, b = 2 * pair, 2 * pair + 1

            @pl.when(mode[pair] == 1)
            def _():
                store(at[a], parts[a][1] + parts[b][1], parts[a][2] + parts[b][2])

            @pl.when(mode[pair] == 0)
            def _():
                store(at[a], *parts[a][1:])
                store(at[b], *parts[b][1:])
        return 0

    lax.fori_loop(0, sched[base + COUNT], step, 0)


def stage(late, sched, queries, grads, stats, blocks, query_grad):
    sizes = tuple(block.shape[0] for block in blocks)
    places = sum(sizes) // 2
    kind = blocks[0].dtype
    block_shape = blocks[0].shape[1:]
    whole = pl.BlockSpec(memory_space=pltpu.VMEM)
    operands = [queries, grads, stats, *blocks] + ([query_grad] if late else [])
    tiles = TILES * places // (PREFIXES // 2)
    return pl.pallas_call(
        functools.partial(stage_kernel, late, sizes),
        out_shape=[
            pltpu.VMEM(queries.shape, kind),
            pltpu.VMEM((places, *block_shape), kind),
            pltpu.VMEM((places, *block_shape), kind),
        ],
        in_specs=[pl.BlockSpec(memory_space=pltpu.SMEM)] + [whole] * len(operands),
        out_specs=[whole] * 3,
        scratch_shapes=[pltpu.VMEM((BATCH, *block_shape), kind)],
        input_output_aliases={len(operands): 0} if late else {},
        compiler_params=pltpu.CompilerParams(vmem_limit_bytes=16 << 20),
        cost_estimate=pl.CostEstimate(
            flops=tiles * 10 * 256 * 256 * 128, bytes_accessed=0, transcendentals=tiles * 65536),
        name="late_stage" if late else "early_stage",
    )(sched, *[held(x) for x in operands])


def add(*parts):
    total = parts[0].astype(jnp.float32)
    for part in parts[1:]:
        total = total + part.astype(jnp.float32)
    return total.astype(jnp.bfloat16)


def shards(queries, output_gradient, prefix_keys, prefix_values, tile_prefix, suffix_lse, suffix_dot):
    tile_count, row_count, _ = queries.shape
    dp = lax.axis_index("dp")
    pos = lax.axis_index("pos")

    own = jnp.concatenate([prefix_keys[0], prefix_values[0]], axis=1)
    line = exchange_line(jnp.broadcast_to(own, (2 * SIDE, *own.shape))).reshape(SIDE, 256, 256)
    low, high = line[0:2], line[2:4]
    up_low = shift(low, 1)
    down_high = shift(high, -1)
    up_high = shift(high, 1)
    down_low = shift(low, -1)
    far_low = shift(up_low, 1)
    far_high = shift(down_high, -1)
    early = [line, up_low, up_high, down_low, down_high]
    late = [far_low, far_high]
    early = early + [swap_cores(x) for x in early]
    late = late + [swap_cores(x) for x in late]

    target = lax.dynamic_slice(tile_prefix[:, 0], (dp * tile_count,), (tile_count,))
    spot = jnp.stack([dp // (2 * SIDE), dp // 2 % SIDE, dp % 2]).astype(jnp.int32)
    sched = plan(spot, target)

    def own_rows(x):
        x = jnp.transpose(x, (0, 2, 1))
        x = lax.dynamic_slice(
            x, (dp * tile_count, 0, pos * row_count), (tile_count, x.shape[1], row_count))
        return x.reshape(tile_count, 1, -1)

    stats = jnp.concatenate([own_rows(suffix_lse), own_rows(suffix_dot)], axis=1)

    query_grad, here, there = stage(0, sched, queries, output_gradient, stats, early, None)
    back = swap_cores(there)
    query_grad, far_here, far_there = stage(
        1, sched, queries, output_gradient, stats, late, query_grad)
    far_back = swap_cores(far_there)
    from_up = shift(add(here[6:8], back[6:8]), -1)
    from_down = shift(add(here[8:10], back[8:10]), 1)
    via_down = shift(add(far_here[0:2], far_back[0:2]), -1)
    via_up = shift(add(far_here[2:4], far_back[2:4]), 1)
    rest_up = shift(add(here[4:6], back[4:6], via_down), -1)
    rest_down = shift(add(here[10:12], back[10:12], via_up), 1)
    line_sum = jnp.concatenate([
        add(here[0:2], back[0:2], rest_up, from_down),
        add(here[2:4], back[2:4], from_up, rest_down),
    ])
    total = add(*exchange_line(line_sum.reshape(2 * SIDE, *own.shape)))
    return query_grad, total[None, :, 0:128], total[None, :, 128:256]


def solution(mesh):
    in_specs = (
        P("dp", "pos", "head"),
        P("dp", "pos", "head"),
        P("dp", "pos", "head"),
        P("dp", "pos", "head"),
        P(),
        P(None, None, "head"),
        P(None, None, "head"),
    )
    out_specs = (P("dp", "pos", "head"), P("dp", "pos", "head"), P("dp", "pos", "head"))
    return jax.shard_map(shards, mesh=mesh, in_specs=in_specs, out_specs=out_specs, check_vma=False)
```

time: 112 us -> 107 us (0.955)
  blocking collectives: 0 us -> 16.7 us
  Pallas kernels: 30 us -> 15.5 us
  starting transfers between devices: 27.4 us -> 22.6 us
  waiting for transfers between devices: 39.9 us -> 35.4 us
  local copies, waits for them, and re-layouts: 7.67 us -> 12 us
  other arithmetic: 5.26 us -> 3.12 us
    all_to_all x0 -> x1, blocking collectives: none -> 16.7 us  [exchange_line(): lax.all_to_all(x, ('dp', 'pos'), 0, 0, axis_index_groups=line_groups(), t...]
    pallas_call x4 -> x3, Pallas kernels: 30 us -> 15.5 us  [the longest x2 11.4 us: stage(): pl.pallas_call(functools.partial(stage_kernel, late, sizes), out_shape=[p...]
    ppermute x22 -> x21, waiting for transfers between devices: 39.9 us -> 27.9 us  [the longest x12 22.8 us: shift(): return lax.ppermute(x, 'dp', pairs)]
    ppermute x22 -> x21, starting transfers between devices: 27.4 us -> 18.9 us  [the longest x12 15.5 us: shift(): return lax.ppermute(x, 'dp', pairs)]
    all_to_all x0 -> x1, waiting for transfers between devices: none -> 7.54 us  [exchange_line(): lax.all_to_all(x, ('dp', 'pos'), 0, 0, axis_index_groups=line_groups(), t...]
    all_to_all x0 -> x1, starting transfers between devices: none -> 3.68 us  [exchange_line(): lax.all_to_all(x, ('dp', 'pos'), 0, 0, axis_index_groups=line_groups(), t...]
    unnamed x28 -> x25, local copies, waits for them, and re-layouts: 5.06 us -> 8.7 us
    convert_element_type x6 -> x5, other arithmetic: 2.98 us -> 0.84 us  [add(): return total.astype(jnp.bfloat16)]
  transfers between devices with their start and end apart: 22 -> 22, of which waited for: 13 -> 11; matrix products, arithmetic and copies ran while one was open for 5% -> 4% of each run, Pallas kernels for 27% -> 15%
where the time goes in v2:
time: 107 us; the launch traced here: 106 us
  waiting for transfers between devices  35.4 us (33%)
  starting transfers between devices  22.6 us (21%)
  blocking collectives  16.7 us (16%)
  Pallas kernels  15.5 us (14%)
  local copies, waits for them, and re-layouts  12 us (11%)
  other arithmetic  3.12 us (3%)
    ppermute x12, waiting for transfers between devices, shift(): return lax.ppermute(x, 'dp', pairs)  22.8 us
    all_to_all x1, blocking collectives, exchange_line(): lax.all_to_all(x, ('dp', 'pos'), 0, 0, axis_index_groups=line_groups(), t...  16.7 us
    ppermute x12, starting transfers between devices, shift(): return lax.ppermute(x, 'dp', pairs)  15.5 us
    pallas_call x2, Pallas kernels, stage(): pl.pallas_call(functools.partial(stage_kernel, late, sizes), out_shape=[p...  11.4 us
    unnamed x25, local copies, waits for them, and re-layouts  8.7 us
    all_to_all x1, waiting for transfers between devices, exchange_line(): lax.all_to_all(x, ('dp', 'pos'), 0, 0, axis_index_groups=line_groups(), t...  7.54 us
    ppermute x9, waiting for transfers between devices, swap_cores(): return lax.ppermute(x, 'dp', [(i, i ^ 1) for i in range(2 * SIDE * SIDE)])  5.09 us
    pallas_call x1, Pallas kernels, plan(): pl.pallas_call(plan_kernel, out_shape=jax.ShapeDtypeStruct((2 * PART,), j...  4.06 us
  transfers between devices with their start and end apart: 22, of which 11 were waited for; matrix products, arithmetic and copies ran while one was open for 4% of the time, Pallas kernels for 15%

profile of v2, /device:TPU:0, one launch (start us, length us, event | category | flops | bytes accessed | tf_op | source)
XLA Modules:
  0.0 106.2 jit_solution(6008347189376204639)
XLA Ops:
  1.5 16.7 %all_to_all.10 = bf16[8,128,256]{2,1,0:T(8,128)(2,1)S(1)} all-to-all(bf16[8,128,256]{2,1,0:T(8,128)(2,1)S(1)} %broadcast_in_dim.9), channel_id=1, replica_groups={{0,1,8,9,16,17,24,25},{32,33,40,41,48,49,56,57},{64,65,72,73,80,81,88,8..., dimensions={0} | all-to-all | bytes 1048576 | tf_op jit(solution)/shard_map/all_to_all | solution.py:33
  19.0 2.7 %collective-permute-start.2 = (bf16[2,256,256]{2,1,0:T(8,128)(2,1)}, bf16[2,256,256]{2,1,0:T(8,128)(2,1)S(1)}, u32[]{:S(2)}, u32[]{:S(2)}) collective-permute-start(bf16[2,256,256]{2,1,0:T(8,128)(2,1)} %bitcast.9), channel_id=1, source_target_pairs={{0,96},{4,28},{8,104},{12,4},{16,112},{20,12},{24,120},{28,20},{32... | collective-permute-start | bytes 786440 | tf_op jit(solution)/shard_map/ppermute | solution.py:42
  22.5 2.5 %collective-permute-start.7 = (bf16[2,256,256]{2,1,0:T(8,128)(2,1)}, bf16[2,256,256]{2,1,0:T(8,128)(2,1)S(1)}, u32[]{:S(2)}, u32[]{:S(2)}) collective-permute-start(bf16[2,256,256]{2,1,0:T(8,128)(2,1)} %bitcast.8), channel_id=1, source_target_pairs={{0,96},{4,28},{8,104},{12,4},{16,112},{20,12},{24,120},{28,20},{32... | collective-permute-start | bytes 786440 | tf_op jit(solution)/shard_map/ppermute | solution.py:42
  26.5 3.1 %collective-permute-done.refs_1_ = bf16[2,256,256]{2,1,0:T(8,128)(2,1)} collective-permute-done((bf16[2,256,256]{2,1,0:T(8,128)(2,1)}, bf16[2,256,256]{2,1,0:T(8,128)(2,1)}, u32[]{:S(2)}, u32[]{:S(2)}) %collective-permute-start) | collective-permute-done | bytes 262176 | tf_op jit(solution)/shard_map/ppermute | solution.py:42
  29.6 2.7 %collective-permute-done.6.refs_2_ = bf16[2,256,256]{2,1,0:T(8,128)(2,1)S(1)} collective-permute-done((bf16[2,256,256]{2,1,0:T(8,128)(2,1)}, bf16[2,256,256]{2,1,0:T(8,128)(2,1)S(1)}, u32[]{:S(2)}, u32[]{:S(2)}) %collective-permute-start.6) | collective-permute-done | bytes 262176 | tf_op jit(solution)/shard_map/ppermute | solution.py:42
  35.0 4.1 %plan.1.sched = s32[256]{0:T(256)} custom-call(s32[3]{0:T(128)} %pad_add_fusion.spot, s32[24]{0:T(128)} %fusion.1.target), custom_call_target="tpu_custom_call" | custom-call | tf_op jit(solution)/shard_map/plan/pallas_call | solution.py:125
  39.2 3.2 %collective-permute-start.3 = (bf16[2,256,256]{2,1,0:T(8,128)(2,1)S(1)}, bf16[2,256,256]{2,1,0:T(8,128)(2,1)S(1)}, u32[]{:S(2)}, u32[]{:S(2)}) collective-permute-start(bf16[2,256,256]{2,1,0:T(8,128)(2,1)S(1)} %collective-permute-done.2.refs_4_), channel_id=1, source_target_pairs={{0,96},{4,28},{8,104},{12,4},{16,112},{20,12},{24,120},{28,20},{32... | collective-permute-start | bytes 786440 | tf_op jit(solution)/shard_map/ppermute | solution.py:42
  43.2 1.4 %copy-done.2 = bf16[24,64,512]{2,1,0:T(8,128)(2,1)S(1)} copy-done((bf16[24,64,512]{2,1,0:T(8,128)(2,1)S(1)}, bf16[24,64,512]{2,1,0:T(8,128)(2,1)}, u32[]{:S(2)}) %copy-start.2) | copy-done | bytes 1572888
  49.3 9.3 %early_stage.1 = (bf16[24,64,512]{2,1,0:T(8,128)(2,1)S(1)}, bf16[12,256,256]{2,1,0:T(8,128)(2,1)S(1)}, bf16[12,256,256]{2,1,0:T(8,128)(2,1)S(1)}) custom-call(s32[256]{0:T(256)S(1)} %copy-done.11, bf16[24,64,512]{2,1,0:T(8,128)(2,1)S(1)} %copy-done.1, bf16[24,64,512]{2,1,0:T(8,128)(2,1)S(1)} %copy-done.2, f32[24,2,256]{2,1,0:T(2,128)S(1)} %pad_maximum_fusion.2.stats, ...), custom_call_target="tpu_custom_call" | custom-call | flops 1509949440 | tf_op jit(solution)/shard_map/early_stage/pallas_call | solution.py:252
  59.3 3.2 %collective-permute-done.4.refs_2_ = bf16[2,256,256]{2,1,0:T(8,128)(2,1)S(1)} collective-permute-done((bf16[2,256,256]{2,1,0:T(8,128)(2,1)S(1)}, bf16[2,256,256]{2,1,0:T(8,128)(2,1)S(1)}, u32[]{:S(2)}, u32[]{:S(2)}) %collective-permute-start.4) | collective-permute-done | bytes 262176 | tf_op jit(solution)/shard_map/ppermute | solution.py:46
  62.9 2.1 %late_stage.1 = (bf16[24,64,512]{2,1,0:T(8,128)(2,1)S(1)}, bf16[4,256,256]{2,1,0:T(8,128)(2,1)S(1)}, bf16[4,256,256]{2,1,0:T(8,128)(2,1)S(1)}) custom-call(s32[256]{0:T(256)S(1)} %copy-done.11, bf16[24,64,512]{2,1,0:T(8,128)(2,1)S(1)} %copy-done.1, bf16[24,64,512]{2,1,0:T(8,128)(2,1)S(1)} %copy-done.2, ...), custom_call_target="tpu_custom_call", output_to_operand_aliasing={{0}: (8, {})} | custom-call | flops 503316480 | tf_op jit(solution)/shard_map/late_stage/pallas_call | solution.py:252
  65.0 1.7 %collective-permute-start.14 = (bf16[4,256,256]{2,1,0:T(8,128)(2,1)S(1)}, bf16[4,256,256]{2,1,0:T(8,128)(2,1)S(1)}, u32[]{:S(2)}, u32[]{:S(2)}) collective-permute-start(bf16[4,256,256]{2,1,0:T(8,128)(2,1)S(1)} %get-tuple-element.14), channel_id=1, source_target_pairs={{0,4},{4,0},{8,12},{12,8},{16,20},{20,16},{24,28},{28,24},{32,36},... | collective-permute-start | bytes 1572872 | tf_op jit(solution)/shard_map/ppermute | solution.py:46
  66.6 1.5 %collective-permute-done.14 = bf16[4,256,256]{2,1,0:T(8,128)(2,1)S(1)} collective-permute-done((bf16[4,256,256]{2,1,0:T(8,128)(2,1)S(1)}, bf16[4,256,256]{2,1,0:T(8,128)(2,1)S(1)}, u32[]{:S(2)}, u32[]{:S(2)}) %collective-permute-start.14) | collective-permute-done | bytes 524320 | tf_op jit(solution)/shard_map/ppermute | solution.py:46
  68.6 1.8 %collective-permute-start.19 = (bf16[2,256,256]{2,1,0:T(8,128)(2,1)S(1)}, bf16[2,256,256]{2,1,0:T(8,128)(2,1)S(1)}, u32[]{:S(2)}, u32[]{:S(2)}) collective-permute-start(bf16[2,256,256]{2,1,0:T(8,128)(2,1)S(1)} %get-tuple-element.21), channel_id=1, source_target_pairs={{0,32},{4,12},{8,40},{12,20},{16,48},{20,28},{24,56},{28,4},{32,64... | collective-permute-start | bytes 786440 | tf_op jit(solution)/shard_map/ppermute | solution.py:42
  70.4 4.3 %collective-permute-done.15 = bf16[2,256,256]{2,1,0:T(8,128)(2,1)S(1)} collective-permute-done((bf16[2,256,256]{2,1,0:T(8,128)(2,1)S(1)}, bf16[2,256,256]{2,1,0:T(8,128)(2,1)S(1)}, u32[]{:S(2)}, u32[]{:S(2)}) %collective-permute-start.15) | collective-permute-done | bytes 262176 | tf_op jit(solution)/shard_map/ppermute | solution.py:42
  74.9 1.5 %collective-permute-start.16 = (bf16[2,256,256]{2,1,0:T(8,128)(2,1)S(1)}, bf16[2,256,256]{2,1,0:T(8,128)(2,1)S(1)}, u32[]{:S(2)}, u32[]{:S(2)}) collective-permute-start(bf16[2,256,256]{2,1,0:T(8,128)(2,1)S(1)} %get-tuple-element.18), channel_id=1, source_target_pairs={{0,96},{4,28},{8,104},{12,4},{16,112},{20,12},{24,120},{28,20},{32... | collective-permute-start | bytes 786440 | tf_op jit(solution)/shard_map/ppermute | solution.py:42
  77.0 4.3 %collective-permute-done.16 = bf16[2,256,256]{2,1,0:T(8,128)(2,1)S(1)} collective-permute-done((bf16[2,256,256]{2,1,0:T(8,128)(2,1)S(1)}, bf16[2,256,256]{2,1,0:T(8,128)(2,1)S(1)}, u32[]{:S(2)}, u32[]{:S(2)}) %collective-permute-start.16) | collective-permute-done | bytes 262176 | tf_op jit(solution)/shard_map/ppermute | solution.py:42
  81.4 2.7 %collective-permute-done.17 = bf16[2,256,256]{2,1,0:T(8,128)(2,1)S(1)} collective-permute-done((bf16[2,256,256]{2,1,0:T(8,128)(2,1)S(1)}, bf16[2,256,256]{2,1,0:T(8,128)(2,1)S(1)}, u32[]{:S(2)}, u32[]{:S(2)}) %collective-permute-start.17) | collective-permute-done | bytes 262176 | tf_op jit(solution)/shard_map/ppermute | solution.py:42
  84.5 2.0 %collective-permute-start.20 = (bf16[2,256,256]{2,1,0:T(8,128)(2,1)S(1)}, bf16[2,256,256]{2,1,0:T(8,128)(2,1)S(1)}, u32[]{:S(2)}, u32[]{:S(2)}) collective-permute-start(bf16[2,256,256]{2,1,0:T(8,128)(2,1)S(1)} %get-tuple-element.16), channel_id=1, source_target_pairs={{0,32},{4,12},{8,40},{12,20},{16,48},{20,28},{24,56},{28,4},{32,64... | collective-permute-start | bytes 786440 | tf_op jit(solution)/shard_map/ppermute | solution.py:42
  86.5 4.3 %collective-permute-done.18 = bf16[2,256,256]{2,1,0:T(8,128)(2,1)S(1)} collective-permute-done((bf16[2,256,256]{2,1,0:T(8,128)(2,1)S(1)}, bf16[2,256,256]{2,1,0:T(8,128)(2,1)S(1)}, u32[]{:S(2)}, u32[]{:S(2)}) %collective-permute-start.18) | collective-permute-done | bytes 262176 | tf_op jit(solution)/shard_map/ppermute | solution.py:42
  90.8 1.3 %collective-permute-done.20 = bf16[2,256,256]{2,1,0:T(8,128)(2,1)S(1)} collective-permute-done((bf16[2,256,256]{2,1,0:T(8,128)(2,1)S(1)}, bf16[2,256,256]{2,1,0:T(8,128)(2,1)S(1)}, u32[]{:S(2)}, u32[]{:S(2)}) %collective-permute-start.20) | collective-permute-done | bytes 262176 | tf_op jit(solution)/shard_map/ppermute | solution.py:42
  93.1 3.7 %all-to-all-start.1 = ((bf16[8,128,256]{2,1,0:T(8,128)(2,1)}), bf16[8,128,256]{2,1,0:T(8,128)(2,1)S(1)}, u32[]{:S(2)}, u32[]{:S(2)}) async-start(bf16[8,128,256]{2,1,0:T(8,128)(2,1)} %bitcast.11), calls=%async_computation.1 | async-start | bytes 1048576 | tf_op jit(solution)/shard_map/all_to_all | solution.py:33
  96.8 1.1 %copy.12 = bf16[24,64,512]{2,1,0:T(8,128)(2,1)} copy(bf16[24,64,512]{2,1,0:T(8,128)(2,1)S(1)} %get-tuple-element.28) | data formatting | bytes 3145728
  97.9 7.5 %all-to-all-done.1 = bf16[8,128,256]{2,1,0:T(8,128)(2,1)S(1)} async-done(((bf16[8,128,256]{2,1,0:T(8,128)(2,1)}), bf16[8,128,256]{2,1,0:T(8,128)(2,1)S(1)}, u32[]{:S(2)}, u32[]{:S(2)}) %all-to-all-start.1) | async-done | bytes 524320 | tf_op jit(solution)/shard_map/all_to_all | solution.py:33
  (65 shorter events, 16.6 us)
Async XLA Ops:
  0.6 32.9 %copy-start = (s32[768,1]{0,1:T(1,128)S(1)}, s32[768,1]{0,1:T(1,128)}, u32[]{:S(2)}) copy-start(s32[768,1]{0,1:T(1,128)} %param.11) | copy-start | bytes 9220
  1.4 41.8 %copy-start.1 = (bf16[24,64,512]{2,1,0:T(8,128)(2,1)S(1)}, bf16[24,64,512]{2,1,0:T(8,128)(2,1)}, u32[]{:S(2)}) copy-start(bf16[24,64,512]{2,1,0:T(8,128)(2,1)} %queries.3) | copy-start | bytes 4718596
  19.0 6.9 %collective-permute-start.2 = (bf16[2,256,256]{2,1,0:T(8,128)(2,1)}, bf16[2,256,256]{2,1,0:T(8,128)(2,1)S(1)}, u32[]{:S(2)}, u32[]{:S(2)}) collective-permute-start(bf16[2,256,256]{2,1,0:T(8,128)(2,1)} %bitcast.9), channel_id=1, source_target_pairs={{0,96},{4,28},{8,104},{12,4},{16,112},{20,12},{24,120},{28,20},{32... | collective-permute-start | bytes 786440 | tf_op jit(solution)/shard_map/ppermute | solution.py:42
  21.7 7.9 %collective-permute-start = (bf16[2,256,256]{2,1,0:T(8,128)(2,1)}, bf16[2,256,256]{2,1,0:T(8,128)(2,1)}, u32[]{:S(2)}, u32[]{:S(2)}) collective-permute-start(bf16[2,256,256]{2,1,0:T(8,128)(2,1)} %bitcast.8), channel_id=1, source_target_pairs={{0,32},{4,12},{8,40},{12,20},{16,48},{20,28},{24,56},{28,4},{32,64... | collective-permute-start | bytes 786440 | tf_op jit(solution)/shard_map/ppermute | solution.py:42
  21.7 10.6 %collective-permute-start.6 = (bf16[2,256,256]{2,1,0:T(8,128)(2,1)}, bf16[2,256,256]{2,1,0:T(8,128)(2,1)S(1)}, u32[]{:S(2)}, u32[]{:S(2)}) collective-permute-start(bf16[2,256,256]{2,1,0:T(8,128)(2,1)} %bitcast.9), channel_id=1, source_target_pairs={{0,32},{4,12},{8,40},{12,20},{16,48},{20,28},{24,56},{28,4},{32,64... | collective-permute-start | bytes 786440 | tf_op jit(solution)/shard_map/ppermute | solution.py:42
  22.5 9.8 %collective-permute-start.7 = (bf16[2,256,256]{2,1,0:T(8,128)(2,1)}, bf16[2,256,256]{2,1,0:T(8,128)(2,1)S(1)}, u32[]{:S(2)}, u32[]{:S(2)}) collective-permute-start(bf16[2,256,256]{2,1,0:T(8,128)(2,1)} %bitcast.8), channel_id=1, source_target_pairs={{0,96},{4,28},{8,104},{12,4},{16,112},{20,12},{24,120},{28,20},{32... | collective-permute-start | bytes 786440 | tf_op jit(solution)/shard_map/ppermute | solution.py:42
  25.0 17.5 %collective-permute-start.8 = (bf16[4,256,256]{2,1,0:T(8,128)(2,1)S(1)}, bf16[4,256,256]{2,1,0:T(8,128)(2,1)S(1)}, u32[]{:S(2)}, u32[]{:S(2)}) collective-permute-start(bf16[4,256,256]{2,1,0:T(8,128)(2,1)S(1)} %bitcast.21), channel_id=1, source_target_pairs={{0,4},{4,0},{8,12},{12,8},{16,20},{20,16},{24,28},{28,24},{32,36},... | collective-permute-start | bytes 1572872 | tf_op jit(solution)/shard_map/ppermute | solution.py:46
  25.9 13.2 %collective-permute-start.12 = (bf16[2,256,256]{2,1,0:T(8,128)(2,1)S(1)}, bf16[2,256,256]{2,1,0:T(8,128)(2,1)}, u32[]{:S(2)}, u32[]{:S(2)}) collective-permute-start(bf16[2,256,256]{2,1,0:T(8,128)(2,1)S(1)} %collective-permute-done.2.refs_4_), channel_id=1, source_target_pairs={{0,4},{4,0},{8,12},{12,8},{16,20},{20,16},{24,28},{28,24},{32,36},... | collective-permute-start | bytes 786440 | tf_op jit(solution)/shard_map/ppermute | solution.py:46
  29.6 9.6 %collective-permute-start.9 = (bf16[2,256,256]{2,1,0:T(8,128)(2,1)}, bf16[2,256,256]{2,1,0:T(8,128)(2,1)}, u32[]{:S(2)}, u32[]{:S(2)}) collective-permute-start(bf16[2,256,256]{2,1,0:T(8,128)(2,1)} %collective-permute-done.refs_1_), channel_id=1, source_target_pairs={{0,4},{4,0},{8,12},{12,8},{16,20},{20,16},{24,28},{28,24},{32,36},... | collective-permute-start | bytes 786440 | tf_op jit(solution)/shard_map/ppermute | solution.py:46
  32.3 10.1 %collective-permute-start.10 = (bf16[2,256,256]{2,1,0:T(8,128)(2,1)S(1)}, bf16[2,256,256]{2,1,0:T(8,128)(2,1)}, u32[]{:S(2)}, u32[]{:S(2)}) collective-permute-start(bf16[2,256,256]{2,1,0:T(8,128)(2,1)S(1)} %collective-permute-done.6.refs_2_), channel_id=1, source_target_pairs={{0,4},{4,0},{8,12},{12,8},{16,20},{20,16},{24,28},{28,24},{32,36},... | collective-permute-start | bytes 786440 | tf_op jit(solution)/shard_map/ppermute | solution.py:46
  32.3 10.1 %collective-permute-start.11 = (bf16[2,256,256]{2,1,0:T(8,128)(2,1)S(1)}, bf16[2,256,256]{2,1,0:T(8,128)(2,1)}, u32[]{:S(2)}, u32[]{:S(2)}) collective-permute-start(bf16[2,256,256]{2,1,0:T(8,128)(2,1)S(1)} %collective-permute-done.7.refs_3_), channel_id=1, source_target_pairs={{0,4},{4,0},{8,12},{12,8},{16,20},{20,16},{24,28},{28,24},{32,36},... | collective-permute-start | bytes 786440 | tf_op jit(solution)/shard_map/ppermute | solution.py:46
  39.1 19.6 %collective-permute-start.1 = (bf16[2,256,256]{2,1,0:T(8,128)(2,1)}, bf16[2,256,256]{2,1,0:T(8,128)(2,1)S(1)}, u32[]{:S(2)}, u32[]{:S(2)}) collective-permute-start(bf16[2,256,256]{2,1,0:T(8,128)(2,1)} %collective-permute-done.refs_1_), channel_id=1, source_target_pairs={{0,32},{4,12},{8,40},{12,20},{16,48},{20,28},{24,56},{28,4},{32,64... | collective-permute-start | bytes 786440 | tf_op jit(solution)/shard_map/ppermute | solution.py:42
  39.2 20.0 %collective-permute-start.3 = (bf16[2,256,256]{2,1,0:T(8,128)(2,1)S(1)}, bf16[2,256,256]{2,1,0:T(8,128)(2,1)S(1)}, u32[]{:S(2)}, u32[]{:S(2)}) collective-permute-start(bf16[2,256,256]{2,1,0:T(8,128)(2,1)S(1)} %collective-permute-done.2.refs_4_), channel_id=1, source_target_pairs={{0,96},{4,28},{8,104},{12,4},{16,112},{20,12},{24,120},{28,20},{32... | collective-permute-start | bytes 786440 | tf_op jit(solution)/shard_map/ppermute | solution.py:42
  58.6 16.1 %collective-permute-start.13 = (bf16[12,256,256]{2,1,0:T(8,128)(2,1)S(1)}, bf16[12,256,256]{2,1,0:T(8,128)(2,1)S(1)}, u32[]{:S(2)}, u32[]{:S(2)}) collective-permute-start(bf16[12,256,256]{2,1,0:T(8,128)(2,1)S(1)} %get-tuple-element.12), channel_id=1, source_target_pairs={{0,4},{4,0},{8,12},{12,8},{16,20},{20,16},{24,28},{28,24},{32,36},... | collective-permute-start | bytes 4718600 | tf_op jit(solution)/shard_map/ppermute | solution.py:46
  58.7 3.8 %collective-permute-start.4 = (bf16[2,256,256]{2,1,0:T(8,128)(2,1)S(1)}, bf16[2,256,256]{2,1,0:T(8,128)(2,1)S(1)}, u32[]{:S(2)}, u32[]{:S(2)}) collective-permute-start(bf16[2,256,256]{2,1,0:T(8,128)(2,1)S(1)} %collective-permute-done.1.refs_0_), channel_id=1, source_target_pairs={{0,4},{4,0},{8,12},{12,8},{16,20},{20,16},{24,28},{28,24},{32,36},... | collective-permute-start | bytes 786440 | tf_op jit(solution)/shard_map/ppermute | solution.py:46
  59.2 3.6 %collective-permute-start.5 = (bf16[2,256,256]{2,1,0:T(8,128)(2,1)S(1)}, bf16[2,256,256]{2,1,0:T(8,128)(2,1)S(1)}, u32[]{:S(2)}, u32[]{:S(2)}) collective-permute-start(bf16[2,256,256]{2,1,0:T(8,128)(2,1)S(1)} %collective-permute-done.3.refs_1_), channel_id=1, source_target_pairs={{0,4},{4,0},{8,12},{12,8},{16,20},{20,16},{24,28},{28,24},{32,36},... | collective-permute-start | bytes 786440 | tf_op jit(solution)/shard_map/ppermute | solution.py:46
  65.0 3.2 %collective-permute-start.14 = (bf16[4,256,256]{2,1,0:T(8,128)(2,1)S(1)}, bf16[4,256,256]{2,1,0:T(8,128)(2,1)S(1)}, u32[]{:S(2)}, u32[]{:S(2)}) collective-permute-start(bf16[4,256,256]{2,1,0:T(8,128)(2,1)S(1)} %get-tuple-element.14), channel_id=1, source_target_pairs={{0,4},{4,0},{8,12},{12,8},{16,20},{20,16},{24,28},{28,24},{32,36},... | collective-permute-start | bytes 1572872 | tf_op jit(solution)/shard_map/ppermute | solution.py:46
  68.3 6.4 %collective-permute-start.15 = (bf16[2,256,256]{2,1,0:T(8,128)(2,1)S(1)}, bf16[2,256,256]{2,1,0:T(8,128)(2,1)S(1)}, u32[]{:S(2)}, u32[]{:S(2)}) collective-permute-start(bf16[2,256,256]{2,1,0:T(8,128)(2,1)S(1)} %get-tuple-element.20), channel_id=1, source_target_pairs={{0,96},{4,28},{8,104},{12,4},{16,112},{20,12},{24,120},{28,20},{32... | collective-permute-start | bytes 786440 | tf_op jit(solution)/shard_map/ppermute | solution.py:42
  68.6 8.4 %collective-permute-start.19 = (bf16[2,256,256]{2,1,0:T(8,128)(2,1)S(1)}, bf16[2,256,256]{2,1,0:T(8,128)(2,1)S(1)}, u32[]{:S(2)}, u32[]{:S(2)}) collective-permute-start(bf16[2,256,256]{2,1,0:T(8,128)(2,1)S(1)} %get-tuple-element.21), channel_id=1, source_target_pairs={{0,32},{4,12},{8,40},{12,20},{16,48},{20,28},{24,56},{28,4},{32,64... | collective-permute-start | bytes 786440 | tf_op jit(solution)/shard_map/ppermute | solution.py:42
  74.9 6.4 %collective-permute-start.16 = (bf16[2,256,256]{2,1,0:T(8,128)(2,1)S(1)}, bf16[2,256,256]{2,1,0:T(8,128)(2,1)S(1)}, u32[]{:S(2)}, u32[]{:S(2)}) collective-permute-start(bf16[2,256,256]{2,1,0:T(8,128)(2,1)S(1)} %get-tuple-element.18), channel_id=1, source_target_pairs={{0,96},{4,28},{8,104},{12,4},{16,112},{20,12},{24,120},{28,20},{32... | collective-permute-start | bytes 786440 | tf_op jit(solution)/shard_map/ppermute | solution.py:42
  76.5 7.6 %collective-permute-start.17 = (bf16[2,256,256]{2,1,0:T(8,128)(2,1)S(1)}, bf16[2,256,256]{2,1,0:T(8,128)(2,1)S(1)}, u32[]{:S(2)}, u32[]{:S(2)}) collective-permute-start(bf16[2,256,256]{2,1,0:T(8,128)(2,1)S(1)} %get-tuple-element.19), channel_id=1, source_target_pairs={{0,32},{4,12},{8,40},{12,20},{16,48},{20,28},{24,56},{28,4},{32,64... | collective-permute-start | bytes 786440 | tf_op jit(solution)/shard_map/ppermute | solution.py:42
  84.4 6.4 %collective-permute-start.18 = (bf16[2,256,256]{2,1,0:T(8,128)(2,1)S(1)}, bf16[2,256,256]{2,1,0:T(8,128)(2,1)S(1)}, u32[]{:S(2)}, u32[]{:S(2)}) collective-permute-start(bf16[2,256,256]{2,1,0:T(8,128)(2,1)S(1)} %get-tuple-element.17), channel_id=1, source_target_pairs={{0,96},{4,28},{8,104},{12,4},{16,112},{20,12},{24,120},{28,20},{32... | collective-permute-start | bytes 786440 | tf_op jit(solution)/shard_map/ppermute | solution.py:42
  84.5 7.7 %collective-permute-start.20 = (bf16[2,256,256]{2,1,0:T(8,128)(2,1)S(1)}, bf16[2,256,256]{2,1,0:T(8,128)(2,1)S(1)}, u32[]{:S(2)}, u32[]{:S(2)}) collective-permute-start(bf16[2,256,256]{2,1,0:T(8,128)(2,1)S(1)} %get-tuple-element.16), channel_id=1, source_target_pairs={{0,32},{4,12},{8,40},{12,20},{16,48},{20,28},{24,56},{28,4},{32,64... | collective-permute-start | bytes 786440 | tf_op jit(solution)/shard_map/ppermute | solution.py:42
  93.1 12.4 %all-to-all-start.1 = ((bf16[8,128,256]{2,1,0:T(8,128)(2,1)}), bf16[8,128,256]{2,1,0:T(8,128)(2,1)S(1)}, u32[]{:S(2)}, u32[]{:S(2)}) async-start(bf16[8,128,256]{2,1,0:T(8,128)(2,1)} %bitcast.11), calls=%async_computation.1 | async-start | bytes 1048576 | tf_op jit(solution)/shard_map/all_to_all | solution.py:33
  (10 other events, 41.9 us)

commit v3 on v2

v3 whole, which is shorter than its diff:
```python
import functools
import math

import jax
import jax.numpy as jnp
from jax import lax
from jax.experimental import pallas as pl
from jax.experimental.pallas import tpu as pltpu
from jax.sharding import PartitionSpec as P

SIDE = 4
TILES = 24
STAGES = 3
BATCH = 4
LOG2E = math.log2(math.e)
PLACE, TILE, MODE, COUNT, PART = 0, 1, 2, 3, 8


def place(z, y, core):
    return (z % SIDE) * 2 * SIDE + (y % SIDE) * 2 + core


def line_groups():
    groups = []
    for core in range(2):
        for other in range(SIDE):
            ring = [place(other, k, 0) if core == 0 else place(k, other, 1) for k in range(SIDE)]
            groups.append([dp * 2 + pos for dp in ring for pos in range(2)])
    return groups


def exchange_line(x):
    return lax.all_to_all(x, ("dp", "pos"), 0, 0, axis_index_groups=line_groups(), tiled=True)


def shift(x, step):
    pairs = []
    for z in range(SIDE):
        for y in range(SIDE):
            pairs.append((place(z, y, 0), place(z + step, y, 0)))
            pairs.append((place(z, y, 1), place(z, y + step, 1)))
    return lax.ppermute(x, "dp", pairs)


def swap_cores(x):
    return lax.ppermute(x, "dp", [(i, i ^ 1) for i in range(2 * SIDE * SIDE)])


def held(x):
    return pltpu.with_memory_space_constraint(x, pltpu.VMEM)


def distant(x):
    return pltpu.with_memory_space_constraint(x, pltpu.HBM)


def spread_kernel(keys, values, out, both, sem):
    both[:, 0:128] = keys[0]
    both[:, 128:256] = values[0]
    copies = [
        pltpu.make_async_copy(both, out.at[k], sem.at[k]) for k in range(out.shape[0])]
    for copy in copies:
        copy.start()
    for copy in copies:
        copy.wait()


def spread(keys, values):
    whole = pl.BlockSpec(memory_space=pltpu.VMEM)
    return pl.pallas_call(
        spread_kernel,
        out_shape=jax.ShapeDtypeStruct((2 * SIDE, keys.shape[1], 256), keys.dtype),
        in_specs=[whole, whole],
        out_specs=pl.BlockSpec(memory_space=pl.ANY),
        scratch_shapes=[
            pltpu.VMEM((keys.shape[1], 256), keys.dtype),
            pltpu.SemaphoreType.DMA((2 * SIDE,)),
        ],
        name="spread",
    )(keys, values)


def plan_kernel(code_ref, out):
    shape = (TILES, 128)
    lane = lax.broadcasted_iota(jnp.int32, shape, 1)
    row = lax.broadcasted_iota(jnp.int32, shape, 0)
    code = jnp.broadcast_to(code_ref[...], shape)
    mine = jnp.sum(jnp.where(lane == row, code, 0), axis=1, keepdims=True)
    code = jnp.where(lane < TILES, code, -1)
    twin = (code >> 10 == mine >> 10) & (lane != row)
    dup = jnp.sum(twin.astype(jnp.int32), axis=1, keepdims=True)
    stage = mine >> 8 & 3
    at = mine & 255
    key = stage * 4096 + (1 - dup) * 2048 + at * 32 + row[:, 0:1]
    keys = jnp.sum(jnp.where(lane == row, key, 0), axis=0, keepdims=True)
    ahead = (keys < key) & (keys >> 12 == stage) & (lane < TILES)
    rank = jnp.sum(ahead.astype(jnp.int32), axis=1, keepdims=True)
    for turn in range(STAGES):
        here = stage == turn
        n = jnp.sum(jnp.where(here & (lane == 0), 1, 0))
        last = jnp.maximum((n + 1) // 2 - 1, 0)
        pair = jnp.minimum(lane // 2, last)
        source = jnp.maximum(jnp.minimum(2 * pair + lane % 2, n - 1), 0)
        picked = here & (rank == source)
        first = PART * turn

        def put(line, value, chosen):
            out[first + line:first + line + 1, :] = jnp.sum(
                jnp.where(chosen, value, 0), axis=0, keepdims=True)

        put(PLACE, at, picked)
        put(TILE, row, picked)
        put(MODE, dup, picked)
        out[first + COUNT:first + COUNT + 1, :] = jnp.full((1, 128), (n + BATCH - 1) // BATCH)


def plan(code):
    whole = pl.BlockSpec(memory_space=pltpu.VMEM)
    return pl.pallas_call(
        plan_kernel,
        out_shape=pltpu.VMEM((STAGES * PART, 128), jnp.int32),
        in_specs=[whole],
        out_specs=whole,
        name="plan",
    )(code)


def tile_grads(query, grad, keys, values, stat, scaling):
    nt = (((1,), (1,)), ((), ()))
    tn = (((0,), (0,)), ((), ()))
    f32, half = jnp.float32, jnp.bfloat16
    tiles = range(len(query))
    scores = [
        lax.dot_general(keys[k], query[k], nt, preferred_element_type=f32) * (scaling * LOG2E)
        for k in tiles
    ]
    prob_grad = [
        lax.dot_general(values[k], grad[k], nt, preferred_element_type=f32) for k in tiles
    ]
    prob_half, score_grad = [], []
    for k in tiles:
        suffix_l = stat[k][0:1] * LOG2E
        suffix_d = stat[k][1:2]
        top = jnp.maximum(jnp.max(scores[k], axis=0, keepdims=True), suffix_l)
        raised = jnp.exp2(scores[k] - top)
        suffix_part = jnp.exp2(suffix_l - top)
        inverse = 1.0 / (jnp.sum(raised, axis=0, keepdims=True) + suffix_part)
        moment = jnp.sum(raised * prob_grad[k], axis=0, keepdims=True) + suffix_part * suffix_d
        probs = raised * inverse
        prob_half.append(probs.astype(half))
        score_grad.append((probs * (prob_grad[k] - moment * inverse)).astype(half))
    parts = []
    for k in tiles:
        query_part = lax.dot_general(keys[k], score_grad[k], tn, preferred_element_type=f32)
        parts.append((
            (query_part * scaling).astype(half).T,
            jnp.dot(score_grad[k], query[k], preferred_element_type=f32) * scaling,
            jnp.dot(prob_half[k], grad[k], preferred_element_type=f32),
        ))
    return parts


def stage_kernel(turn, sizes, sched, *refs):
    if turn == 0:
        queries, grads, stats, *blocks = refs[:3 + len(sizes)]
        query_grad, sums, there, tile_rows, near, arrived = refs[3 + len(sizes):]
    else:
        tile_rows, stats, *blocks = refs[:2 + len(sizes)]
        query_grad, sums, there, *result, near, arrived = refs[3 + len(sizes):]
    _, _, rows, width = tile_rows.shape
    heads = width // 128
    scaling = 128 ** -0.5
    base = turn * PART
    places = sums.shape[0]
    count = sched[base + COUNT, 0]
    loads, first = [], 0
    for block, size in zip(blocks, sizes):
        loads.append(pltpu.make_async_copy(
            block, near.at[first:first + size], arrived.at[len(loads)]))
        first += size
    if turn == 0:
        for which, source in enumerate((queries, grads)):
            loads.append(pltpu.make_async_copy(
                source, tile_rows.at[which], arrived.at[len(loads)]))
    for load in loads:
        load.start()
    sums[...] = jnp.zeros(sums.shape, sums.dtype)
    for load in loads:
        load.wait()

    def stacked(which, tile):
        return jnp.concatenate(
            [tile_rows[which, tile, :, h * 128:(h + 1) * 128] for h in range(heads)], axis=0)

    def step(batch, _):
        at = [sched[base + PLACE, batch * BATCH + k] for k in range(BATCH)]
        tile = [sched[base + TILE, batch * BATCH + k] for k in range(BATCH)]
        twins = [sched[base + MODE, batch * BATCH + 2 * pair] for pair in range(BATCH // 2)]
        parts = tile_grads(
            [stacked(0, t) for t in tile], [stacked(1, t) for t in tile],
            [near[k, :, 0:128] for k in at], [near[k, :, 128:256] for k in at],
            [stats[t] for t in tile], scaling)
        for k in range(BATCH):
            for h in range(heads):
                query_grad[tile[k], :, h * 128:(h + 1) * 128] = parts[k][0][h * rows:(h + 1) * rows]
        for pair in range(BATCH // 2):
            a, b = 2 * pair, 2 * pair + 1
            other = jnp.where(twins[pair] == 1, 1.0, 0.0)
            for one, two in ((a, b), (b, a)):
                for part in (1, 2):
                    sums[at[one], :, part * 128 - 128:part * 128] = (
                        parts[one][part] + other * parts[two][part]).astype(sums.dtype)
        return 0

    lax.fori_loop(0, count, step, 0)
    handed = pltpu.make_async_copy(sums.at[places // 2:places], there, arrived.at[0])
    handed.start()
    if turn == STAGES - 1:
        final = pltpu.make_async_copy(query_grad, result[0], arrived.at[1])
        final.start()
        final.wait()
    handed.wait()


def stage(turn, sched, tile_rows, stats, blocks, query_grad):
    sizes = tuple(block.shape[0] for block in blocks)
    places = sum(sizes)
    kind = blocks[0].dtype
    block_shape = blocks[0].shape[1:]
    whole = pl.BlockSpec(memory_space=pltpu.VMEM)
    away = pl.BlockSpec(memory_space=pl.ANY)
    first, last = turn == 0, turn == STAGES - 1
    shape = tile_rows[0].shape
    rows = [distant(x) for x in tile_rows] if first else [held(tile_rows)]
    operands = [sched, *rows, held(stats), *blocks] + ([] if first else [held(query_grad)])
    return pl.pallas_call(
        functools.partial(stage_kernel, turn, sizes),
        out_shape=[
            pltpu.VMEM(shape, kind),
            pltpu.VMEM((places, *block_shape), kind),
            jax.ShapeDtypeStruct((places // 2, *block_shape), kind),
        ] + [pltpu.VMEM((2, *shape), kind)] * first + [jax.ShapeDtypeStruct(shape, kind)] * last,
        in_specs=[pl.BlockSpec(memory_space=pltpu.SMEM)] + ([pl.BlockSpec(memory_space=pltpu.HBM)] * 2 if first else [whole]) + [whole]
        + [away] * len(blocks) + [whole] * (not first),
        out_specs=[whole, whole, away] + [whole] * first + [away] * last,
        scratch_shapes=[
            pltpu.VMEM((places, *block_shape), kind),
            pltpu.SemaphoreType.DMA((len(blocks) + 2,)),
        ],
        input_output_aliases={} if first else {len(operands) - 1: 0},
        compiler_params=pltpu.CompilerParams(vmem_limit_bytes=8 << 20),
        cost_estimate=pl.CostEstimate(
            flops=6 * 10 * 256 * 256 * 128, bytes_accessed=0,
            transcendentals=6 * 65536),
        name=("line_stage", "next_stage", "far_stage")[turn],
    )(*operands)


def add(*parts):
    total = parts[0].astype(jnp.float32)
    for part in parts[1:]:
        total = total + part.astype(jnp.float32)
    return total.astype(jnp.bfloat16)


def shards(queries, output_gradient, prefix_keys, prefix_values, tile_prefix, suffix_lse, suffix_dot):
    tile_count, row_count, _ = queries.shape
    dp = lax.axis_index("dp")
    pos = lax.axis_index("pos")

    own = spread(prefix_keys, prefix_values)
    line = exchange_line(own).reshape(SIDE, 256, 256)
    target = lax.dynamic_slice(tile_prefix, (dp * tile_count, 0), (tile_count, 1)).reshape(1, -1)
    far_z, far_y, far_core = target >> 3, target >> 1 & 3, target & 1
    near = jnp.where(far_core == 0, far_y, far_z)
    far = jnp.where(far_core == 0, (dp >> 3) - far_z, (dp >> 1 & 3) - far_y) & 3
    side = far_core ^ (dp & 1)
    next_one = far & 1
    at = side * (SIDE + SIDE * next_one) + next_one * (far >> 1) * SIDE + near
    code = target * 1024 + jnp.where(far == 0, 0, 2 - next_one) * 256 + at
    code = jnp.pad(code, ((0, 0), (0, 128 - tile_count)))
    sched = plan(code)

    def own_rows(x):
        x = jnp.transpose(x, (0, 2, 1))
        x = lax.dynamic_slice(
            x, (dp * tile_count, 0, pos * row_count), (tile_count, x.shape[1], row_count))
        return x.reshape(tile_count, 1, -1)

    stats = jnp.concatenate([own_rows(suffix_lse), own_rows(suffix_dot)], axis=1)

    line, sched, stats = lax.optimization_barrier((line, sched, stats))
    up, down = shift(line, 1), shift(line, -1)
    here, back = [], []

    def work(turn, block, tile_rows, query_grad):
        query_grad, sums, there, *rest = stage(turn, sched, tile_rows, stats, block, query_grad)
        here.append(sums)
        back.append(swap_cores(there))
        return query_grad, *rest

    def both(*block):
        return [*block, *map(swap_cores, block)]

    query_grad, tile_rows = work(0, both(line), (queries, output_gradient), None)
    up, down, query_grad = lax.optimization_barrier((up, down, query_grad))
    far = shift(up[0:2], 1), shift(down[2:4], -1)
    query_grad, = work(1, both(up, down), tile_rows, query_grad)
    far, query_grad = lax.optimization_barrier((far, query_grad))
    _, query_grad = work(2, both(*far), tile_rows, query_grad)

    from_up = shift(add(here[1][0:4], back[1][0:4]), -1)
    from_down = shift(add(here[1][4:8], back[1][4:8]), 1)
    from_far = shift(add(here[2][0:4], back[2]), 2)
    line_sum = add(here[0][0:4], back[0], from_up, from_down, from_far)
    total = add(*exchange_line(line_sum.reshape(own.shape)))
    return query_grad, total[None, :, 0:128], total[None, :, 128:256]


def solution(mesh):
    in_specs = (
        P("dp", "pos", "head"),
        P("dp", "pos", "head"),
        P("dp", "pos", "head"),
        P("dp", "pos", "head"),
        P(),
        P(None, None, "head"),
        P(None, None, "head"),
    )
    out_specs = (P("dp", "pos", "head"), P("dp", "pos", "head"), P("dp", "pos", "head"))
    return jax.shard_map(shards, mesh=mesh, in_specs=in_specs, out_specs=out_specs, check_vma=False)
```

time: 107 us -> 78.8 us (0.74)
  the two profiles are of different devices: /device:TPU:0 before, /device:TPU:1 now
where the time goes in v3:
time: 78.8 us; the launch traced here: 77.8 us
  starting transfers between devices  21.6 us (27%)
  waiting for transfers between devices  21.4 us (27%)
  Pallas kernels  17 us (22%)
  blocking collectives  13.1 us (17%)
  local copies, waits for them, and re-layouts  2.32 us (3%)
  other arithmetic  1.66 us (2%)
    pallas_call x3, Pallas kernels, stage(): pl.pallas_call(functools.partial(stage_kernel, turn, sizes), out_shape=[p...  14.4 us
    ppermute x7, waiting for transfers between devices, shift(): return lax.ppermute(x, 'dp', pairs)  13.8 us
    all_to_all x1, blocking collectives, exchange_line(): lax.all_to_all(x, ('dp', 'pos'), 0, 0, axis_index_groups=line_groups(), t...  13.1 us
    ppermute x7, starting transfers between devices, shift(): return lax.ppermute(x, 'dp', pairs)  8.7 us
    all_to_all x1, starting transfers between devices, exchange_line(): lax.all_to_all(x, ('dp', 'pos'), 0, 0, axis_index_groups=line_groups(), t...  6.8 us
    ppermute x8, starting transfers between devices, swap_cores(): return lax.ppermute(x, 'dp', [(i, i ^ 1) for i in range(2 * SIDE * SIDE)])  6.12 us
    all_to_all x1, waiting for transfers between devices, exchange_line(): lax.all_to_all(x, ('dp', 'pos'), 0, 0, axis_index_groups=line_groups(), t...  5.16 us
    ppermute x8, waiting for transfers between devices, swap_cores(): return lax.ppermute(x, 'dp', [(i, i ^ 1) for i in range(2 * SIDE * SIDE)])  2.44 us
  transfers between devices with their start and end apart: 16, of which 7 were waited for; matrix products, arithmetic and copies ran while one was open for 4% of the time, Pallas kernels for 20%

profile of v3, /device:TPU:1, one launch (start us, length us, event | category | flops | bytes accessed | tf_op | source)
XLA Modules:
  0.0 77.8 jit_solution(1654675057992149113)
XLA Ops:
  0.6 1.6 %spread.1 = bf16[8,128,256]{2,1,0:T(8,128)(2,1)} custom-call(bf16[1,128,128]{2,1,0:T(8,128)(2,1)} %keys.1, bf16[1,128,128]{2,1,0:T(8,128)(2,1)} %values.1), custom_call_target="tpu_custom_call" | custom-call | tf_op jit(solution)/shard_map/spread/pallas_call | solution.py:70
  2.3 6.8 %all-to-all-start = ((bf16[8,128,256]{2,1,0:T(8,128)(2,1)}), bf16[8,128,256]{2,1,0:T(8,128)(2,1)S(1)}, u32[]{:S(2)}, u32[]{:S(2)}) async-start(bf16[8,128,256]{2,1,0:T(8,128)(2,1)} %spread.1), calls=%async_computation | async-start | bytes 1048576 | tf_op jit(solution)/shard_map/all_to_all | solution.py:33
  9.1 0.9 %dynamic-slice_bitcast_fusion = (f32[24,4,64]{2,1,0:T(4,128)S(1)}, f32[24,4,64]{2,1,0:T(4,128)S(1)}) fusion(f32[768,128,4]{1,2,0:T(4,128)} %param.13, s32[]{:T(128)S(6)} %select_n.44, s32[]{:T(128)S(6)} %select_n.48, f32[768,128,4]{1,2,0:T(4,128)} %param.12), kind=kLoop, calls=%fused_computation.7 | loop fusion | bytes 98312 | tf_op jit(solution)/shard_map/dynamic_slice | solution.py:286
  10.2 0.8 fusion.5
  11.0 0.5 pad.4.code_ref
  11.5 0.9 %plan.1.sched = s32[24,128]{1,0:T(8,128)S(1)} custom-call(s32[1,128]{1,0:T(1,128)} %pad.4.code_ref), custom_call_target="tpu_custom_call" | custom-call | tf_op jit(solution)/shard_map/plan/pallas_call | solution.py:119
  12.5 5.2 %all-to-all-done = bf16[8,128,256]{2,1,0:T(8,128)(2,1)S(1)} async-done(((bf16[8,128,256]{2,1,0:T(8,128)(2,1)}), bf16[8,128,256]{2,1,0:T(8,128)(2,1)S(1)}, u32[]{:S(2)}, u32[]{:S(2)}) %all-to-all-start) | async-done | bytes 524320 | tf_op jit(solution)/shard_map/all_to_all | solution.py:33
  17.7 2.8 %collective-permute-start = (bf16[4,256,256]{2,1,0:T(8,128)(2,1)S(1)}, bf16[4,256,256]{2,1,0:T(8,128)(2,1)S(1)}, u32[]{:S(2)}, u32[]{:S(2)}) collective-permute-start(bf16[4,256,256]{2,1,0:T(8,128)(2,1)S(1)} %bitcast.47), channel_id=1, source_target_pairs={{0,4},{4,0},{8,12},{12,8},{16,20},{20,16},{24,28},{28,24},{32,36},... | collective-permute-start | bytes 1572872 | tf_op jit(solution)/shard_map/ppermute | solution.py:46
  20.5 2.7 %collective-permute-start.2 = (bf16[4,256,256]{2,1,0:T(8,128)(2,1)S(1)}, bf16[4,256,256]{2,1,0:T(8,128)(2,1)S(1)}, u32[]{:S(2)}, u32[]{:S(2)}) collective-permute-start(bf16[4,256,256]{2,1,0:T(8,128)(2,1)S(1)} %bitcast.49), channel_id=1, source_target_pairs={{0,96},{4,28},{8,104},{12,4},{16,112},{20,12},{24,120},{28,20},{32... | collective-permute-start | bytes 1572872 | tf_op jit(solution)/shard_map/ppermute | solution.py:42
  23.1 5.2 %line_stage.1 = (bf16[24,64,512]{2,1,0:T(8,128)(2,1)S(1)}, bf16[8,256,256]{2,1,0:T(8,128)(2,1)S(1)}, bf16[4,256,256]{2,1,0:T(8,128)(2,1)S(1)}, bf16[2,24,64,512]{3,2,1,0:T(8,128)(2,1)S(1)}) custom-call(s32[24,128]{1,0:T(8,128)S(1)} %plan.1.sched, bf16[24,64,512]{2,1,0:T(8,128)(2,1)} %refs_0_.1, bf16[24,64,512]{2,1,0:T(8,128)(2,1)} %refs_1_.1, ...), custom_call_target="tpu_custom_call" | custom-call | flops 503316480 | tf_op jit(solution)/shard_map/line_stage/pallas_call | solution.py:236
  28.3 1.7 %collective-permute-done.1.refs_2_ = bf16[4,256,256]{2,1,0:T(8,128)(2,1)S(1)} collective-permute-done((bf16[4,256,256]{2,1,0:T(8,128)(2,1)S(1)}, bf16[4,256,256]{2,1,0:T(8,128)(2,1)S(1)}, u32[]{:S(2)}, u32[]{:S(2)}) %collective-permute-start.1) | collective-permute-done | bytes 524320 | tf_op jit(solution)/shard_map/ppermute | solution.py:42
  30.0 1.1 %collective-permute-start.5 = (bf16[4,256,256]{2,1,0:T(8,128)(2,1)S(1)}, bf16[4,256,256]{2,1,0:T(8,128)(2,1)S(1)}, u32[]{:S(2)}, u32[]{:S(2)}) collective-permute-start(bf16[4,256,256]{2,1,0:T(8,128)(2,1)S(1)} %collective-permute-done.1.refs_2_), channel_id=1, source_target_pairs={{0,4},{4,0},{8,12},{12,8},{16,20},{20,16},{24,28},{28,24},{32,36},... | collective-permute-start | bytes 1572872 | tf_op jit(solution)/shard_map/ppermute | solution.py:46
  31.2 2.7 %collective-permute-start.4 = (bf16[2,256,256]{2,1,0:T(8,128)(2,1)S(1)}, bf16[2,256,256]{2,1,0:T(8,128)(2,1)S(1)}, u32[]{:S(2)}, u32[]{:S(2)}) collective-permute-start(bf16[2,256,256]{2,1,0:T(8,128)(2,1)S(1)} %slice.31), channel_id=1, source_target_pairs={{0,96},{4,28},{8,104},{12,4},{16,112},{20,12},{24,120},{28,20},{32... | collective-permute-start | bytes 786440 | tf_op jit(solution)/shard_map/ppermute | solution.py:42
  33.9 4.8 %next_stage.1 = (bf16[24,64,512]{2,1,0:T(8,128)(2,1)S(1)}, bf16[16,256,256]{2,1,0:T(8,128)(2,1)S(1)}, bf16[8,256,256]{2,1,0:T(8,128)(2,1)S(1)}) custom-call(s32[24,128]{1,0:T(8,128)S(1)} %plan.1.sched, bf16[2,24,64,512]{3,2,1,0:T(8,128)(2,1)S(1)} %get-tuple-element.25.refs_0_, ...), custom_call_target="tpu_custom_call", output_to_operand_aliasing={{0}: (7, {})} | custom-call | flops 503316480 | tf_op jit(solution)/shard_map/next_stage/pallas_call | solution.py:236
  38.7 1.1 %collective-permute-start.7 = (bf16[2,256,256]{2,1,0:T(8,128)(2,1)S(1)}, bf16[2,256,256]{2,1,0:T(8,128)(2,1)S(1)}, u32[]{:S(2)}, u32[]{:S(2)}) collective-permute-start(bf16[2,256,256]{2,1,0:T(8,128)(2,1)S(1)} %collective-permute-done.3.refs_2_), channel_id=1, source_target_pairs={{0,4},{4,0},{8,12},{12,8},{16,20},{20,16},{24,28},{28,24},{32,36},... | collective-permute-start | bytes 786440 | tf_op jit(solution)/shard_map/ppermute | solution.py:46
  40.3 0.7 collective-permute-done.7.refs_4_
  41.4 4.5 %far_stage.1 = (bf16[24,64,512]{2,1,0:T(8,128)(2,1)S(1)}, bf16[8,256,256]{2,1,0:T(8,128)(2,1)S(1)}, bf16[4,256,256]{2,1,0:T(8,128)(2,1)S(1)}, bf16[24,64,512]{2,1,0:T(8,128)(2,1)}) custom-call(s32[24,128]{1,0:T(8,128)S(1)} %plan.1.sched, bf16[2,24,64,512]{3,2,1,0:T(8,128)(2,1)S(1)} %get-tuple-element.25.refs_0_, ...), custom_call_target="tpu_custom_call", output_to_operand_aliasing={{0}: (7, {})} | custom-call | flops 503316480 | tf_op jit(solution)/shard_map/far_stage/pallas_call | solution.py:236
  46.5 1.4 %collective-permute-done.13 = bf16[4,256,256]{2,1,0:T(8,128)(2,1)S(1)} collective-permute-done((bf16[4,256,256]{2,1,0:T(8,128)(2,1)S(1)}, bf16[4,256,256]{2,1,0:T(8,128)(2,1)S(1)}, u32[]{:S(2)}, u32[]{:S(2)}) %collective-permute-start.13) | collective-permute-done | bytes 524320 | tf_op jit(solution)/shard_map/ppermute | solution.py:46
  48.0 0.5 collective-permute-start.14
  48.9 2.4 %collective-permute-start.11 = (bf16[4,256,256]{2,1,0:T(8,128)(2,1)S(1)}, bf16[4,256,256]{2,1,0:T(8,128)(2,1)S(1)}, u32[]{:S(2)}, u32[]{:S(2)}) collective-permute-start(bf16[4,256,256]{2,1,0:T(8,128)(2,1)S(1)} %get-tuple-element.41), channel_id=1, source_target_pairs={{0,96},{4,28},{8,104},{12,4},{16,112},{20,12},{24,120},{28,20},{32... | collective-permute-start | bytes 1572872 | tf_op jit(solution)/shard_map/ppermute | solution.py:42
  51.6 6.4 %collective-permute-done.14 = bf16[4,256,256]{2,1,0:T(8,128)(2,1)S(1)} collective-permute-done((bf16[4,256,256]{2,1,0:T(8,128)(2,1)S(1)}, bf16[4,256,256]{2,1,0:T(8,128)(2,1)S(1)}, u32[]{:S(2)}, u32[]{:S(2)}) %collective-permute-start.14) | collective-permute-done | bytes 524320 | tf_op jit(solution)/shard_map/ppermute | solution.py:42
  58.0 5.7 %collective-permute-done.11 = bf16[4,256,256]{2,1,0:T(8,128)(2,1)S(1)} collective-permute-done((bf16[4,256,256]{2,1,0:T(8,128)(2,1)S(1)}, bf16[4,256,256]{2,1,0:T(8,128)(2,1)S(1)}, u32[]{:S(2)}, u32[]{:S(2)}) %collective-permute-start.11) | collective-permute-done | bytes 524320 | tf_op jit(solution)/shard_map/ppermute | solution.py:42
  64.0 13.1 %all_to_all.10 = bf16[8,128,256]{2,1,0:T(8,128)(2,1)S(1)} all-to-all(bf16[8,128,256]{2,1,0:T(8,128)(2,1)S(1)} %bitcast.51), channel_id=1, replica_groups={{0,1,8,9,16,17,24,25},{32,33,40,41,48,49,56,57},{64,65,72,73,80,81,88,8..., dimensions={0} | all-to-all | bytes 1048576 | tf_op jit(solution)/shard_map/all_to_all | solution.py:33
  77.2 0.6 slice_bitcast_fusion
  (27 shorter events, 3.1 us)
Async XLA Ops:
  2.3 15.4 %all-to-all-start = ((bf16[8,128,256]{2,1,0:T(8,128)(2,1)}), bf16[8,128,256]{2,1,0:T(8,128)(2,1)S(1)}, u32[]{:S(2)}, u32[]{:S(2)}) async-start(bf16[8,128,256]{2,1,0:T(8,128)(2,1)} %spread.1), calls=%async_computation | async-start | bytes 1048576 | tf_op jit(solution)/shard_map/all_to_all | solution.py:33
  17.7 5.5 %collective-permute-start = (bf16[4,256,256]{2,1,0:T(8,128)(2,1)S(1)}, bf16[4,256,256]{2,1,0:T(8,128)(2,1)S(1)}, u32[]{:S(2)}, u32[]{:S(2)}) collective-permute-start(bf16[4,256,256]{2,1,0:T(8,128)(2,1)S(1)} %bitcast.47), channel_id=1, source_target_pairs={{0,4},{4,0},{8,12},{12,8},{16,20},{20,16},{24,28},{28,24},{32,36},... | collective-permute-start | bytes 1572872 | tf_op jit(solution)/shard_map/ppermute | solution.py:46
  20.4 9.5 %collective-permute-start.1 = (bf16[4,256,256]{2,1,0:T(8,128)(2,1)S(1)}, bf16[4,256,256]{2,1,0:T(8,128)(2,1)S(1)}, u32[]{:S(2)}, u32[]{:S(2)}) collective-permute-start(bf16[4,256,256]{2,1,0:T(8,128)(2,1)S(1)} %bitcast.48), channel_id=1, source_target_pairs={{0,32},{4,12},{8,40},{12,20},{16,48},{20,28},{24,56},{28,4},{32,64... | collective-permute-start | bytes 1572872 | tf_op jit(solution)/shard_map/ppermute | solution.py:42
  20.5 9.5 %collective-permute-start.2 = (bf16[4,256,256]{2,1,0:T(8,128)(2,1)S(1)}, bf16[4,256,256]{2,1,0:T(8,128)(2,1)S(1)}, u32[]{:S(2)}, u32[]{:S(2)}) collective-permute-start(bf16[4,256,256]{2,1,0:T(8,128)(2,1)S(1)} %bitcast.49), channel_id=1, source_target_pairs={{0,96},{4,28},{8,104},{12,4},{16,112},{20,12},{24,120},{28,20},{32... | collective-permute-start | bytes 1572872 | tf_op jit(solution)/shard_map/ppermute | solution.py:42
  30.0 3.9 %collective-permute-start.5 = (bf16[4,256,256]{2,1,0:T(8,128)(2,1)S(1)}, bf16[4,256,256]{2,1,0:T(8,128)(2,1)S(1)}, u32[]{:S(2)}, u32[]{:S(2)}) collective-permute-start(bf16[4,256,256]{2,1,0:T(8,128)(2,1)S(1)} %collective-permute-done.1.refs_2_), channel_id=1, source_target_pairs={{0,4},{4,0},{8,12},{12,8},{16,20},{20,16},{24,28},{28,24},{32,36},... | collective-permute-start | bytes 1572872 | tf_op jit(solution)/shard_map/ppermute | solution.py:46
  31.1 2.8 %collective-permute-start.6 = (bf16[4,256,256]{2,1,0:T(8,128)(2,1)S(1)}, bf16[4,256,256]{2,1,0:T(8,128)(2,1)S(1)}, u32[]{:S(2)}, u32[]{:S(2)}) collective-permute-start(bf16[4,256,256]{2,1,0:T(8,128)(2,1)S(1)} %collective-permute-done.2.refs_3_), channel_id=1, source_target_pairs={{0,4},{4,0},{8,12},{12,8},{16,20},{20,16},{24,28},{28,24},{32,36},... | collective-permute-start | bytes 1572872 | tf_op jit(solution)/shard_map/ppermute | solution.py:46
  31.1 7.5 %collective-permute-start.3 = (bf16[2,256,256]{2,1,0:T(8,128)(2,1)S(1)}, bf16[2,256,256]{2,1,0:T(8,128)(2,1)S(1)}, u32[]{:S(2)}, u32[]{:S(2)}) collective-permute-start(bf16[2,256,256]{2,1,0:T(8,128)(2,1)S(1)} %slice.30), channel_id=1, source_target_pairs={{0,32},{4,12},{8,40},{12,20},{16,48},{20,28},{24,56},{28,4},{32,64... | collective-permute-start | bytes 786440 | tf_op jit(solution)/shard_map/ppermute | solution.py:42
  31.2 7.5 %collective-permute-start.4 = (bf16[2,256,256]{2,1,0:T(8,128)(2,1)S(1)}, bf16[2,256,256]{2,1,0:T(8,128)(2,1)S(1)}, u32[]{:S(2)}, u32[]{:S(2)}) collective-permute-start(bf16[2,256,256]{2,1,0:T(8,128)(2,1)S(1)} %slice.31), channel_id=1, source_target_pairs={{0,96},{4,28},{8,104},{12,4},{16,112},{20,12},{24,120},{28,20},{32... | collective-permute-start | bytes 786440 | tf_op jit(solution)/shard_map/ppermute | solution.py:42
  38.7 2.3 %collective-permute-start.7 = (bf16[2,256,256]{2,1,0:T(8,128)(2,1)S(1)}, bf16[2,256,256]{2,1,0:T(8,128)(2,1)S(1)}, u32[]{:S(2)}, u32[]{:S(2)}) collective-permute-start(bf16[2,256,256]{2,1,0:T(8,128)(2,1)S(1)} %collective-permute-done.3.refs_2_), channel_id=1, source_target_pairs={{0,4},{4,0},{8,12},{12,8},{16,20},{20,16},{24,28},{28,24},{32,36},... | collective-permute-start | bytes 786440 | tf_op jit(solution)/shard_map/ppermute | solution.py:46
  39.8 1.5 %collective-permute-start.8 = (bf16[2,256,256]{2,1,0:T(8,128)(2,1)S(1)}, bf16[2,256,256]{2,1,0:T(8,128)(2,1)S(1)}, u32[]{:S(2)}, u32[]{:S(2)}) collective-permute-start(bf16[2,256,256]{2,1,0:T(8,128)(2,1)S(1)} %collective-permute-done.4.refs_3_), channel_id=1, source_target_pairs={{0,4},{4,0},{8,12},{12,8},{16,20},{20,16},{24,28},{28,24},{32,36},... | collective-permute-start | bytes 786440 | tf_op jit(solution)/shard_map/ppermute | solution.py:46
  39.9 8.6 %collective-permute-start.10 = (bf16[8,256,256]{2,1,0:T(8,128)(2,1)S(1)}, bf16[8,256,256]{2,1,0:T(8,128)(2,1)S(1)}, u32[]{:S(2)}, u32[]{:S(2)}) collective-permute-start(bf16[8,256,256]{2,1,0:T(8,128)(2,1)S(1)} %get-tuple-element.38), channel_id=1, source_target_pairs={{0,4},{4,0},{8,12},{12,8},{16,20},{20,16},{24,28},{28,24},{32,36},... | collective-permute-start | bytes 3145736 | tf_op jit(solution)/shard_map/ppermute | solution.py:46
  45.9 2.0 %collective-permute-start.13 = (bf16[4,256,256]{2,1,0:T(8,128)(2,1)S(1)}, bf16[4,256,256]{2,1,0:T(8,128)(2,1)S(1)}, u32[]{:S(2)}, u32[]{:S(2)}) collective-permute-start(bf16[4,256,256]{2,1,0:T(8,128)(2,1)S(1)} %get-tuple-element.40), channel_id=1, source_target_pairs={{0,4},{4,0},{8,12},{12,8},{16,20},{20,16},{24,28},{28,24},{32,36},... | collective-permute-start | bytes 1572872 | tf_op jit(solution)/shard_map/ppermute | solution.py:46
  46.4 5.3 %collective-permute-start.9 = (bf16[4,256,256]{2,1,0:T(8,128)(2,1)S(1)}, bf16[4,256,256]{2,1,0:T(8,128)(2,1)S(1)}, u32[]{:S(2)}, u32[]{:S(2)}) collective-permute-start(bf16[4,256,256]{2,1,0:T(8,128)(2,1)S(1)} %get-tuple-element.36), channel_id=1, source_target_pairs={{0,4},{4,0},{8,12},{12,8},{16,20},{20,16},{24,28},{28,24},{32,36},... | collective-permute-start | bytes 1572872 | tf_op jit(solution)/shard_map/ppermute | solution.py:46
  48.0 10.0 %collective-permute-start.14 = (bf16[4,256,256]{2,1,0:T(8,128)(2,1)S(1)}, bf16[4,256,256]{2,1,0:T(8,128)(2,1)S(1)}, u32[]{:S(2)}, u32[]{:S(2)}) collective-permute-start(bf16[4,256,256]{2,1,0:T(8,128)(2,1)S(1)} %add_convert_fusion.1), channel_id=1, source_target_pairs={{0,64},{4,20},{8,72},{12,28},{16,80},{20,4},{24,88},{28,12},{32,96... | collective-permute-start | bytes 1572872 | tf_op jit(solution)/shard_map/ppermute | solution.py:42
  48.9 14.8 %collective-permute-start.11 = (bf16[4,256,256]{2,1,0:T(8,128)(2,1)S(1)}, bf16[4,256,256]{2,1,0:T(8,128)(2,1)S(1)}, u32[]{:S(2)}, u32[]{:S(2)}) collective-permute-start(bf16[4,256,256]{2,1,0:T(8,128)(2,1)S(1)} %get-tuple-element.41), channel_id=1, source_target_pairs={{0,96},{4,28},{8,104},{12,4},{16,112},{20,12},{24,120},{28,20},{32... | collective-permute-start | bytes 1572872 | tf_op jit(solution)/shard_map/ppermute | solution.py:42
  51.2 12.5 %collective-permute-start.12 = (bf16[4,256,256]{2,1,0:T(8,128)(2,1)S(1)}, bf16[4,256,256]{2,1,0:T(8,128)(2,1)S(1)}, u32[]{:S(2)}, u32[]{:S(2)}) collective-permute-start(bf16[4,256,256]{2,1,0:T(8,128)(2,1)S(1)} %get-tuple-element.42), channel_id=1, source_target_pairs={{0,32},{4,12},{8,40},{12,20},{16,48},{20,28},{24,56},{28,4},{32,64... | collective-permute-start | bytes 1572872 | tf_op jit(solution)/shard_map/ppermute | solution.py:42

commit v4 on v3

--- a/solution.py
+++ b/solution.py
@@ -78,6 +78,24 @@
         ],
         name="spread",
     )(keys, values)
+
+
+def settle_kernel(source, target, sem):
+    copy = pltpu.make_async_copy(source, target, sem)
+    copy.start()
+    copy.wait()
+
+
+def settle(x):
+    return pl.pallas_call(
+        settle_kernel,
+        out_shape=jax.ShapeDtypeStruct(x.shape, x.dtype),
+        in_specs=[pl.BlockSpec(memory_space=pltpu.VMEM)],
+        out_specs=pl.BlockSpec(memory_space=pl.ANY),
+        scratch_shapes=[pltpu.SemaphoreType.DMA],
+        compiler_params=pltpu.CompilerParams(vmem_limit_bytes=1 << 20),
+        name="settle",
+    )(held(x))
 
 
 def plan_kernel(code_ref, out):
@@ -166,7 +184,7 @@
         query_grad, sums, there, tile_rows, near, arrived = refs[3 + len(sizes):]
     else:
         tile_rows, stats, *blocks = refs[:2 + len(sizes)]
-        query_grad, sums, there, *result, near, arrived = refs[3 + len(sizes):]
+        query_grad, sums, there, near, arrived = refs[3 + len(sizes):]
     _, _, rows, width = tile_rows.shape
     heads = width // 128
     scaling = 128 ** -0.5
@@ -215,10 +233,6 @@
     lax.fori_loop(0, count, step, 0)
     handed = pltpu.make_async_copy(sums.at[places // 2:places], there, arrived.at[0])
     handed.start()
-    if turn == STAGES - 1:
-        final = pltpu.make_async_copy(query_grad, result[0], arrived.at[1])
-        final.start()
-        final.wait()
     handed.wait()
 
 
@@ -229,7 +243,7 @@
     block_shape = blocks[0].shape[1:]
     whole = pl.BlockSpec(memory_space=pltpu.VMEM)
     away = pl.BlockSpec(memory_space=pl.ANY)
-    first, last = turn == 0, turn == STAGES - 1
+    first = turn == 0
     shape = tile_rows[0].shape
     rows = [distant(x) for x in tile_rows] if first else [held(tile_rows)]
     operands = [sched, *rows, held(stats), *blocks] + ([] if first else [held(query_grad)])
@@ -239,10 +253,10 @@
             pltpu.VMEM(shape, kind),
             pltpu.VMEM((places, *block_shape), kind),
             jax.ShapeDtypeStruct((places // 2, *block_shape), kind),
-        ] + [pltpu.VMEM((2, *shape), kind)] * first + [jax.ShapeDtypeStruct(shape, kind)] * last,
+        ] + [pltpu.VMEM((2, *shape), kind)] * first,
         in_specs=[pl.BlockSpec(memory_space=pltpu.SMEM)] + ([pl.BlockSpec(memory_space=pltpu.HBM)] * 2 if first else [whole]) + [whole]
         + [away] * len(blocks) + [whole] * (not first),
-        out_specs=[whole, whole, away] + [whole] * first + [away] * last,
+        out_specs=[whole, whole, away] + [whole] * first,
         scratch_shapes=[
             pltpu.VMEM((places, *block_shape), kind),
             pltpu.SemaphoreType.DMA((len(blocks) + 2,)),
@@ -256,11 +270,15 @@
     )(*operands)
 
 
-def add(*parts):
+def wide(*parts):
     total = parts[0].astype(jnp.float32)
     for part in parts[1:]:
         total = total + part.astype(jnp.float32)
-    return total.astype(jnp.bfloat16)
+    return total
+
+
+def add(*parts):
+    return wide(*parts).astype(jnp.bfloat16)
 
 
 def shards(queries, output_gradient, prefix_keys, prefix_values, tile_prefix, suffix_lse, suffix_dot):
@@ -296,7 +314,7 @@
     def work(turn, block, tile_rows, query_grad):
         query_grad, sums, there, *rest = stage(turn, sched, tile_rows, stats, block, query_grad)
         here.append(sums)
-        back.append(swap_cores(there))
+        back.append(there)
         return query_grad, *rest
 
     def both(*block):
@@ -307,12 +325,19 @@
     far = shift(up[0:2], 1), shift(down[2:4], -1)
     query_grad, = work(1, both(up, down), tile_rows, query_grad)
     far, query_grad = lax.optimization_barrier((far, query_grad))
-    _, query_grad = work(2, both(*far), tile_rows, query_grad)
-
-    from_up = shift(add(here[1][0:4], back[1][0:4]), -1)
-    from_down = shift(add(here[1][4:8], back[1][4:8]), 1)
+    others = [swap_cores(x) for x in far]
+    back[1], *others = lax.optimization_barrier((back[1], *others))
+    query_grad, = work(2, [*far, *others], tile_rows, query_grad)
+    back = [swap_cores(x) for x in back]
+
+    to_up, to_down = add(here[1][0:4], back[1][0:4]), add(here[1][4:8], back[1][4:8])
+    to_up, to_down, back[2] = lax.optimization_barrier((to_up, to_down, back[2]))
+    from_up, from_down = shift(to_up, -1), shift(to_down, 1)
     from_far = shift(add(here[2][0:4], back[2]), 2)
-    line_sum = add(here[0][0:4], back[0], from_up, from_down, from_far)
+    query_grad = settle(query_grad)
+    near_sum, query_grad = lax.optimization_barrier(
+        (wide(here[0][0:4], back[0], from_up, from_down), query_grad))
+    line_sum = add(near_sum, from_far)
     total = add(*exchange_line(line_sum.reshape(own.shape)))
     return query_grad, total[None, :, 0:128], total[None, :, 128:256]
 

time: 78.8 us -> 77.6 us (0.985)
  the two profiles are of different devices: /device:TPU:1 before, /device:TPU:0 now
where the time goes in v4:
time: 77.6 us; the launch traced here: 77.3 us
  waiting for transfers between devices  24.6 us (32%)
  starting transfers between devices  18 us (23%)
  Pallas kernels  17 us (22%)
  blocking collectives  12.9 us (17%)
  local copies, waits for them, and re-layouts  2.33 us (3%)
  other arithmetic  1.69 us (2%)
    ppermute x7, waiting for transfers between devices, shift(): return lax.ppermute(x, 'dp', pairs)  14.3 us
    pallas_call x3, Pallas kernels, stage(): pl.pallas_call(functools.partial(stage_kernel, turn, sizes), out_shape=[p...  13.3 us
    all_to_all x1, blocking collectives, exchange_line(): lax.all_to_all(x, ('dp', 'pos'), 0, 0, axis_index_groups=line_groups(), t...  12.9 us
    ppermute x7, starting transfers between devices, shift(): return lax.ppermute(x, 'dp', pairs)  10.6 us
    all_to_all x1, waiting for transfers between devices, exchange_line(): lax.all_to_all(x, ('dp', 'pos'), 0, 0, axis_index_groups=line_groups(), t...  7.81 us
    all_to_all x1, starting transfers between devices, exchange_line(): lax.all_to_all(x, ('dp', 'pos'), 0, 0, axis_index_groups=line_groups(), t...  5.49 us
    ppermute x8, waiting for transfers between devices, swap_cores(): return lax.ppermute(x, 'dp', [(i, i ^ 1) for i in range(2 * SIDE * SIDE)])  2.52 us
    ppermute x8, starting transfers between devices, swap_cores(): return lax.ppermute(x, 'dp', [(i, i ^ 1) for i in range(2 * SIDE * SIDE)])  1.82 us
  transfers between devices with their start and end apart: 16, of which 9 were waited for; matrix products, arithmetic and copies ran while one was open for 4% of the time, Pallas kernels for 20%

profile of v4, /device:TPU:0, one launch (start us, length us, event | category | flops | bytes accessed | tf_op | source)
XLA Modules:
  0.0 77.3 jit_solution(10372019153697273378)
XLA Ops:
  0.6 1.6 %spread.1 = bf16[8,128,256]{2,1,0:T(8,128)(2,1)} custom-call(bf16[1,128,128]{2,1,0:T(8,128)(2,1)} %keys.1, bf16[1,128,128]{2,1,0:T(8,128)(2,1)} %values.1), custom_call_target="tpu_custom_call" | custom-call | tf_op jit(solution)/shard_map/spread/pallas_call | solution.py:70
  2.3 5.5 %all-to-all-start = ((bf16[8,128,256]{2,1,0:T(8,128)(2,1)}), bf16[8,128,256]{2,1,0:T(8,128)(2,1)S(1)}, u32[]{:S(2)}, u32[]{:S(2)}) async-start(bf16[8,128,256]{2,1,0:T(8,128)(2,1)} %spread.1), calls=%async_computation | async-start | bytes 1048576 | tf_op jit(solution)/shard_map/all_to_all | solution.py:33
  7.8 0.8 fusion.5
  9.0 0.9 %plan.1.sched = s32[24,128]{1,0:T(8,128)S(1)} custom-call(s32[1,128]{1,0:T(1,128)} %pad.4.code_ref), custom_call_target="tpu_custom_call" | custom-call | tf_op jit(solution)/shard_map/plan/pallas_call | solution.py:137
  10.0 0.9 %dynamic-slice_bitcast_fusion = (f32[24,4,64]{2,1,0:T(4,128)S(1)}, f32[24,4,64]{2,1,0:T(4,128)S(1)}) fusion(f32[768,128,4]{1,2,0:T(4,128)} %param.13, s32[]{:T(128)S(6)} %select_n.44, s32[]{:T(128)S(6)} %select_n.48, f32[768,128,4]{1,2,0:T(4,128)} %param.12), kind=kLoop, calls=%fused_computation.8 | loop fusion | bytes 98312 | tf_op jit(solution)/shard_map/dynamic_slice | solution.py:304
  11.2 7.8 %all-to-all-done = bf16[8,128,256]{2,1,0:T(8,128)(2,1)S(1)} async-done(((bf16[8,128,256]{2,1,0:T(8,128)(2,1)}), bf16[8,128,256]{2,1,0:T(8,128)(2,1)S(1)}, u32[]{:S(2)}, u32[]{:S(2)}) %all-to-all-start) | async-done | bytes 524320 | tf_op jit(solution)/shard_map/all_to_all | solution.py:33
  19.0 1.5 %collective-permute-start.2 = (bf16[4,256,256]{2,1,0:T(8,128)(2,1)S(1)}, bf16[4,256,256]{2,1,0:T(8,128)(2,1)S(1)}, u32[]{:S(2)}, u32[]{:S(2)}) collective-permute-start(bf16[4,256,256]{2,1,0:T(8,128)(2,1)S(1)} %bitcast.48), channel_id=1, source_target_pairs={{0,32},{4,12},{8,40},{12,20},{16,48},{20,28},{24,56},{28,4},{32,64... | collective-permute-start | bytes 1572872 | tf_op jit(solution)/shard_map/ppermute | solution.py:42
  20.5 1.8 %collective-permute-start.3 = (bf16[4,256,256]{2,1,0:T(8,128)(2,1)S(1)}, bf16[4,256,256]{2,1,0:T(8,128)(2,1)S(1)}, u32[]{:S(2)}, u32[]{:S(2)}) collective-permute-start(bf16[4,256,256]{2,1,0:T(8,128)(2,1)S(1)} %bitcast.49), channel_id=1, source_target_pairs={{0,96},{4,28},{8,104},{12,4},{16,112},{20,12},{24,120},{28,20},{32... | collective-permute-start | bytes 1572872 | tf_op jit(solution)/shard_map/ppermute | solution.py:42
  22.3 4.0 %line_stage.1 = (bf16[24,64,512]{2,1,0:T(8,128)(2,1)S(1)}, bf16[8,256,256]{2,1,0:T(8,128)(2,1)S(1)}, bf16[4,256,256]{2,1,0:T(8,128)(2,1)S(1)}, bf16[2,24,64,512]{3,2,1,0:T(8,128)(2,1)S(1)}) custom-call(s32[24,128]{1,0:T(8,128)S(1)} %plan.1.sched, bf16[24,64,512]{2,1,0:T(8,128)(2,1)} %refs_0_.1, bf16[24,64,512]{2,1,0:T(8,128)(2,1)} %refs_1_.1, ...), custom_call_target="tpu_custom_call" | custom-call | flops 503316480 | tf_op jit(solution)/shard_map/line_stage/pallas_call | solution.py:250
  26.2 3.2 %collective-permute-done.2.refs_2_ = bf16[4,256,256]{2,1,0:T(8,128)(2,1)S(1)} collective-permute-done((bf16[4,256,256]{2,1,0:T(8,128)(2,1)S(1)}, bf16[4,256,256]{2,1,0:T(8,128)(2,1)S(1)}, u32[]{:S(2)}, u32[]{:S(2)}) %collective-permute-start.2) | collective-permute-done | bytes 524320 | tf_op jit(solution)/shard_map/ppermute | solution.py:42
  30.2 1.5 %collective-permute-start.6 = (bf16[2,256,256]{2,1,0:T(8,128)(2,1)S(1)}, bf16[2,256,256]{2,1,0:T(8,128)(2,1)S(1)}, u32[]{:S(2)}, u32[]{:S(2)}) collective-permute-start(bf16[2,256,256]{2,1,0:T(8,128)(2,1)S(1)} %slice.32), channel_id=1, source_target_pairs={{0,32},{4,12},{8,40},{12,20},{16,48},{20,28},{24,56},{28,4},{32,64... | collective-permute-start | bytes 786440 | tf_op jit(solution)/shard_map/ppermute | solution.py:42
  31.8 1.8 %collective-permute-start.7 = (bf16[2,256,256]{2,1,0:T(8,128)(2,1)S(1)}, bf16[2,256,256]{2,1,0:T(8,128)(2,1)S(1)}, u32[]{:S(2)}, u32[]{:S(2)}) collective-permute-start(bf16[2,256,256]{2,1,0:T(8,128)(2,1)S(1)} %slice.33), channel_id=1, source_target_pairs={{0,96},{4,28},{8,104},{12,4},{16,112},{20,12},{24,120},{28,20},{32... | collective-permute-start | bytes 786440 | tf_op jit(solution)/shard_map/ppermute | solution.py:42
  33.5 6.0 %next_stage.1 = (bf16[24,64,512]{2,1,0:T(8,128)(2,1)S(1)}, bf16[16,256,256]{2,1,0:T(8,128)(2,1)S(1)}, bf16[8,256,256]{2,1,0:T(8,128)(2,1)S(1)}) custom-call(s32[24,128]{1,0:T(8,128)S(1)} %plan.1.sched, bf16[2,24,64,512]{3,2,1,0:T(8,128)(2,1)S(1)} %get-tuple-element.35.refs_0_, ...), custom_call_target="tpu_custom_call", output_to_operand_aliasing={{0}: (7, {})} | custom-call | flops 503316480 | tf_op jit(solution)/shard_map/next_stage/pallas_call | solution.py:250
  40.1 1.0 %collective-permute-done.8.refs_4_ = bf16[2,256,256]{2,1,0:T(8,128)(2,1)S(1)} collective-permute-done((bf16[2,256,256]{2,1,0:T(8,128)(2,1)S(1)}, bf16[2,256,256]{2,1,0:T(8,128)(2,1)S(1)}, u32[]{:S(2)}, u32[]{:S(2)}) %collective-permute-start.8) | collective-permute-done | bytes 262176 | tf_op jit(solution)/shard_map/ppermute | solution.py:46
  41.7 3.4 %far_stage.1 = (bf16[24,64,512]{2,1,0:T(8,128)(2,1)S(1)}, bf16[8,256,256]{2,1,0:T(8,128)(2,1)S(1)}, bf16[4,256,256]{2,1,0:T(8,128)(2,1)S(1)}) custom-call(s32[24,128]{1,0:T(8,128)S(1)} %plan.1.sched, bf16[2,24,64,512]{3,2,1,0:T(8,128)(2,1)S(1)} %get-tuple-element.35.refs_0_, ...), custom_call_target="tpu_custom_call", output_to_operand_aliasing={{0}: (7, {})} | custom-call | flops 503316480 | tf_op jit(solution)/shard_map/far_stage/pallas_call | solution.py:250
  45.9 1.1 %collective-permute-done.11 = bf16[4,256,256]{2,1,0:T(8,128)(2,1)S(1)} collective-permute-done((bf16[4,256,256]{2,1,0:T(8,128)(2,1)S(1)}, bf16[4,256,256]{2,1,0:T(8,128)(2,1)S(1)}, u32[]{:S(2)}, u32[]{:S(2)}) %collective-permute-start.11) | collective-permute-done | bytes 524320 | tf_op jit(solution)/shard_map/ppermute | solution.py:46
  47.0 0.8 collective-permute-start.13
  47.8 2.5 %collective-permute-start.12 = (bf16[4,256,256]{2,1,0:T(8,128)(2,1)S(1)}, bf16[4,256,256]{2,1,0:T(8,128)(2,1)S(1)}, u32[]{:S(2)}, u32[]{:S(2)}) collective-permute-start(bf16[4,256,256]{2,1,0:T(8,128)(2,1)S(1)} %get-tuple-element.50), channel_id=1, source_target_pairs={{0,96},{4,28},{8,104},{12,4},{16,112},{20,12},{24,120},{28,20},{32... | collective-permute-start | bytes 1572872 | tf_op jit(solution)/shard_map/ppermute | solution.py:42
  50.4 0.9 %collective-permute-start.14 = (bf16[4,256,256]{2,1,0:T(8,128)(2,1)S(1)}, bf16[4,256,256]{2,1,0:T(8,128)(2,1)S(1)}, u32[]{:S(2)}, u32[]{:S(2)}) collective-permute-start(bf16[4,256,256]{2,1,0:T(8,128)(2,1)S(1)} %add_convert_fusion.1), channel_id=1, source_target_pairs={{0,64},{4,20},{8,72},{12,28},{16,80},{20,4},{24,88},{28,12},{32,96... | collective-permute-start | bytes 1572872 | tf_op jit(solution)/shard_map/ppermute | solution.py:42
  51.3 1.1 %settle.1 = bf16[24,64,512]{2,1,0:T(8,128)(2,1)} custom-call(bf16[24,64,512]{2,1,0:T(8,128)(2,1)S(1)} %get-tuple-element.52.source), custom_call_target="tpu_custom_call" | custom-call | tf_op jit(solution)/shard_map/settle/pallas_call | solution.py:90
  52.4 5.0 %collective-permute-done.13 = bf16[4,256,256]{2,1,0:T(8,128)(2,1)S(1)} collective-permute-done((bf16[4,256,256]{2,1,0:T(8,128)(2,1)S(1)}, bf16[4,256,256]{2,1,0:T(8,128)(2,1)S(1)}, u32[]{:S(2)}, u32[]{:S(2)}) %collective-permute-start.13) | collective-permute-done | bytes 524320 | tf_op jit(solution)/shard_map/ppermute | solution.py:42
  57.4 5.2 %collective-permute-done.12 = bf16[4,256,256]{2,1,0:T(8,128)(2,1)S(1)} collective-permute-done((bf16[4,256,256]{2,1,0:T(8,128)(2,1)S(1)}, bf16[4,256,256]{2,1,0:T(8,128)(2,1)S(1)}, u32[]{:S(2)}, u32[]{:S(2)}) %collective-permute-start.12) | collective-permute-done | bytes 524320 | tf_op jit(solution)/shard_map/ppermute | solution.py:42
  62.9 0.7 collective-permute-done.14
  63.7 12.9 %all_to_all.10 = bf16[8,128,256]{2,1,0:T(8,128)(2,1)S(1)} all-to-all(bf16[8,128,256]{2,1,0:T(8,128)(2,1)S(1)} %bitcast.51), channel_id=1, replica_groups={{0,1,8,9,16,17,24,25},{32,33,40,41,48,49,56,57},{64,65,72,73,80,81,88,8..., dimensions={0} | all-to-all | bytes 1048576 | tf_op jit(solution)/shard_map/all_to_all | solution.py:33
  (29 shorter events, 4.8 us)
Async XLA Ops:
  2.3 16.8 %all-to-all-start = ((bf16[8,128,256]{2,1,0:T(8,128)(2,1)}), bf16[8,128,256]{2,1,0:T(8,128)(2,1)S(1)}, u32[]{:S(2)}, u32[]{:S(2)}) async-start(bf16[8,128,256]{2,1,0:T(8,128)(2,1)} %spread.1), calls=%async_computation | async-start | bytes 1048576 | tf_op jit(solution)/shard_map/all_to_all | solution.py:33
  19.0 3.2 %collective-permute-start = (bf16[4,256,256]{2,1,0:T(8,128)(2,1)S(1)}, bf16[4,256,256]{2,1,0:T(8,128)(2,1)S(1)}, u32[]{:S(2)}, u32[]{:S(2)}) collective-permute-start(bf16[4,256,256]{2,1,0:T(8,128)(2,1)S(1)} %bitcast.47), channel_id=1, source_target_pairs={{0,4},{4,0},{8,12},{12,8},{16,20},{20,16},{24,28},{28,24},{32,36},... | collective-permute-start | bytes 1572872 | tf_op jit(solution)/shard_map/ppermute | solution.py:46
  19.0 10.4 %collective-permute-start.2 = (bf16[4,256,256]{2,1,0:T(8,128)(2,1)S(1)}, bf16[4,256,256]{2,1,0:T(8,128)(2,1)S(1)}, u32[]{:S(2)}, u32[]{:S(2)}) collective-permute-start(bf16[4,256,256]{2,1,0:T(8,128)(2,1)S(1)} %bitcast.48), channel_id=1, source_target_pairs={{0,32},{4,12},{8,40},{12,20},{16,48},{20,28},{24,56},{28,4},{32,64... | collective-permute-start | bytes 1572872 | tf_op jit(solution)/shard_map/ppermute | solution.py:42
  20.5 9.2 %collective-permute-start.3 = (bf16[4,256,256]{2,1,0:T(8,128)(2,1)S(1)}, bf16[4,256,256]{2,1,0:T(8,128)(2,1)S(1)}, u32[]{:S(2)}, u32[]{:S(2)}) collective-permute-start(bf16[4,256,256]{2,1,0:T(8,128)(2,1)S(1)} %bitcast.49), channel_id=1, source_target_pairs={{0,96},{4,28},{8,104},{12,4},{16,112},{20,12},{24,120},{28,20},{32... | collective-permute-start | bytes 1572872 | tf_op jit(solution)/shard_map/ppermute | solution.py:42
  29.7 3.9 %collective-permute-start.4 = (bf16[4,256,256]{2,1,0:T(8,128)(2,1)S(1)}, bf16[4,256,256]{2,1,0:T(8,128)(2,1)S(1)}, u32[]{:S(2)}, u32[]{:S(2)}) collective-permute-start(bf16[4,256,256]{2,1,0:T(8,128)(2,1)S(1)} %collective-permute-done.2.refs_2_), channel_id=1, source_target_pairs={{0,4},{4,0},{8,12},{12,8},{16,20},{20,16},{24,28},{28,24},{32,36},... | collective-permute-start | bytes 1572872 | tf_op jit(solution)/shard_map/ppermute | solution.py:46
  29.7 3.9 %collective-permute-start.5 = (bf16[4,256,256]{2,1,0:T(8,128)(2,1)S(1)}, bf16[4,256,256]{2,1,0:T(8,128)(2,1)S(1)}, u32[]{:S(2)}, u32[]{:S(2)}) collective-permute-start(bf16[4,256,256]{2,1,0:T(8,128)(2,1)S(1)} %collective-permute-done.3.refs_3_), channel_id=1, source_target_pairs={{0,4},{4,0},{8,12},{12,8},{16,20},{20,16},{24,28},{28,24},{32,36},... | collective-permute-start | bytes 1572872 | tf_op jit(solution)/shard_map/ppermute | solution.py:46
  30.2 9.3 %collective-permute-start.6 = (bf16[2,256,256]{2,1,0:T(8,128)(2,1)S(1)}, bf16[2,256,256]{2,1,0:T(8,128)(2,1)S(1)}, u32[]{:S(2)}, u32[]{:S(2)}) collective-permute-start(bf16[2,256,256]{2,1,0:T(8,128)(2,1)S(1)} %slice.32), channel_id=1, source_target_pairs={{0,32},{4,12},{8,40},{12,20},{16,48},{20,28},{24,56},{28,4},{32,64... | collective-permute-start | bytes 786440 | tf_op jit(solution)/shard_map/ppermute | solution.py:42
  31.8 7.8 %collective-permute-start.7 = (bf16[2,256,256]{2,1,0:T(8,128)(2,1)S(1)}, bf16[2,256,256]{2,1,0:T(8,128)(2,1)S(1)}, u32[]{:S(2)}, u32[]{:S(2)}) collective-permute-start(bf16[2,256,256]{2,1,0:T(8,128)(2,1)S(1)} %slice.33), channel_id=1, source_target_pairs={{0,96},{4,28},{8,104},{12,4},{16,112},{20,12},{24,120},{28,20},{32... | collective-permute-start | bytes 786440 | tf_op jit(solution)/shard_map/ppermute | solution.py:42
  39.5 1.6 %collective-permute-start.8 = (bf16[2,256,256]{2,1,0:T(8,128)(2,1)S(1)}, bf16[2,256,256]{2,1,0:T(8,128)(2,1)S(1)}, u32[]{:S(2)}, u32[]{:S(2)}) collective-permute-start(bf16[2,256,256]{2,1,0:T(8,128)(2,1)S(1)} %collective-permute-done.6.refs_2_), channel_id=1, source_target_pairs={{0,4},{4,0},{8,12},{12,8},{16,20},{20,16},{24,28},{28,24},{32,36},... | collective-permute-start | bytes 786440 | tf_op jit(solution)/shard_map/ppermute | solution.py:46
  39.6 1.9 %collective-permute-start.9 = (bf16[2,256,256]{2,1,0:T(8,128)(2,1)S(1)}, bf16[2,256,256]{2,1,0:T(8,128)(2,1)S(1)}, u32[]{:S(2)}, u32[]{:S(2)}) collective-permute-start(bf16[2,256,256]{2,1,0:T(8,128)(2,1)S(1)} %collective-permute-done.7.refs_3_), channel_id=1, source_target_pairs={{0,4},{4,0},{8,12},{12,8},{16,20},{20,16},{24,28},{28,24},{32,36},... | collective-permute-start | bytes 786440 | tf_op jit(solution)/shard_map/ppermute | solution.py:46
  41.5 4.1 %collective-permute-start.10 = (bf16[8,256,256]{2,1,0:T(8,128)(2,1)S(1)}, bf16[8,256,256]{2,1,0:T(8,128)(2,1)S(1)}, u32[]{:S(2)}, u32[]{:S(2)}) collective-permute-start(bf16[8,256,256]{2,1,0:T(8,128)(2,1)S(1)} %get-tuple-element.45), channel_id=1, source_target_pairs={{0,4},{4,0},{8,12},{12,8},{16,20},{20,16},{24,28},{28,24},{32,36},... | collective-permute-start | bytes 3145736 | tf_op jit(solution)/shard_map/ppermute | solution.py:46
  45.1 2.0 %collective-permute-start.11 = (bf16[4,256,256]{2,1,0:T(8,128)(2,1)S(1)}, bf16[4,256,256]{2,1,0:T(8,128)(2,1)S(1)}, u32[]{:S(2)}, u32[]{:S(2)}) collective-permute-start(bf16[4,256,256]{2,1,0:T(8,128)(2,1)S(1)} %get-tuple-element.49), channel_id=1, source_target_pairs={{0,4},{4,0},{8,12},{12,8},{16,20},{20,16},{24,28},{28,24},{32,36},... | collective-permute-start | bytes 1572872 | tf_op jit(solution)/shard_map/ppermute | solution.py:46
  45.5 6.9 %collective-permute-start.1 = (bf16[4,256,256]{2,1,0:T(8,128)(2,1)S(1)}, bf16[4,256,256]{2,1,0:T(8,128)(2,1)S(1)}, u32[]{:S(2)}, u32[]{:S(2)}) collective-permute-start(bf16[4,256,256]{2,1,0:T(8,128)(2,1)S(1)} %get-tuple-element.34), channel_id=1, source_target_pairs={{0,4},{4,0},{8,12},{12,8},{16,20},{20,16},{24,28},{28,24},{32,36},... | collective-permute-start | bytes 1572872 | tf_op jit(solution)/shard_map/ppermute | solution.py:46
  47.0 10.4 %collective-permute-start.13 = (bf16[4,256,256]{2,1,0:T(8,128)(2,1)S(1)}, bf16[4,256,256]{2,1,0:T(8,128)(2,1)S(1)}, u32[]{:S(2)}, u32[]{:S(2)}) collective-permute-start(bf16[4,256,256]{2,1,0:T(8,128)(2,1)S(1)} %get-tuple-element.51), channel_id=1, source_target_pairs={{0,32},{4,12},{8,40},{12,20},{16,48},{20,28},{24,56},{28,4},{32,64... | collective-permute-start | bytes 1572872 | tf_op jit(solution)/shard_map/ppermute | solution.py:42
  47.8 14.8 %collective-permute-start.12 = (bf16[4,256,256]{2,1,0:T(8,128)(2,1)S(1)}, bf16[4,256,256]{2,1,0:T(8,128)(2,1)S(1)}, u32[]{:S(2)}, u32[]{:S(2)}) collective-permute-start(bf16[4,256,256]{2,1,0:T(8,128)(2,1)S(1)} %get-tuple-element.50), channel_id=1, source_target_pairs={{0,96},{4,28},{8,104},{12,4},{16,112},{20,12},{24,120},{28,20},{32... | collective-permute-start | bytes 1572872 | tf_op jit(solution)/shard_map/ppermute | solution.py:42
  50.4 13.1 %collective-permute-start.14 = (bf16[4,256,256]{2,1,0:T(8,128)(2,1)S(1)}, bf16[4,256,256]{2,1,0:T(8,128)(2,1)S(1)}, u32[]{:S(2)}, u32[]{:S(2)}) collective-permute-start(bf16[4,256,256]{2,1,0:T(8,128)(2,1)S(1)} %add_convert_fusion.1), channel_id=1, source_target_pairs={{0,64},{4,20},{8,72},{12,28},{16,80},{20,4},{24,88},{28,12},{32,96... | collective-permute-start | bytes 1572872 | tf_op jit(solution)/shard_map/ppermute | solution.py:42

commit v5 on v4

--- a/solution.py
+++ b/solution.py
@@ -331,7 +331,7 @@
     back = [swap_cores(x) for x in back]
 
     to_up, to_down = add(here[1][0:4], back[1][0:4]), add(here[1][4:8], back[1][4:8])
-    to_up, to_down, back[2] = lax.optimization_barrier((to_up, to_down, back[2]))
+    _, _, back[2] = lax.optimization_barrier((to_up, to_down, back[2]))
     from_up, from_down = shift(to_up, -1), shift(to_down, 1)
     from_far = shift(add(here[2][0:4], back[2]), 2)
     query_grad = settle(query_grad)

time: 77.6 us -> 76.3 us (0.983)
  waiting for transfers between devices: 24.6 us -> 22.4 us
    ppermute x7, waiting for transfers between devices: 14.3 us -> 13.1 us  [shift(): return lax.ppermute(x, 'dp', pairs)]
    ppermute x8, waiting for transfers between devices: 2.52 us -> 1.46 us  [swap_cores(): return lax.ppermute(x, 'dp', [(i, i ^ 1) for i in range(2 * SIDE * SIDE)])]
  transfers between devices with their start and end apart: 16 -> 16, of which waited for: 9 -> 8; matrix products, arithmetic and copies ran while one was open for 4% -> 4% of each run, Pallas kernels for 20% -> 20%
where the time goes in v5:
time: 76.3 us; the launch traced here: 76 us
  waiting for transfers between devices  22.4 us (29%)
  starting transfers between devices  18.7 us (25%)
  Pallas kernels  17 us (22%)
  blocking collectives  13.1 us (17%)
  local copies, waits for them, and re-layouts  2.33 us (3%)
  other arithmetic  1.69 us (2%)
  between operations  0.77 us (1%)
    pallas_call x3, Pallas kernels, stage(): pl.pallas_call(functools.partial(stage_kernel, turn, sizes), out_shape=[p...  13.3 us
    all_to_all x1, blocking collectives, exchange_line(): lax.all_to_all(x, ('dp', 'pos'), 0, 0, axis_index_groups=line_groups(), t...  13.1 us
    ppermute x7, waiting for transfers between devices, shift(): return lax.ppermute(x, 'dp', pairs)  13.1 us
    ppermute x7, starting transfers between devices, shift(): return lax.ppermute(x, 'dp', pairs)  10.9 us
    all_to_all x1, waiting for transfers between devices, exchange_line(): lax.all_to_all(x, ('dp', 'pos'), 0, 0, axis_index_groups=line_groups(), t...  7.81 us
    all_to_all x1, starting transfers between devices, exchange_line(): lax.all_to_all(x, ('dp', 'pos'), 0, 0, axis_index_groups=line_groups(), t...  5.49 us
    ppermute x8, starting transfers between devices, swap_cores(): return lax.ppermute(x, 'dp', [(i, i ^ 1) for i in range(2 * SIDE * SIDE)])  2.29 us
    pallas_call x1, Pallas kernels, spread(): pl.pallas_call(spread_kernel, out_shape=jax.ShapeDtypeStruct((2 * SIDE, k...  1.63 us
  transfers between devices with their start and end apart: 16, of which 8 were waited for; matrix products, arithmetic and copies ran while one was open for 4% of the time, Pallas kernels for 20%

profile of v5, /device:TPU:0, one launch (start us, length us, event | category | flops | bytes accessed | tf_op | source)
XLA Modules:
  0.0 76.0 jit_solution(734549135970711346)
XLA Ops:
  0.6 1.6 %spread.1 = bf16[8,128,256]{2,1,0:T(8,128)(2,1)} custom-call(bf16[1,128,128]{2,1,0:T(8,128)(2,1)} %keys.1, bf16[1,128,128]{2,1,0:T(8,128)(2,1)} %values.1), custom_call_target="tpu_custom_call" | custom-call | tf_op jit(solution)/shard_map/spread/pallas_call | solution.py:70
  2.3 5.5 %all-to-all-start = ((bf16[8,128,256]{2,1,0:T(8,128)(2,1)}), bf16[8,128,256]{2,1,0:T(8,128)(2,1)S(1)}, u32[]{:S(2)}, u32[]{:S(2)}) async-start(bf16[8,128,256]{2,1,0:T(8,128)(2,1)} %spread.1), calls=%async_computation | async-start | bytes 1048576 | tf_op jit(solution)/shard_map/all_to_all | solution.py:33
  7.8 0.8 %fusion.5 = s32[1,24]{1,0:T(1,128)S(1)} fusion(s32[768,1]{0,1:T(1,128)} %param.11, s32[]{:T(128)S(6)} %select_n.44, s32[]{:T(128)S(6)} %and.62, s32[]{:T(128)S(6)} %and.57, s32[]{:T(128)S(6)} %shift_right_arithmetic.43), kind=kLoop, calls=%fused_computation.20 | loop fusion | flops 648 | bytes 208 | tf_op jit(solution)/shard_map/add | solution.py:298
  9.0 0.9 %plan.1.sched = s32[24,128]{1,0:T(8,128)S(1)} custom-call(s32[1,128]{1,0:T(1,128)} %pad.4.code_ref), custom_call_target="tpu_custom_call" | custom-call | tf_op jit(solution)/shard_map/plan/pallas_call | solution.py:137
  10.0 0.9 %dynamic-slice_bitcast_fusion = (f32[24,4,64]{2,1,0:T(4,128)S(1)}, f32[24,4,64]{2,1,0:T(4,128)S(1)}) fusion(f32[768,128,4]{1,2,0:T(4,128)} %param.13, s32[]{:T(128)S(6)} %select_n.44, s32[]{:T(128)S(6)} %select_n.48, f32[768,128,4]{1,2,0:T(4,128)} %param.12), kind=kLoop, calls=%fused_computation.8 | loop fusion | bytes 98312 | tf_op jit(solution)/shard_map/dynamic_slice | solution.py:304
  11.2 7.8 %all-to-all-done = bf16[8,128,256]{2,1,0:T(8,128)(2,1)S(1)} async-done(((bf16[8,128,256]{2,1,0:T(8,128)(2,1)}), bf16[8,128,256]{2,1,0:T(8,128)(2,1)S(1)}, u32[]{:S(2)}, u32[]{:S(2)}) %all-to-all-start) | async-done | bytes 524320 | tf_op jit(solution)/shard_map/all_to_all | solution.py:33
  19.0 1.5 %collective-permute-start.2 = (bf16[4,256,256]{2,1,0:T(8,128)(2,1)S(1)}, bf16[4,256,256]{2,1,0:T(8,128)(2,1)S(1)}, u32[]{:S(2)}, u32[]{:S(2)}) collective-permute-start(bf16[4,256,256]{2,1,0:T(8,128)(2,1)S(1)} %bitcast.48), channel_id=1, source_target_pairs={{0,32},{4,12},{8,40},{12,20},{16,48},{20,28},{24,56},{28,4},{32,64... | collective-permute-start | bytes 1572872 | tf_op jit(solution)/shard_map/ppermute | solution.py:42
  20.5 1.8 %collective-permute-start.3 = (bf16[4,256,256]{2,1,0:T(8,128)(2,1)S(1)}, bf16[4,256,256]{2,1,0:T(8,128)(2,1)S(1)}, u32[]{:S(2)}, u32[]{:S(2)}) collective-permute-start(bf16[4,256,256]{2,1,0:T(8,128)(2,1)S(1)} %bitcast.49), channel_id=1, source_target_pairs={{0,96},{4,28},{8,104},{12,4},{16,112},{20,12},{24,120},{28,20},{32... | collective-permute-start | bytes 1572872 | tf_op jit(solution)/shard_map/ppermute | solution.py:42
  22.3 5.2 %line_stage.1 = (bf16[24,64,512]{2,1,0:T(8,128)(2,1)S(1)}, bf16[8,256,256]{2,1,0:T(8,128)(2,1)S(1)}, bf16[4,256,256]{2,1,0:T(8,128)(2,1)S(1)}, bf16[2,24,64,512]{3,2,1,0:T(8,128)(2,1)S(1)}) custom-call(s32[24,128]{1,0:T(8,128)S(1)} %plan.1.sched, bf16[24,64,512]{2,1,0:T(8,128)(2,1)} %refs_0_.1, bf16[24,64,512]{2,1,0:T(8,128)(2,1)} %refs_1_.1, ...), custom_call_target="tpu_custom_call" | custom-call | flops 503316480 | tf_op jit(solution)/shard_map/line_stage/pallas_call | solution.py:250
  27.4 2.0 %collective-permute-done.2.refs_2_ = bf16[4,256,256]{2,1,0:T(8,128)(2,1)S(1)} collective-permute-done((bf16[4,256,256]{2,1,0:T(8,128)(2,1)S(1)}, bf16[4,256,256]{2,1,0:T(8,128)(2,1)S(1)}, u32[]{:S(2)}, u32[]{:S(2)}) %collective-permute-start.2) | collective-permute-done | bytes 524320 | tf_op jit(solution)/shard_map/ppermute | solution.py:42
  30.2 1.5 %collective-permute-start.6 = (bf16[2,256,256]{2,1,0:T(8,128)(2,1)S(1)}, bf16[2,256,256]{2,1,0:T(8,128)(2,1)S(1)}, u32[]{:S(2)}, u32[]{:S(2)}) collective-permute-start(bf16[2,256,256]{2,1,0:T(8,128)(2,1)S(1)} %slice.32), channel_id=1, source_target_pairs={{0,32},{4,12},{8,40},{12,20},{16,48},{20,28},{24,56},{28,4},{32,64... | collective-permute-start | bytes 786440 | tf_op jit(solution)/shard_map/ppermute | solution.py:42
  31.8 1.8 %collective-permute-start.7 = (bf16[2,256,256]{2,1,0:T(8,128)(2,1)S(1)}, bf16[2,256,256]{2,1,0:T(8,128)(2,1)S(1)}, u32[]{:S(2)}, u32[]{:S(2)}) collective-permute-start(bf16[2,256,256]{2,1,0:T(8,128)(2,1)S(1)} %slice.33), channel_id=1, source_target_pairs={{0,96},{4,28},{8,104},{12,4},{16,112},{20,12},{24,120},{28,20},{32... | collective-permute-start | bytes 786440 | tf_op jit(solution)/shard_map/ppermute | solution.py:42
  33.5 4.8 %next_stage.1 = (bf16[24,64,512]{2,1,0:T(8,128)(2,1)S(1)}, bf16[16,256,256]{2,1,0:T(8,128)(2,1)S(1)}, bf16[8,256,256]{2,1,0:T(8,128)(2,1)S(1)}) custom-call(s32[24,128]{1,0:T(8,128)S(1)} %plan.1.sched, bf16[2,24,64,512]{3,2,1,0:T(8,128)(2,1)S(1)} %get-tuple-element.33.refs_0_, ...), custom_call_target="tpu_custom_call", output_to_operand_aliasing={{0}: (7, {})} | custom-call | flops 503316480 | tf_op jit(solution)/shard_map/next_stage/pallas_call | solution.py:250
  38.3 0.7 collective-permute-start.8
  39.2 1.1 %collective-permute-done.8.refs_4_ = bf16[2,256,256]{2,1,0:T(8,128)(2,1)S(1)} collective-permute-done((bf16[2,256,256]{2,1,0:T(8,128)(2,1)S(1)}, bf16[2,256,256]{2,1,0:T(8,128)(2,1)S(1)}, u32[]{:S(2)}, u32[]{:S(2)}) %collective-permute-start.8) | collective-permute-done | bytes 262176 | tf_op jit(solution)/shard_map/ppermute | solution.py:46
  41.0 3.4 %far_stage.1 = (bf16[24,64,512]{2,1,0:T(8,128)(2,1)S(1)}, bf16[8,256,256]{2,1,0:T(8,128)(2,1)S(1)}, bf16[4,256,256]{2,1,0:T(8,128)(2,1)S(1)}) custom-call(s32[24,128]{1,0:T(8,128)S(1)} %plan.1.sched, bf16[2,24,64,512]{3,2,1,0:T(8,128)(2,1)S(1)} %get-tuple-element.33.refs_0_, ...), custom_call_target="tpu_custom_call", output_to_operand_aliasing={{0}: (7, {})} | custom-call | flops 503316480 | tf_op jit(solution)/shard_map/far_stage/pallas_call | solution.py:250
  45.7 2.8 %collective-permute-start.11 = (bf16[4,256,256]{2,1,0:T(8,128)(2,1)S(1)}, bf16[4,256,256]{2,1,0:T(8,128)(2,1)S(1)}, u32[]{:S(2)}, u32[]{:S(2)}) collective-permute-start(bf16[4,256,256]{2,1,0:T(8,128)(2,1)S(1)} %get-tuple-element.53), channel_id=1, source_target_pairs={{0,96},{4,28},{8,104},{12,4},{16,112},{20,12},{24,120},{28,20},{32... | collective-permute-start | bytes 1572872 | tf_op jit(solution)/shard_map/ppermute | solution.py:42
  48.7 1.1 %collective-permute-start.14 = (bf16[4,256,256]{2,1,0:T(8,128)(2,1)S(1)}, bf16[4,256,256]{2,1,0:T(8,128)(2,1)S(1)}, u32[]{:S(2)}, u32[]{:S(2)}) collective-permute-start(bf16[4,256,256]{2,1,0:T(8,128)(2,1)S(1)} %add_convert_fusion.1), channel_id=1, source_target_pairs={{0,64},{4,20},{8,72},{12,28},{16,80},{20,4},{24,88},{28,12},{32,96... | collective-permute-start | bytes 1572872 | tf_op jit(solution)/shard_map/ppermute | solution.py:42
  49.8 1.1 %settle.1 = bf16[24,64,512]{2,1,0:T(8,128)(2,1)} custom-call(bf16[24,64,512]{2,1,0:T(8,128)(2,1)S(1)} %get-tuple-element.47.source), custom_call_target="tpu_custom_call" | custom-call | tf_op jit(solution)/shard_map/settle/pallas_call | solution.py:90
  50.9 4.8 %collective-permute-done.12 = bf16[4,256,256]{2,1,0:T(8,128)(2,1)S(1)} collective-permute-done((bf16[4,256,256]{2,1,0:T(8,128)(2,1)S(1)}, bf16[4,256,256]{2,1,0:T(8,128)(2,1)S(1)}, u32[]{:S(2)}, u32[]{:S(2)}) %collective-permute-start.12) | collective-permute-done | bytes 524320 | tf_op jit(solution)/shard_map/ppermute | solution.py:42
  55.7 5.2 %collective-permute-done.11 = bf16[4,256,256]{2,1,0:T(8,128)(2,1)S(1)} collective-permute-done((bf16[4,256,256]{2,1,0:T(8,128)(2,1)S(1)}, bf16[4,256,256]{2,1,0:T(8,128)(2,1)S(1)}, u32[]{:S(2)}, u32[]{:S(2)}) %collective-permute-start.11) | collective-permute-done | bytes 524320 | tf_op jit(solution)/shard_map/ppermute | solution.py:42
  61.1 0.9 %collective-permute-done.14 = bf16[4,256,256]{2,1,0:T(8,128)(2,1)S(1)} collective-permute-done((bf16[4,256,256]{2,1,0:T(8,128)(2,1)S(1)}, bf16[4,256,256]{2,1,0:T(8,128)(2,1)S(1)}, u32[]{:S(2)}, u32[]{:S(2)}) %collective-permute-start.14) | collective-permute-done | bytes 524320 | tf_op jit(solution)/shard_map/ppermute | solution.py:42
  62.2 13.1 %all_to_all.10 = bf16[8,128,256]{2,1,0:T(8,128)(2,1)S(1)} all-to-all(bf16[8,128,256]{2,1,0:T(8,128)(2,1)S(1)} %bitcast.51), channel_id=1, replica_groups={{0,1,8,9,16,17,24,25},{32,33,40,41,48,49,56,57},{64,65,72,73,80,81,88,8..., dimensions={0} | all-to-all | bytes 1048576 | tf_op jit(solution)/shard_map/all_to_all | solution.py:33
  75.4 0.6 slice_bitcast_fusion
  (29 shorter events, 4.4 us)
Async XLA Ops:
  2.3 16.8 %all-to-all-start = ((bf16[8,128,256]{2,1,0:T(8,128)(2,1)}), bf16[8,128,256]{2,1,0:T(8,128)(2,1)S(1)}, u32[]{:S(2)}, u32[]{:S(2)}) async-start(bf16[8,128,256]{2,1,0:T(8,128)(2,1)} %spread.1), calls=%async_computation | async-start | bytes 1048576 | tf_op jit(solution)/shard_map/all_to_all | solution.py:33
  19.0 3.2 %collective-permute-start = (bf16[4,256,256]{2,1,0:T(8,128)(2,1)S(1)}, bf16[4,256,256]{2,1,0:T(8,128)(2,1)S(1)}, u32[]{:S(2)}, u32[]{:S(2)}) collective-permute-start(bf16[4,256,256]{2,1,0:T(8,128)(2,1)S(1)} %bitcast.47), channel_id=1, source_target_pairs={{0,4},{4,0},{8,12},{12,8},{16,20},{20,16},{24,28},{28,24},{32,36},... | collective-permute-start | bytes 1572872 | tf_op jit(solution)/shard_map/ppermute | solution.py:46
  19.0 10.4 %collective-permute-start.2 = (bf16[4,256,256]{2,1,0:T(8,128)(2,1)S(1)}, bf16[4,256,256]{2,1,0:T(8,128)(2,1)S(1)}, u32[]{:S(2)}, u32[]{:S(2)}) collective-permute-start(bf16[4,256,256]{2,1,0:T(8,128)(2,1)S(1)} %bitcast.48), channel_id=1, source_target_pairs={{0,32},{4,12},{8,40},{12,20},{16,48},{20,28},{24,56},{28,4},{32,64... | collective-permute-start | bytes 1572872 | tf_op jit(solution)/shard_map/ppermute | solution.py:42
  20.5 9.2 %collective-permute-start.3 = (bf16[4,256,256]{2,1,0:T(8,128)(2,1)S(1)}, bf16[4,256,256]{2,1,0:T(8,128)(2,1)S(1)}, u32[]{:S(2)}, u32[]{:S(2)}) collective-permute-start(bf16[4,256,256]{2,1,0:T(8,128)(2,1)S(1)} %bitcast.49), channel_id=1, source_target_pairs={{0,96},{4,28},{8,104},{12,4},{16,112},{20,12},{24,120},{28,20},{32... | collective-permute-start | bytes 1572872 | tf_op jit(solution)/shard_map/ppermute | solution.py:42
  29.7 3.9 %collective-permute-start.4 = (bf16[4,256,256]{2,1,0:T(8,128)(2,1)S(1)}, bf16[4,256,256]{2,1,0:T(8,128)(2,1)S(1)}, u32[]{:S(2)}, u32[]{:S(2)}) collective-permute-start(bf16[4,256,256]{2,1,0:T(8,128)(2,1)S(1)} %collective-permute-done.2.refs_2_), channel_id=1, source_target_pairs={{0,4},{4,0},{8,12},{12,8},{16,20},{20,16},{24,28},{28,24},{32,36},... | collective-permute-start | bytes 1572872 | tf_op jit(solution)/shard_map/ppermute | solution.py:46
  29.7 3.9 %collective-permute-start.5 = (bf16[4,256,256]{2,1,0:T(8,128)(2,1)S(1)}, bf16[4,256,256]{2,1,0:T(8,128)(2,1)S(1)}, u32[]{:S(2)}, u32[]{:S(2)}) collective-permute-start(bf16[4,256,256]{2,1,0:T(8,128)(2,1)S(1)} %collective-permute-done.3.refs_3_), channel_id=1, source_target_pairs={{0,4},{4,0},{8,12},{12,8},{16,20},{20,16},{24,28},{28,24},{32,36},... | collective-permute-start | bytes 1572872 | tf_op jit(solution)/shard_map/ppermute | solution.py:46
  30.2 8.1 %collective-permute-start.6 = (bf16[2,256,256]{2,1,0:T(8,128)(2,1)S(1)}, bf16[2,256,256]{2,1,0:T(8,128)(2,1)S(1)}, u32[]{:S(2)}, u32[]{:S(2)}) collective-permute-start(bf16[2,256,256]{2,1,0:T(8,128)(2,1)S(1)} %slice.32), channel_id=1, source_target_pairs={{0,32},{4,12},{8,40},{12,20},{16,48},{20,28},{24,56},{28,4},{32,64... | collective-permute-start | bytes 786440 | tf_op jit(solution)/shard_map/ppermute | solution.py:42
  31.8 6.6 %collective-permute-start.7 = (bf16[2,256,256]{2,1,0:T(8,128)(2,1)S(1)}, bf16[2,256,256]{2,1,0:T(8,128)(2,1)S(1)}, u32[]{:S(2)}, u32[]{:S(2)}) collective-permute-start(bf16[2,256,256]{2,1,0:T(8,128)(2,1)S(1)} %slice.33), channel_id=1, source_target_pairs={{0,96},{4,28},{8,104},{12,4},{16,112},{20,12},{24,120},{28,20},{32... | collective-permute-start | bytes 786440 | tf_op jit(solution)/shard_map/ppermute | solution.py:42
  38.3 1.9 %collective-permute-start.8 = (bf16[2,256,256]{2,1,0:T(8,128)(2,1)S(1)}, bf16[2,256,256]{2,1,0:T(8,128)(2,1)S(1)}, u32[]{:S(2)}, u32[]{:S(2)}) collective-permute-start(bf16[2,256,256]{2,1,0:T(8,128)(2,1)S(1)} %collective-permute-done.6.refs_2_), channel_id=1, source_target_pairs={{0,4},{4,0},{8,12},{12,8},{16,20},{20,16},{24,28},{28,24},{32,36},... | collective-permute-start | bytes 786440 | tf_op jit(solution)/shard_map/ppermute | solution.py:46
  39.1 1.5 %collective-permute-start.9 = (bf16[2,256,256]{2,1,0:T(8,128)(2,1)S(1)}, bf16[2,256,256]{2,1,0:T(8,128)(2,1)S(1)}, u32[]{:S(2)}, u32[]{:S(2)}) collective-permute-start(bf16[2,256,256]{2,1,0:T(8,128)(2,1)S(1)} %collective-permute-done.7.refs_3_), channel_id=1, source_target_pairs={{0,4},{4,0},{8,12},{12,8},{16,20},{20,16},{24,28},{28,24},{32,36},... | collective-permute-start | bytes 786440 | tf_op jit(solution)/shard_map/ppermute | solution.py:46
  40.6 4.4 %collective-permute-start.10 = (bf16[8,256,256]{2,1,0:T(8,128)(2,1)S(1)}, bf16[8,256,256]{2,1,0:T(8,128)(2,1)S(1)}, u32[]{:S(2)}, u32[]{:S(2)}) collective-permute-start(bf16[8,256,256]{2,1,0:T(8,128)(2,1)S(1)} %get-tuple-element.43), channel_id=1, source_target_pairs={{0,4},{4,0},{8,12},{12,8},{16,20},{20,16},{24,28},{28,24},{32,36},... | collective-permute-start | bytes 3145736 | tf_op jit(solution)/shard_map/ppermute | solution.py:46
  44.4 4.2 %collective-permute-start.13 = (bf16[4,256,256]{2,1,0:T(8,128)(2,1)S(1)}, bf16[4,256,256]{2,1,0:T(8,128)(2,1)S(1)}, u32[]{:S(2)}, u32[]{:S(2)}) collective-permute-start(bf16[4,256,256]{2,1,0:T(8,128)(2,1)S(1)} %get-tuple-element.51), channel_id=1, source_target_pairs={{0,4},{4,0},{8,12},{12,8},{16,20},{20,16},{24,28},{28,24},{32,36},... | collective-permute-start | bytes 1572872 | tf_op jit(solution)/shard_map/ppermute | solution.py:46
  44.6 6.3 %collective-permute-start.1 = (bf16[4,256,256]{2,1,0:T(8,128)(2,1)S(1)}, bf16[4,256,256]{2,1,0:T(8,128)(2,1)S(1)}, u32[]{:S(2)}, u32[]{:S(2)}) collective-permute-start(bf16[4,256,256]{2,1,0:T(8,128)(2,1)S(1)} %get-tuple-element.32), channel_id=1, source_target_pairs={{0,4},{4,0},{8,12},{12,8},{16,20},{20,16},{24,28},{28,24},{32,36},... | collective-permute-start | bytes 1572872 | tf_op jit(solution)/shard_map/ppermute | solution.py:46
  45.2 10.5 %collective-permute-start.12 = (bf16[4,256,256]{2,1,0:T(8,128)(2,1)S(1)}, bf16[4,256,256]{2,1,0:T(8,128)(2,1)S(1)}, u32[]{:S(2)}, u32[]{:S(2)}) collective-permute-start(bf16[4,256,256]{2,1,0:T(8,128)(2,1)S(1)} %get-tuple-element.54), channel_id=1, source_target_pairs={{0,32},{4,12},{8,40},{12,20},{16,48},{20,28},{24,56},{28,4},{32,64... | collective-permute-start | bytes 1572872 | tf_op jit(solution)/shard_map/ppermute | solution.py:42
  45.7 15.2 %collective-permute-start.11 = (bf16[4,256,256]{2,1,0:T(8,128)(2,1)S(1)}, bf16[4,256,256]{2,1,0:T(8,128)(2,1)S(1)}, u32[]{:S(2)}, u32[]{:S(2)}) collective-permute-start(bf16[4,256,256]{2,1,0:T(8,128)(2,1)S(1)} %get-tuple-element.53), channel_id=1, source_target_pairs={{0,96},{4,28},{8,104},{12,4},{16,112},{20,12},{24,120},{28,20},{32... | collective-permute-start | bytes 1572872 | tf_op jit(solution)/shard_map/ppermute | solution.py:42
  48.7 13.3 %collective-permute-start.14 = (bf16[4,256,256]{2,1,0:T(8,128)(2,1)S(1)}, bf16[4,256,256]{2,1,0:T(8,128)(2,1)S(1)}, u32[]{:S(2)}, u32[]{:S(2)}) collective-permute-start(bf16[4,256,256]{2,1,0:T(8,128)(2,1)S(1)} %add_convert_fusion.1), channel_id=1, source_target_pairs={{0,64},{4,20},{8,72},{12,28},{16,80},{20,4},{24,88},{28,12},{32,96... | collective-permute-start | bytes 1572872 | tf_op jit(solution)/shard_map/ppermute | solution.py:42

commit v6 on v5

--- a/solution.py
+++ b/solution.py
@@ -231,9 +231,7 @@
         return 0
 
     lax.fori_loop(0, count, step, 0)
-    handed = pltpu.make_async_copy(sums.at[places // 2:places], there, arrived.at[0])
-    handed.start()
-    handed.wait()
+    there[...] = sums[places // 2:places]
 
 
 def stage(turn, sched, tile_rows, stats, blocks, query_grad):
@@ -252,11 +250,11 @@
         out_shape=[
             pltpu.VMEM(shape, kind),
             pltpu.VMEM((places, *block_shape), kind),
-            jax.ShapeDtypeStruct((places // 2, *block_shape), kind),
+            pltpu.VMEM((places // 2, *block_shape), kind),
         ] + [pltpu.VMEM((2, *shape), kind)] * first,
         in_specs=[pl.BlockSpec(memory_space=pltpu.SMEM)] + ([pl.BlockSpec(memory_space=pltpu.HBM)] * 2 if first else [whole]) + [whole]
         + [away] * len(blocks) + [whole] * (not first),
-        out_specs=[whole, whole, away] + [whole] * first,
+        out_specs=[whole, whole, whole] + [whole] * first,
         scratch_shapes=[
             pltpu.VMEM((places, *block_shape), kind),
             pltpu.SemaphoreType.DMA((len(blocks) + 2,)),

time: 76.3 us -> 76.1 us (level)
  no operation moved by 1% of the time
where the time goes in v6:
time: 76.1 us; the launch traced here: 75.7 us
  waiting for transfers between devices  22 us (29%)
  starting transfers between devices  18.7 us (25%)
  Pallas kernels  17 us (22%)
  blocking collectives  13.2 us (17%)
  local copies, waits for them, and re-layouts  2.33 us (3%)
  other arithmetic  1.69 us (2%)
  between operations  0.77 us (1%)
    pallas_call x3, Pallas kernels, stage(): pl.pallas_call(functools.partial(stage_kernel, turn, sizes), out_shape=[p...  13.3 us
    all_to_all x1, blocking collectives, exchange_line(): lax.all_to_all(x, ('dp', 'pos'), 0, 0, axis_index_groups=line_groups(), t...  13.2 us
    ppermute x7, waiting for transfers between devices, shift(): return lax.ppermute(x, 'dp', pairs)  12.8 us
    ppermute x7, starting transfers between devices, shift(): return lax.ppermute(x, 'dp', pairs)  11.4 us
    all_to_all x1, waiting for transfers between devices, exchange_line(): lax.all_to_all(x, ('dp', 'pos'), 0, 0, axis_index_groups=line_groups(), t...  7.81 us
    all_to_all x1, starting transfers between devices, exchange_line(): lax.all_to_all(x, ('dp', 'pos'), 0, 0, axis_index_groups=line_groups(), t...  5.49 us
    ppermute x8, starting transfers between devices, swap_cores(): return lax.ppermute(x, 'dp', [(i, i ^ 1) for i in range(2 * SIDE * SIDE)])  1.82 us
    pallas_call x1, Pallas kernels, spread(): pl.pallas_call(spread_kernel, out_shape=jax.ShapeDtypeStruct((2 * SIDE, k...  1.63 us
  transfers between devices with their start and end apart: 16, of which 8 were waited for; matrix products, arithmetic and copies ran while one was open for 4% of the time, Pallas kernels for 20%

profile of v6, /device:TPU:0, one launch (start us, length us, event | category | flops | bytes accessed | tf_op | source)
XLA Modules:
  0.0 75.7 jit_solution(17581665209846229433)
XLA Ops:
  0.6 1.6 %spread.1 = bf16[8,128,256]{2,1,0:T(8,128)(2,1)} custom-call(bf16[1,128,128]{2,1,0:T(8,128)(2,1)} %keys.1, bf16[1,128,128]{2,1,0:T(8,128)(2,1)} %values.1), custom_call_target="tpu_custom_call" | custom-call | tf_op jit(solution)/shard_map/spread/pallas_call | solution.py:70
  2.3 5.5 %all-to-all-start = ((bf16[8,128,256]{2,1,0:T(8,128)(2,1)}), bf16[8,128,256]{2,1,0:T(8,128)(2,1)S(1)}, u32[]{:S(2)}, u32[]{:S(2)}) async-start(bf16[8,128,256]{2,1,0:T(8,128)(2,1)} %spread.1), calls=%async_computation | async-start | bytes 1048576 | tf_op jit(solution)/shard_map/all_to_all | solution.py:33
  7.8 0.8 %fusion.5 = s32[1,24]{1,0:T(1,128)S(1)} fusion(s32[768,1]{0,1:T(1,128)} %param.11, s32[]{:T(128)S(6)} %select_n.44, s32[]{:T(128)S(6)} %and.62, s32[]{:T(128)S(6)} %and.57, s32[]{:T(128)S(6)} %shift_right_arithmetic.43), kind=kLoop, calls=%fused_computation.20 | loop fusion | flops 648 | bytes 208 | tf_op jit(solution)/shard_map/add | solution.py:296
  9.0 0.9 %plan.1.sched = s32[24,128]{1,0:T(8,128)S(1)} custom-call(s32[1,128]{1,0:T(1,128)} %pad.4.code_ref), custom_call_target="tpu_custom_call" | custom-call | tf_op jit(solution)/shard_map/plan/pallas_call | solution.py:137
  10.0 0.9 %dynamic-slice_bitcast_fusion = (f32[24,4,64]{2,1,0:T(4,128)S(1)}, f32[24,4,64]{2,1,0:T(4,128)S(1)}) fusion(f32[768,128,4]{1,2,0:T(4,128)} %param.13, s32[]{:T(128)S(6)} %select_n.44, s32[]{:T(128)S(6)} %select_n.48, f32[768,128,4]{1,2,0:T(4,128)} %param.12), kind=kLoop, calls=%fused_computation.8 | loop fusion | bytes 98312 | tf_op jit(solution)/shard_map/dynamic_slice | solution.py:302
  11.2 7.8 %all-to-all-done = bf16[8,128,256]{2,1,0:T(8,128)(2,1)S(1)} async-done(((bf16[8,128,256]{2,1,0:T(8,128)(2,1)}), bf16[8,128,256]{2,1,0:T(8,128)(2,1)S(1)}, u32[]{:S(2)}, u32[]{:S(2)}) %all-to-all-start) | async-done | bytes 524320 | tf_op jit(solution)/shard_map/all_to_all | solution.py:33
  19.0 1.5 %collective-permute-start.2 = (bf16[4,256,256]{2,1,0:T(8,128)(2,1)S(1)}, bf16[4,256,256]{2,1,0:T(8,128)(2,1)S(1)}, u32[]{:S(2)}, u32[]{:S(2)}) collective-permute-start(bf16[4,256,256]{2,1,0:T(8,128)(2,1)S(1)} %bitcast.48), channel_id=1, source_target_pairs={{0,32},{4,12},{8,40},{12,20},{16,48},{20,28},{24,56},{28,4},{32,64... | collective-permute-start | bytes 1572872 | tf_op jit(solution)/shard_map/ppermute | solution.py:42
  20.5 1.8 %collective-permute-start.3 = (bf16[4,256,256]{2,1,0:T(8,128)(2,1)S(1)}, bf16[4,256,256]{2,1,0:T(8,128)(2,1)S(1)}, u32[]{:S(2)}, u32[]{:S(2)}) collective-permute-start(bf16[4,256,256]{2,1,0:T(8,128)(2,1)S(1)} %bitcast.49), channel_id=1, source_target_pairs={{0,96},{4,28},{8,104},{12,4},{16,112},{20,12},{24,120},{28,20},{32... | collective-permute-start | bytes 1572872 | tf_op jit(solution)/shard_map/ppermute | solution.py:42
  22.3 5.2 %line_stage.1 = (bf16[24,64,512]{2,1,0:T(8,128)(2,1)S(1)}, bf16[8,256,256]{2,1,0:T(8,128)(2,1)S(1)}, bf16[4,256,256]{2,1,0:T(8,128)(2,1)S(1)}, bf16[2,24,64,512]{3,2,1,0:T(8,128)(2,1)S(1)}) custom-call(s32[24,128]{1,0:T(8,128)S(1)} %plan.1.sched, bf16[24,64,512]{2,1,0:T(8,128)(2,1)} %refs_0_.1, bf16[24,64,512]{2,1,0:T(8,128)(2,1)} %refs_1_.1, ...), custom_call_target="tpu_custom_call" | custom-call | flops 503316480 | tf_op jit(solution)/shard_map/line_stage/pallas_call | solution.py:248
  27.4 2.0 %collective-permute-done.2.refs_2_ = bf16[4,256,256]{2,1,0:T(8,128)(2,1)S(1)} collective-permute-done((bf16[4,256,256]{2,1,0:T(8,128)(2,1)S(1)}, bf16[4,256,256]{2,1,0:T(8,128)(2,1)S(1)}, u32[]{:S(2)}, u32[]{:S(2)}) %collective-permute-start.2) | collective-permute-done | bytes 524320 | tf_op jit(solution)/shard_map/ppermute | solution.py:42
  30.2 1.5 %collective-permute-start.6 = (bf16[2,256,256]{2,1,0:T(8,128)(2,1)S(1)}, bf16[2,256,256]{2,1,0:T(8,128)(2,1)S(1)}, u32[]{:S(2)}, u32[]{:S(2)}) collective-permute-start(bf16[2,256,256]{2,1,0:T(8,128)(2,1)S(1)} %slice.32), channel_id=1, source_target_pairs={{0,32},{4,12},{8,40},{12,20},{16,48},{20,28},{24,56},{28,4},{32,64... | collective-permute-start | bytes 786440 | tf_op jit(solution)/shard_map/ppermute | solution.py:42
  31.8 1.8 %collective-permute-start.7 = (bf16[2,256,256]{2,1,0:T(8,128)(2,1)S(1)}, bf16[2,256,256]{2,1,0:T(8,128)(2,1)S(1)}, u32[]{:S(2)}, u32[]{:S(2)}) collective-permute-start(bf16[2,256,256]{2,1,0:T(8,128)(2,1)S(1)} %slice.33), channel_id=1, source_target_pairs={{0,96},{4,28},{8,104},{12,4},{16,112},{20,12},{24,120},{28,20},{32... | collective-permute-start | bytes 786440 | tf_op jit(solution)/shard_map/ppermute | solution.py:42
  33.5 4.8 %next_stage.1 = (bf16[24,64,512]{2,1,0:T(8,128)(2,1)S(1)}, bf16[16,256,256]{2,1,0:T(8,128)(2,1)S(1)}, bf16[8,256,256]{2,1,0:T(8,128)(2,1)S(1)}) custom-call(s32[24,128]{1,0:T(8,128)S(1)} %plan.1.sched, bf16[2,24,64,512]{3,2,1,0:T(8,128)(2,1)S(1)} %get-tuple-element.33.refs_0_, ...), custom_call_target="tpu_custom_call", output_to_operand_aliasing={{0}: (7, {})} | custom-call | flops 503316480 | tf_op jit(solution)/shard_map/next_stage/pallas_call | solution.py:248
  38.9 1.0 %collective-permute-done.8.refs_4_ = bf16[2,256,256]{2,1,0:T(8,128)(2,1)S(1)} collective-permute-done((bf16[2,256,256]{2,1,0:T(8,128)(2,1)S(1)}, bf16[2,256,256]{2,1,0:T(8,128)(2,1)S(1)}, u32[]{:S(2)}, u32[]{:S(2)}) %collective-permute-start.8) | collective-permute-done | bytes 262176 | tf_op jit(solution)/shard_map/ppermute | solution.py:46
  40.5 3.4 %far_stage.1 = (bf16[24,64,512]{2,1,0:T(8,128)(2,1)S(1)}, bf16[8,256,256]{2,1,0:T(8,128)(2,1)S(1)}, bf16[4,256,256]{2,1,0:T(8,128)(2,1)S(1)}) custom-call(s32[24,128]{1,0:T(8,128)S(1)} %plan.1.sched, bf16[2,24,64,512]{3,2,1,0:T(8,128)(2,1)S(1)} %get-tuple-element.33.refs_0_, ...), custom_call_target="tpu_custom_call", output_to_operand_aliasing={{0}: (7, {})} | custom-call | flops 503316480 | tf_op jit(solution)/shard_map/far_stage/pallas_call | solution.py:248
  44.7 1.0 %collective-permute-start.12 = (bf16[4,256,256]{2,1,0:T(8,128)(2,1)S(1)}, bf16[4,256,256]{2,1,0:T(8,128)(2,1)S(1)}, u32[]{:S(2)}, u32[]{:S(2)}) collective-permute-start(bf16[4,256,256]{2,1,0:T(8,128)(2,1)S(1)} %get-tuple-element.54), channel_id=1, source_target_pairs={{0,32},{4,12},{8,40},{12,20},{16,48},{20,28},{24,56},{28,4},{32,64... | collective-permute-start | bytes 1572872 | tf_op jit(solution)/shard_map/ppermute | solution.py:42
  45.7 2.3 %collective-permute-start.11 = (bf16[4,256,256]{2,1,0:T(8,128)(2,1)S(1)}, bf16[4,256,256]{2,1,0:T(8,128)(2,1)S(1)}, u32[]{:S(2)}, u32[]{:S(2)}) collective-permute-start(bf16[4,256,256]{2,1,0:T(8,128)(2,1)S(1)} %get-tuple-element.53), channel_id=1, source_target_pairs={{0,96},{4,28},{8,104},{12,4},{16,112},{20,12},{24,120},{28,20},{32... | collective-permute-start | bytes 1572872 | tf_op jit(solution)/shard_map/ppermute | solution.py:42
  48.2 1.6 %collective-permute-start.14 = (bf16[4,256,256]{2,1,0:T(8,128)(2,1)S(1)}, bf16[4,256,256]{2,1,0:T(8,128)(2,1)S(1)}, u32[]{:S(2)}, u32[]{:S(2)}) collective-permute-start(bf16[4,256,256]{2,1,0:T(8,128)(2,1)S(1)} %add_convert_fusion.1), channel_id=1, source_target_pairs={{0,64},{4,20},{8,72},{12,28},{16,80},{20,4},{24,88},{28,12},{32,96... | collective-permute-start | bytes 1572872 | tf_op jit(solution)/shard_map/ppermute | solution.py:42
  49.8 1.1 %settle.1 = bf16[24,64,512]{2,1,0:T(8,128)(2,1)} custom-call(bf16[24,64,512]{2,1,0:T(8,128)(2,1)S(1)} %get-tuple-element.47.source), custom_call_target="tpu_custom_call" | custom-call | tf_op jit(solution)/shard_map/settle/pallas_call | solution.py:90
  50.9 4.3 %collective-permute-done.12 = bf16[4,256,256]{2,1,0:T(8,128)(2,1)S(1)} collective-permute-done((bf16[4,256,256]{2,1,0:T(8,128)(2,1)S(1)}, bf16[4,256,256]{2,1,0:T(8,128)(2,1)S(1)}, u32[]{:S(2)}, u32[]{:S(2)}) %collective-permute-start.12) | collective-permute-done | bytes 524320 | tf_op jit(solution)/shard_map/ppermute | solution.py:42
  55.2 5.2 %collective-permute-done.11 = bf16[4,256,256]{2,1,0:T(8,128)(2,1)S(1)} collective-permute-done((bf16[4,256,256]{2,1,0:T(8,128)(2,1)S(1)}, bf16[4,256,256]{2,1,0:T(8,128)(2,1)S(1)}, u32[]{:S(2)}, u32[]{:S(2)}) %collective-permute-start.11) | collective-permute-done | bytes 524320 | tf_op jit(solution)/shard_map/ppermute | solution.py:42
  60.6 1.1 %collective-permute-done.14 = bf16[4,256,256]{2,1,0:T(8,128)(2,1)S(1)} collective-permute-done((bf16[4,256,256]{2,1,0:T(8,128)(2,1)S(1)}, bf16[4,256,256]{2,1,0:T(8,128)(2,1)S(1)}, u32[]{:S(2)}, u32[]{:S(2)}) %collective-permute-start.14) | collective-permute-done | bytes 524320 | tf_op jit(solution)/shard_map/ppermute | solution.py:42
  61.9 13.2 %all_to_all.10 = bf16[8,128,256]{2,1,0:T(8,128)(2,1)S(1)} all-to-all(bf16[8,128,256]{2,1,0:T(8,128)(2,1)S(1)} %bitcast.51), channel_id=1, replica_groups={{0,1,8,9,16,17,24,25},{32,33,40,41,48,49,56,57},{64,65,72,73,80,81,88,8..., dimensions={0} | all-to-all | bytes 1048576 | tf_op jit(solution)/shard_map/all_to_all | solution.py:33
  75.1 0.6 slice_bitcast_fusion
  (29 shorter events, 4.2 us)
Async XLA Ops:
  2.3 16.8 %all-to-all-start = ((bf16[8,128,256]{2,1,0:T(8,128)(2,1)}), bf16[8,128,256]{2,1,0:T(8,128)(2,1)S(1)}, u32[]{:S(2)}, u32[]{:S(2)}) async-start(bf16[8,128,256]{2,1,0:T(8,128)(2,1)} %spread.1), calls=%async_computation | async-start | bytes 1048576 | tf_op jit(solution)/shard_map/all_to_all | solution.py:33
  19.0 3.2 %collective-permute-start = (bf16[4,256,256]{2,1,0:T(8,128)(2,1)S(1)}, bf16[4,256,256]{2,1,0:T(8,128)(2,1)S(1)}, u32[]{:S(2)}, u32[]{:S(2)}) collective-permute-start(bf16[4,256,256]{2,1,0:T(8,128)(2,1)S(1)} %bitcast.47), channel_id=1, source_target_pairs={{0,4},{4,0},{8,12},{12,8},{16,20},{20,16},{24,28},{28,24},{32,36},... | collective-permute-start | bytes 1572872 | tf_op jit(solution)/shard_map/ppermute | solution.py:46
  19.0 10.4 %collective-permute-start.2 = (bf16[4,256,256]{2,1,0:T(8,128)(2,1)S(1)}, bf16[4,256,256]{2,1,0:T(8,128)(2,1)S(1)}, u32[]{:S(2)}, u32[]{:S(2)}) collective-permute-start(bf16[4,256,256]{2,1,0:T(8,128)(2,1)S(1)} %bitcast.48), channel_id=1, source_target_pairs={{0,32},{4,12},{8,40},{12,20},{16,48},{20,28},{24,56},{28,4},{32,64... | collective-permute-start | bytes 1572872 | tf_op jit(solution)/shard_map/ppermute | solution.py:42
  20.5 9.2 %collective-permute-start.3 = (bf16[4,256,256]{2,1,0:T(8,128)(2,1)S(1)}, bf16[4,256,256]{2,1,0:T(8,128)(2,1)S(1)}, u32[]{:S(2)}, u32[]{:S(2)}) collective-permute-start(bf16[4,256,256]{2,1,0:T(8,128)(2,1)S(1)} %bitcast.49), channel_id=1, source_target_pairs={{0,96},{4,28},{8,104},{12,4},{16,112},{20,12},{24,120},{28,20},{32... | collective-permute-start | bytes 1572872 | tf_op jit(solution)/shard_map/ppermute | solution.py:42
  29.7 3.9 %collective-permute-start.4 = (bf16[4,256,256]{2,1,0:T(8,128)(2,1)S(1)}, bf16[4,256,256]{2,1,0:T(8,128)(2,1)S(1)}, u32[]{:S(2)}, u32[]{:S(2)}) collective-permute-start(bf16[4,256,256]{2,1,0:T(8,128)(2,1)S(1)} %collective-permute-done.2.refs_2_), channel_id=1, source_target_pairs={{0,4},{4,0},{8,12},{12,8},{16,20},{20,16},{24,28},{28,24},{32,36},... | collective-permute-start | bytes 1572872 | tf_op jit(solution)/shard_map/ppermute | solution.py:46
  29.7 3.9 %collective-permute-start.5 = (bf16[4,256,256]{2,1,0:T(8,128)(2,1)S(1)}, bf16[4,256,256]{2,1,0:T(8,128)(2,1)S(1)}, u32[]{:S(2)}, u32[]{:S(2)}) collective-permute-start(bf16[4,256,256]{2,1,0:T(8,128)(2,1)S(1)} %collective-permute-done.3.refs_3_), channel_id=1, source_target_pairs={{0,4},{4,0},{8,12},{12,8},{16,20},{20,16},{24,28},{28,24},{32,36},... | collective-permute-start | bytes 1572872 | tf_op jit(solution)/shard_map/ppermute | solution.py:46
  30.2 8.1 %collective-permute-start.6 = (bf16[2,256,256]{2,1,0:T(8,128)(2,1)S(1)}, bf16[2,256,256]{2,1,0:T(8,128)(2,1)S(1)}, u32[]{:S(2)}, u32[]{:S(2)}) collective-permute-start(bf16[2,256,256]{2,1,0:T(8,128)(2,1)S(1)} %slice.32), channel_id=1, source_target_pairs={{0,32},{4,12},{8,40},{12,20},{16,48},{20,28},{24,56},{28,4},{32,64... | collective-permute-start | bytes 786440 | tf_op jit(solution)/shard_map/ppermute | solution.py:42
  31.8 6.6 %collective-permute-start.7 = (bf16[2,256,256]{2,1,0:T(8,128)(2,1)S(1)}, bf16[2,256,256]{2,1,0:T(8,128)(2,1)S(1)}, u32[]{:S(2)}, u32[]{:S(2)}) collective-permute-start(bf16[2,256,256]{2,1,0:T(8,128)(2,1)S(1)} %slice.33), channel_id=1, source_target_pairs={{0,96},{4,28},{8,104},{12,4},{16,112},{20,12},{24,120},{28,20},{32... | collective-permute-start | bytes 786440 | tf_op jit(solution)/shard_map/ppermute | solution.py:42
  38.3 1.6 %collective-permute-start.8 = (bf16[2,256,256]{2,1,0:T(8,128)(2,1)S(1)}, bf16[2,256,256]{2,1,0:T(8,128)(2,1)S(1)}, u32[]{:S(2)}, u32[]{:S(2)}) collective-permute-start(bf16[2,256,256]{2,1,0:T(8,128)(2,1)S(1)} %collective-permute-done.6.refs_2_), channel_id=1, source_target_pairs={{0,4},{4,0},{8,12},{12,8},{16,20},{20,16},{24,28},{28,24},{32,36},... | collective-permute-start | bytes 786440 | tf_op jit(solution)/shard_map/ppermute | solution.py:46
  38.4 1.9 %collective-permute-start.9 = (bf16[2,256,256]{2,1,0:T(8,128)(2,1)S(1)}, bf16[2,256,256]{2,1,0:T(8,128)(2,1)S(1)}, u32[]{:S(2)}, u32[]{:S(2)}) collective-permute-start(bf16[2,256,256]{2,1,0:T(8,128)(2,1)S(1)} %collective-permute-done.7.refs_3_), channel_id=1, source_target_pairs={{0,4},{4,0},{8,12},{12,8},{16,20},{20,16},{24,28},{28,24},{32,36},... | collective-permute-start | bytes 786440 | tf_op jit(solution)/shard_map/ppermute | solution.py:46
  40.3 4.1 %collective-permute-start.10 = (bf16[8,256,256]{2,1,0:T(8,128)(2,1)S(1)}, bf16[8,256,256]{2,1,0:T(8,128)(2,1)S(1)}, u32[]{:S(2)}, u32[]{:S(2)}) collective-permute-start(bf16[8,256,256]{2,1,0:T(8,128)(2,1)S(1)} %get-tuple-element.43), channel_id=1, source_target_pairs={{0,4},{4,0},{8,12},{12,8},{16,20},{20,16},{24,28},{28,24},{32,36},... | collective-permute-start | bytes 3145736 | tf_op jit(solution)/shard_map/ppermute | solution.py:46
  43.8 4.2 %collective-permute-start.13 = (bf16[4,256,256]{2,1,0:T(8,128)(2,1)S(1)}, bf16[4,256,256]{2,1,0:T(8,128)(2,1)S(1)}, u32[]{:S(2)}, u32[]{:S(2)}) collective-permute-start(bf16[4,256,256]{2,1,0:T(8,128)(2,1)S(1)} %get-tuple-element.51), channel_id=1, source_target_pairs={{0,4},{4,0},{8,12},{12,8},{16,20},{20,16},{24,28},{28,24},{32,36},... | collective-permute-start | bytes 1572872 | tf_op jit(solution)/shard_map/ppermute | solution.py:46
  44.3 6.6 %collective-permute-start.1 = (bf16[4,256,256]{2,1,0:T(8,128)(2,1)S(1)}, bf16[4,256,256]{2,1,0:T(8,128)(2,1)S(1)}, u32[]{:S(2)}, u32[]{:S(2)}) collective-permute-start(bf16[4,256,256]{2,1,0:T(8,128)(2,1)S(1)} %get-tuple-element.32), channel_id=1, source_target_pairs={{0,4},{4,0},{8,12},{12,8},{16,20},{20,16},{24,28},{28,24},{32,36},... | collective-permute-start | bytes 1572872 | tf_op jit(solution)/shard_map/ppermute | solution.py:46
  44.7 10.5 %collective-permute-start.12 = (bf16[4,256,256]{2,1,0:T(8,128)(2,1)S(1)}, bf16[4,256,256]{2,1,0:T(8,128)(2,1)S(1)}, u32[]{:S(2)}, u32[]{:S(2)}) collective-permute-start(bf16[4,256,256]{2,1,0:T(8,128)(2,1)S(1)} %get-tuple-element.54), channel_id=1, source_target_pairs={{0,32},{4,12},{8,40},{12,20},{16,48},{20,28},{24,56},{28,4},{32,64... | collective-permute-start | bytes 1572872 | tf_op jit(solution)/shard_map/ppermute | solution.py:42
  45.7 14.7 %collective-permute-start.11 = (bf16[4,256,256]{2,1,0:T(8,128)(2,1)S(1)}, bf16[4,256,256]{2,1,0:T(8,128)(2,1)S(1)}, u32[]{:S(2)}, u32[]{:S(2)}) collective-permute-start(bf16[4,256,256]{2,1,0:T(8,128)(2,1)S(1)} %get-tuple-element.53), channel_id=1, source_target_pairs={{0,96},{4,28},{8,104},{12,4},{16,112},{20,12},{24,120},{28,20},{32... | collective-permute-start | bytes 1572872 | tf_op jit(solution)/shard_map/ppermute | solution.py:42
  48.2 13.6 %collective-permute-start.14 = (bf16[4,256,256]{2,1,0:T(8,128)(2,1)S(1)}, bf16[4,256,256]{2,1,0:T(8,128)(2,1)S(1)}, u32[]{:S(2)}, u32[]{:S(2)}) collective-permute-start(bf16[4,256,256]{2,1,0:T(8,128)(2,1)S(1)} %add_convert_fusion.1), channel_id=1, source_target_pairs={{0,64},{4,20},{8,72},{12,28},{16,80},{20,4},{24,88},{28,12},{32,96... | collective-permute-start | bytes 1572872 | tf_op jit(solution)/shard_map/ppermute | solution.py:42
